TPU v7x, 32 devices: a whole 2x2x4 slice. The times are simulated.
32 devices in a mesh: row: 4 (over y, x), col: 8 (over z, core).
Axes of the slice: x: 2, y: 2, z: 4, core: 2. Of those that a mesh axis runs over, the one named last changes fastest.
Arguments:
- step_index: int32 [2], replicated, may hold values from 50 to 899
- coarse_state: float32 [8, 128, 1024], P(None, 'row', 'col'), may hold values from -6 to 6
- coarse_forcing: bfloat16 [8, 128, 1024], P(None, 'row', 'col'), may hold values from -6 to 6
- fine_state: float32 [8, 512, 4096], P(None, ('row', 'col')), may hold values from -6 to 6
- land_mask: int32 [512, 4096], P(('row', 'col')), may hold values 0 or 1
- inlet_one: bfloat16 [3, 3, 128, 16], replicated, may hold values from -0.5 to 0.5
- timing_one: bfloat16 [128, 128], replicated, may hold values from -0.5 to 0.5
- scale_one: float32 [128], replicated, may hold values from 0.1 to 1.9
- middle_one: bfloat16 [3, 3, 128, 128], replicated, may hold values from -0.1875 to 0.1875
- outlet_one: bfloat16 [3, 3, 8, 128], replicated, may hold values from -0.1875 to 0.1875
- inlet_two: bfloat16 [3, 3, 32, 17], replicated, may hold values from -0.5 to 0.5
- timing_two: bfloat16 [128, 32], replicated, may hold values from -0.5 to 0.5
- land_bias: float32 [32], replicated, may hold values from -4 to 4
- middle_two: bfloat16 [3, 3, 32, 32], replicated, may hold values from -0.375 to 0.375
- outlet_two: bfloat16 [3, 3, 8, 32], replicated, may hold values from -0.375 to 0.375
Outputs:
- coarse_next: float32 [8, 128, 1024], P(None, 'row', 'col')
- noise_one: float32 [8, 128, 1024], P(None, 'row', 'col')
- fine_next: float32 [8, 512, 4096], P(None, ('row', 'col'))
- noise_two: float32 [8, 512, 4096], P(None, ('row', 'col'))
Inputs may be any that keep to these rules, and one draw needn't show every extreme that they name: `step_index`: the first entry is the step of the 3 km section, the second that of the 750 m section. `land_mask`: 1 on land, 0 on sea.
All inputs are finite; a program needn't handle non-finite values. No bound on the sum of `land_mask` on one device may be relied on, other than what follows from the above.
Results may differ from a plain program's by a relative error of at most 0.0095.
Values may be sent and summed in bfloat16 or wider, within the bound.
No kernel may reach another device: no remote copies, remote signals or barrier semaphores. Data moves between devices by JAX's collectives and lax.ppermute only.
A program may use at most 192 MiB of HBM per device.

v0:
```python
import math

import jax
import jax.numpy as jnp
from jax import lax
from jax.sharding import PartitionSpec as P


def with_halo(cells, sides, width):
    for axis, dim in sides:
        count = lax.axis_size(axis)
        ends = count - 1
        head = lax.slice_in_dim(cells, 0, width, axis=dim)
        tail = lax.slice_in_dim(cells, cells.shape[dim] - width, cells.shape[dim], axis=dim)
        cells = jnp.concatenate(
            [
                lax.ppermute(tail, axis, [(i, (i + 1) % count) for i in range(ends)]),
                cells,
                lax.ppermute(head, axis, [((i + 1) % count, i) for i in range(ends)]),
            ],
            axis=dim,
        )
    return cells


def alpha_bar(moment):
    return jnp.cos((moment / 1000.0 + 0.008) / 1.008 * (math.pi / 2.0)) ** 2


def plan(step_value):
    current_time = step_value.astype(jnp.float32)
    current = alpha_bar(current_time)
    earlier = alpha_bar(current_time - 50.0)
    keeping = jnp.sqrt(earlier / current)
    blending = jnp.sqrt(1.0 - earlier) - jnp.sqrt(earlier) * jnp.sqrt(1.0 - current) / jnp.sqrt(
        current
    )
    return (keeping, blending)


def embedding(step_value, timing):
    half_width = timing.shape[0] // 2
    ladder = jnp.arange(half_width, dtype=jnp.float32)
    frequency = jnp.exp(-math.log(10000.0) * ladder / float(half_width))
    angles = step_value.astype(jnp.float32) * frequency
    feature = jnp.concatenate([jnp.sin(angles), jnp.cos(angles)])
    return jnp.dot(feature[None, :], timing.astype(jnp.float32), precision=lax.Precision.HIGHEST)[0]


def conv_valid(padded, weight):
    in_chan = padded.shape[0]
    out_rows = padded.shape[1] - 2
    out_cols = padded.shape[2] - 2
    out_chan = weight.shape[2]
    stacked = jnp.concatenate(
        [padded[:, :, offset : offset + out_cols] for offset in range(3)], axis=0
    )
    accumulated = jnp.zeros((out_chan, out_rows * out_cols), jnp.float32)
    for offset in range(3):
        tap_matrix = jnp.transpose(weight[offset], (1, 0, 2)).reshape(out_chan, 3 * in_chan)
        window = stacked[:, offset : offset + out_rows, :].reshape(3 * in_chan, out_rows * out_cols)
        accumulated = accumulated + jnp.dot(tap_matrix, window, preferred_element_type=jnp.float32)
    return accumulated.reshape(out_chan, out_rows, out_cols)


def pad_cols(values):
    return jnp.pad(values, ((0, 0), (0, 0), (1, 1)))


def normalize(hidden, scale):
    values = hidden.astype(jnp.float32)
    mean_square = jnp.mean(values * values, axis=0, keepdims=True)
    return jax.nn.silu(values * lax.rsqrt(mean_square + 1e-06) * scale[:, None, None]).astype(
        jnp.bfloat16
    )


def refine(values, axis):
    count = values.shape[axis] - 2
    before = lax.slice_in_dim(values, 0, count, axis=axis)
    middle = lax.slice_in_dim(values, 1, count + 1, axis=axis)
    after = lax.slice_in_dim(values, 2, count + 2, axis=axis)
    pieces = [
        0.375 * before + 0.625 * middle,
        0.125 * before + 0.875 * middle,
        0.875 * middle + 0.125 * after,
        0.625 * middle + 0.375 * after,
    ]
    stacked = jnp.stack(pieces, axis=axis + 1)
    shape = values.shape[:axis] + (4 * count,) + values.shape[axis + 1 :]
    return stacked.reshape(shape)


def clamp_edge(padded, axis, first_dev, last_dev):
    length = padded.shape[axis]
    head = jnp.where(
        first_dev,
        lax.slice_in_dim(padded, 1, 2, axis=axis),
        lax.slice_in_dim(padded, 0, 1, axis=axis),
    )
    tail = jnp.where(
        last_dev,
        lax.slice_in_dim(padded, length - 2, length - 1, axis=axis),
        lax.slice_in_dim(padded, length - 1, length, axis=axis),
    )
    return jnp.concatenate(
        [head, lax.slice_in_dim(padded, 1, length - 1, axis=axis), tail], axis=axis
    )


def body(
    step_index,
    coarse_state,
    coarse_forcing,
    fine_state,
    land_mask,
    inlet_one,
    timing_one,
    scale_one,
    middle_one,
    outlet_one,
    inlet_two,
    timing_two,
    land_bias,
    middle_two,
    outlet_two,
):
    keep_one, blend_one = plan(step_index[0])
    keep_two, blend_two = plan(step_index[1])
    coarse_input = jnp.concatenate([coarse_state.astype(jnp.bfloat16), coarse_forcing], axis=0)
    bias_one = embedding(step_index[0], timing_one)
    padded = with_halo(coarse_input, (("row", 1), ("col", 2)), 1)
    hidden_one = jax.nn.silu(conv_valid(padded, inlet_one) + bias_one[:, None, None]).astype(
        jnp.bfloat16
    )
    active_one = normalize(hidden_one, scale_one)
    padded_act = with_halo(active_one, (("row", 1), ("col", 2)), 1)
    summed_one = (hidden_one.astype(jnp.float32) + conv_valid(padded_act, middle_one)).astype(
        jnp.bfloat16
    )
    padded_sum = with_halo(summed_one, (("row", 1), ("col", 2)), 1)
    noise_one = conv_valid(padded_sum, outlet_one)
    coarse_next = keep_one * coarse_state + blend_one * noise_one
    rimmed = with_halo(coarse_next, (("row", 1), ("col", 2)), 1)
    row_last = lax.axis_size("row") - 1
    col_last = lax.axis_size("col") - 1
    rimmed = clamp_edge(rimmed, 1, lax.axis_index("row") == 0, lax.axis_index("row") == row_last)
    vertical = refine(rimmed, 1)
    vertical = clamp_edge(
        vertical, 2, lax.axis_index("col") == 0, lax.axis_index("col") == col_last
    )
    refined = refine(vertical, 2)
    lifted = lax.all_to_all(
        refined.astype(jnp.bfloat16), "col", split_axis=1, concat_axis=2, tiled=True
    ).astype(refined.dtype)
    fine_input = jnp.concatenate(
        [
            fine_state.astype(jnp.bfloat16),
            lifted.astype(jnp.bfloat16),
            land_mask.astype(jnp.bfloat16)[None],
        ],
        axis=0,
    )
    bias_two = embedding(step_index[1], timing_two)
    padded_two = with_halo(fine_input, ((("row", "col"), 1),), 1)
    land_float = fine_input[-1].astype(jnp.float32)
    before_act = (
        conv_valid(pad_cols(padded_two), inlet_two)
        + bias_two[:, None, None]
        + land_bias[:, None, None] * land_float[None]
    )
    hidden_two = jax.nn.silu(before_act).astype(jnp.bfloat16)
    padded_hidden = with_halo(hidden_two, ((("row", "col"), 1),), 1)
    summed_two = (
        hidden_two.astype(jnp.float32) + conv_valid(pad_cols(padded_hidden), middle_two)
    ).astype(jnp.bfloat16)
    padded_summed = with_halo(summed_two, ((("row", "col"), 1),), 1)
    noise_two = conv_valid(pad_cols(padded_summed), outlet_two)
    fine_next = keep_two * fine_state + blend_two * noise_two
    return (coarse_next, noise_one, fine_next, noise_two)


def solution(mesh):
    return jax.shard_map(
        body,
        mesh=mesh,
        in_specs=(
            P(),
            P(None, "row", "col"),
            P(None, "row", "col"),
            P(None, ("row", "col"), None),
            P(("row", "col"), None),
            P(),
            P(),
            P(),
            P(),
            P(),
            P(),
            P(),
            P(),
            P(),
            P(),
        ),
        out_specs=(
            P(None, "row", "col"),
            P(None, "row", "col"),
            P(None, ("row", "col"), None),
            P(None, ("row", "col"), None),
        ),
        check_vma=False,
    )
```

profile of v0, /device:TPU:1, one launch (start us, length us, event | category | flops | bytes accessed | tf_op | source)
XLA Modules:
  0.0 513.4 jit_solution(11680174473376910360)
XLA Ops:
  2.3 3.9 collective-permute-start
  11.7 5.2 %collective-permute-start.2 = (bf16[16,34,1]{2,1,0:T(8,128)(2,1)S(1)}, bf16[16,34,1]{2,1,0:T(8,128)(2,1)S(1)}, u32[]{:S(2)}, u32[]{:S(2)}) collective-permute-start(bf16[16,34,1]{2,1,0:T(8,128)(2,1)S(1)} %get-tuple-element.87), channel_id=1, source_target_pairs={{0,1},{1,2},{2,3},{3,4},{4,5},{5,6},{6,7},{8,9},{9,10},{10,11},{11... | collective-permute-start | bytes 3272 | tf_op jit(solution)/shard_map/ppermute | solution.py:17
  19.2 4.4 collective-permute-done.3
  28.4 4.0 collective-permute-start.4
  33.7 3.3 collective-permute-done.5
  37.1 3.2 collective-permute-start.6
  43.3 2.2 collective-permute-done.7
  45.5 5.9 %fusion.16 = bf16[384,34,128]{0,2,1:T(8,128)(2,1)S(1)} fusion(bf16[128,34,1]{0,2,1:T(2,128)(2,1)} %collective-permute-done.7, bf16[128,1,128]{0,2,1:T(8,128)(2,1)S(1)} %collective-permute-done.5, bf16[128,32,128]{0,2,1:T(8,128)(2,1)S(1)} %fusion.24, bf16[128,1,128]{0,2,1:T(8,128)(2,1)S(1)} %collective-permute-done.4, ...), kind=kLoop, calls=%fused_computation.49 | loop fusion | flops 36765696 | bytes 4473856 | tf_op jit(solution)/shard_map/concatenate | solution.py:55
  56.8 3.8 collective-permute-start.8
  61.9 3.3 collective-permute-done.9
  65.3 3.3 collective-permute-start.10
  68.5 2.2 collective-permute-start.11
  71.2 2.5 collective-permute-done.11
  73.6 5.1 fusion.14
  84.0 2.5 collective-permute-start.12
  87.8 3.0 collective-permute-done.13
  91.0 3.4 collective-permute-start.14
  96.6 4.4 collective-permute-done.15
  105.6 3.0 copy.89
  108.6 4.3 all-to-all-start
  115.4 23.5 %all-to-all-done = bf16[8,128,512]{2,0,1:T(8,128)(2,1)} async-done(((bf16[8,128,512]{2,0,1:T(8,128)(2,1)}), bf16[8,128,512]{2,0,1:T(8,128)(2,1)}, u32[]{:S(2)}, u32[]{:S(2)}) %all-to-all-start) | async-done | bytes 1048608 | tf_op jit(solution)/shard_map/all_to_all | solution.py:153
  141.2 2.2 pad_maximum_fusion.30
  145.4 2.4 collective-permute-start.17
  149.1 7.1 %collective-permute-done.17 = bf16[17,1,4096]{2,1,0:T(2,128)(2,1)S(1)} collective-permute-done((bf16[17,1,4096]{2,1,0:T(2,128)(2,1)S(1)}, bf16[17,1,4096]{2,1,0:T(2,128)(2,1)S(1)}, u32[]{:S(2)}, u32[]{:S(2)}) %collective-permute-start.17) | collective-permute-done | bytes 139296 | tf_op jit(solution)/shard_map/ppermute | solution.py:19
  156.2 7.6 %select_maximum_fusion.2 = bf16[17,18,4098]{2,1,0:T(8,128)(2,1)S(1)} fusion(bf16[17,1,4096]{2,1,0:T(2,128)(2,1)S(1)} %collective-permute-done.17, bf16[17,1,4096]{2,1,0:T(2,128)(2,1)S(1)} %collective-permute-done.16, bf16[1,16,4096]{2,1,0:T(8,128)(2,1)} %get-tuple-element.82, bf16[8,16,4096]{2,1,0:T(8,128)(2,1)S(1)} %all_to_all.16, ...), kind=kLoop, calls=%fused_computation.33 | loop fusion | flops 22571784 | bytes 5014728 | tf_op jit(solution)/shard_map/concatenate | solution.py:15
  165.6 4.1 pad_maximum_fusion.2
  169.7 15.2 %fusion.61 = (bf16[51,16,4096]{2,1,0:T(8,128)(2,1)}, bf16[51,16,4096]{2,1,0:T(8,128)(2,1)}, bf16[51,16,4096]{2,1,0:T(8,128)(2,1)S(1)}) fusion(bf16[51,18,4096]{2,1,0:T(8,128)(2,1)S(1)} %pad_maximum_fusion.2), kind=kLoop, calls=%fused_computation.164 | loop fusion | bytes 40108032 | tf_op jit(solution)/shard_map/slice | solution.py:61
  184.9 3.6 pad.240
  188.5 7.7 %copy.111 = bf16[7,8,16,4096]{3,1,2,0:T(8,128)(2,1)S(1)} copy(bf16[7,8,16,4096]{3,2,1,0:T(8,128)(2,1)} %bitcast.265) | data formatting | bytes 14680064
  196.2 6.8 %pad.241 = bf16[56,16,4096]{2,1,0:T(8,128)(2,1)} pad(bf16[51,16,4096]{2,1,0:T(8,128)(2,1)} %get-tuple-element.35, bf16[]{:T(256)} %constant.69.clone.1), padding=0_5x0_0x0_0 | pad | bytes 14024706
  203.0 10.6 %copy.112 = bf16[7,8,16,4096]{3,1,2,0:T(8,128)(2,1)} copy(bf16[7,8,16,4096]{3,2,1,0:T(8,128)(2,1)} %bitcast.266) | data formatting | bytes 14680064
  213.7 6.8 %pad.242 = bf16[56,16,4096]{2,1,0:T(8,128)(2,1)} pad(bf16[51,16,4096]{2,1,0:T(8,128)(2,1)} %get-tuple-element.34, bf16[]{:T(256)} %constant.69.clone.1), padding=0_5x0_0x0_0 | pad | bytes 14024706
  220.5 11.0 %copy.113 = bf16[7,8,16,4096]{3,1,2,0:T(8,128)(2,1)} copy(bf16[7,8,16,4096]{3,2,1,0:T(8,128)(2,1)} %bitcast.264) | data formatting | bytes 14680064
  232.8 4.7 convolution_add_fusion.3
  237.5 4.7 convolution_add_fusion.2
  242.2 4.9 copy.114
  247.1 3.3 multiply_convert_fusion
  254.3 2.4 collective-permute-start.19
  257.1 3.3 collective-permute-done.18
  260.4 10.0 %collective-permute-done.19 = bf16[32,1,4096]{2,1,0:T(2,128)(2,1)S(1)} collective-permute-done((bf16[32,1,4096]{2,1,0:T(2,128)(2,1)S(1)}, bf16[32,1,4096]{2,1,0:T(2,128)(2,1)S(1)}, u32[]{:S(2)}, u32[]{:S(2)}) %collective-permute-start.19) | collective-permute-done | bytes 262176 | tf_op jit(solution)/shard_map/ppermute | solution.py:19
  270.4 11.8 %fusion.8 = bf16[32,18,4098]{2,1,0:T(8,128)(2,1)S(1)} fusion(bf16[32,1,4096]{2,1,0:T(2,128)(2,1)S(1)} %collective-permute-done.19, bf16[32,16,4096]{2,1,0:T(8,128)(2,1)} %copy-done.3, bf16[32,1,4096]{2,1,0:T(2,128)(2,1)S(1)} %collective-permute-done.18), kind=kLoop, calls=%fused_computation.26 | loop fusion | flops 28325376 | bytes 9439488 | tf_op jit(solution)/shard_map/concatenate | solution.py:15
  282.1 6.1 %fusion.63 = (bf16[32,18,4096]{2,1,0:T(8,128)(2,1)}, bf16[32,18,4096]{2,1,0:T(8,128)(2,1)}) fusion(bf16[32,18,4098]{2,1,0:T(8,128)(2,1)S(1)} %fusion.8), kind=kLoop, calls=%fused_computation.166 | loop fusion | bytes 18874368 | tf_op jit(solution)/shard_map/slice | solution.py:56
  288.3 9.7 %pad_maximum_fusion = bf16[96,18,4096]{2,1,0:T(8,128)(2,1)S(1)} fusion(bf16[32,18,4096]{2,1,0:T(8,128)(2,1)} %get-tuple-element.40, bf16[32,1,4096]{2,1,0:T(2,128)(2,1)S(1)} %collective-permute-done.19, bf16[32,16,4096]{2,1,0:T(8,128)(2,1)S(1)} %copy-done.4, bf16[32,1,4096]{2,1,0:T(2,128)(2,1)S(1)} %collective-permute-done.18, ...), kind=kLoop, calls=%fused_computation.8 | loop fusion | flops 70778880 | bytes 28311552 | tf_op jit(solution)/shard_map/concatenate | solution.py:55
  297.9 13.4 %fusion.60 = (bf16[96,16,4096]{2,1,0:T(8,128)(2,1)}, bf16[96,16,4096]{2,1,0:T(8,128)(2,1)}, bf16[96,16,4096]{2,1,0:T(8,128)(2,1)}) fusion(bf16[96,18,4096]{2,1,0:T(8,128)(2,1)S(1)} %pad_maximum_fusion), kind=kLoop, calls=%fused_computation.163 | loop fusion | bytes 75497472 | tf_op jit(solution)/shard_map/slice | solution.py:61
  311.4 16.8 %copy.115 = bf16[12,8,16,4096]{3,1,2,0:T(8,128)(2,1)} copy(bf16[12,8,16,4096]{3,2,1,0:T(8,128)(2,1)} %bitcast.256) | data formatting | bytes 25165824
  328.2 8.7 %copy.116 = bf16[12,8,16,4096]{3,1,2,0:T(8,128)(2,1)} copy(bf16[12,8,16,4096]{3,2,1,0:T(8,128)(2,1)S(1)} %bitcast.252) | data formatting | bytes 25165824
  336.9 17.1 %copy.117 = bf16[12,8,16,4096]{3,1,2,0:T(8,128)(2,1)S(1)} copy(bf16[12,8,16,4096]{3,2,1,0:T(8,128)(2,1)S(1)} %bitcast.248) | data formatting | bytes 25165824
  354.0 9.6 %fusion.81 = f32[65536,32]{0,1:T(8,128)} fusion(bf16[32,96]{1,0:T(8,128)(2,1)S(1)} %reshape.201, bf16[96,65536]{1,0:T(8,128)(2,1)} %bitcast.258), kind=kOutput, calls=%fused_computation.184 | convolution fusion | flops 402653184 | bytes 20977664 | tf_op jit(solution)/shard_map/dot_general | solution.py:62
  363.6 12.2 %convolution_add_fusion.1 = f32[65536,32]{0,1:T(8,128)} fusion(f32[65536,32]{0,1:T(8,128)} %fusion.81, bf16[32,96]{1,0:T(8,128)(2,1)S(1)} %reshape.203, bf16[96,65536]{1,0:T(8,128)(2,1)} %bitcast.244), kind=kOutput, calls=%fused_computation.1 | convolution fusion | flops 404750336 | bytes 29366272 | tf_op jit(solution)/shard_map/dot_general | solution.py:62
  375.8 6.8 %convolution_add_fusion = f32[65536,32]{0,1:T(8,128)} fusion(f32[65536,32]{0,1:T(8,128)} %convolution_add_fusion.1, bf16[32,96]{1,0:T(8,128)(2,1)S(1)} %reshape.205, bf16[96,65536]{1,0:T(8,128)(2,1)S(1)} %bitcast.243), kind=kOutput, calls=%fused_computation | convolution fusion | flops 404750336 | bytes 29366272 | tf_op jit(solution)/shard_map/dot_general | solution.py:62
  382.6 8.2 %copy.118 = f32[4,8,16,4096]{3,2,1,0:T(8,128)S(1)} copy(f32[4,8,16,4096]{3,1,2,0:T(8,128)} %bitcast.261) | data formatting | bytes 16777216
  390.9 4.1 fusion.1
  400.0 2.4 collective-permute-start.21
  403.2 2.9 collective-permute-done.20
  406.1 8.6 %collective-permute-done.21 = bf16[32,1,4096]{2,1,0:T(2,128)(2,1)S(1)} collective-permute-done((bf16[32,1,4096]{2,1,0:T(2,128)(2,1)S(1)}, bf16[32,1,4096]{2,1,0:T(2,128)(2,1)S(1)}, u32[]{:S(2)}, u32[]{:S(2)}) %collective-permute-start.21) | collective-permute-done | bytes 262176 | tf_op jit(solution)/shard_map/ppermute | solution.py:19
  414.7 11.8 %select_maximum_fusion = bf16[32,18,4098]{2,1,0:T(8,128)(2,1)S(1)} fusion(bf16[32,1,4096]{2,1,0:T(2,128)(2,1)S(1)} %collective-permute-done.21, bf16[32,16,4096]{2,1,0:T(8,128)(2,1)} %copy-done.5, bf16[32,1,4096]{2,1,0:T(2,128)(2,1)S(1)} %collective-permute-done.20), kind=kLoop, calls=%fused_computation.20 | loop fusion | flops 28325376 | bytes 9439488 | tf_op jit(solution)/shard_map/concatenate | solution.py:15
  426.5 6.1 %fusion.62 = (bf16[32,18,4096]{2,1,0:T(8,128)(2,1)}, bf16[32,18,4096]{2,1,0:T(8,128)(2,1)}) fusion(bf16[32,18,4098]{2,1,0:T(8,128)(2,1)S(1)} %select_maximum_fusion), kind=kLoop, calls=%fused_computation.165 | loop fusion | bytes 18874368 | tf_op jit(solution)/shard_map/slice | solution.py:56
  432.6 9.7 %pad_maximum_fusion.1 = bf16[96,18,4096]{2,1,0:T(8,128)(2,1)S(1)} fusion(bf16[32,18,4096]{2,1,0:T(8,128)(2,1)} %get-tuple-element.38, bf16[32,1,4096]{2,1,0:T(2,128)(2,1)S(1)} %collective-permute-done.21, bf16[32,16,4096]{2,1,0:T(8,128)(2,1)S(1)} %copy-done.6, bf16[32,1,4096]{2,1,0:T(2,128)(2,1)S(1)} %collective-permute-done.20, ...), kind=kLoop, calls=%fused_computation.9 | loop fusion | flops 70778880 | bytes 28311552 | tf_op jit(solution)/shard_map/concatenate | solution.py:55
  442.3 13.4 %fusion.59 = (bf16[96,16,4096]{2,1,0:T(8,128)(2,1)}, bf16[96,16,4096]{2,1,0:T(8,128)(2,1)}, bf16[96,16,4096]{2,1,0:T(8,128)(2,1)}) fusion(bf16[96,18,4096]{2,1,0:T(8,128)(2,1)S(1)} %pad_maximum_fusion.1), kind=kLoop, calls=%fused_computation.162 | loop fusion | bytes 75497472 | tf_op jit(solution)/shard_map/slice | solution.py:61
  455.7 16.7 %copy.119 = bf16[12,8,16,4096]{3,1,2,0:T(8,128)(2,1)} copy(bf16[12,8,16,4096]{3,2,1,0:T(8,128)(2,1)} %bitcast.257) | data formatting | bytes 25165824
  472.4 16.7 %copy.120 = bf16[12,8,16,4096]{3,1,2,0:T(8,128)(2,1)S(1)} copy(bf16[12,8,16,4096]{3,2,1,0:T(8,128)(2,1)S(1)} %bitcast.255) | data formatting | bytes 25165824
  489.1 11.4 %copy.121 = bf16[12,8,16,4096]{3,1,2,0:T(8,128)(2,1)S(1)} copy(bf16[12,8,16,4096]{3,2,1,0:T(8,128)(2,1)} %bitcast.249) | data formatting | bytes 25165824
  500.5 5.7 %fusion.80 = f32[65536,8]{0,1:T(8,128)S(1)} fusion(bf16[96,65536]{1,0:T(8,128)(2,1)} %bitcast.245, bf16[8,96]{1,0:T(8,128)(2,1)S(1)} %reshape.208), kind=kOutput, calls=%fused_computation.183 | convolution fusion | flops 100663296 | bytes 14681600 | tf_op jit(solution)/shard_map/dot_general | solution.py:62
  509.7 3.4 multiply_add_fusion
  (169 shorter events, 61.1 us)
Async XLA Ops:
  0.6 18.2 %copy-start = (bf16[128,128]{1,0:T(8,128)(2,1)S(1)}, bf16[128,128]{1,0:T(8,128)(2,1)}, u32[]{:S(2)}) copy-start(bf16[128,128]{1,0:T(8,128)(2,1)} %param.21) | copy-start | bytes 98308
  2.3 8.1 %collective-permute-start = (bf16[16,1,128]{2,1,0:T(2,128)(2,1)S(1)}, bf16[16,1,128]{2,1,0:T(2,128)(2,1)S(1)}, u32[]{:S(2)}, u32[]{:S(2)}) collective-permute-start(bf16[16,1,128]{2,1,0:T(2,128)(2,1)S(1)} %get-tuple-element.91), channel_id=1, source_target_pairs={{0,8},{8,16},{16,24},{1,9},{9,17},{17,25},{2,10},{10,18},{18,26},{... | collective-permute-start | bytes 12296 | tf_op jit(solution)/shard_map/ppermute | solution.py:17
  6.3 4.4 collective-permute-start.1
  11.7 7.4 %collective-permute-start.2 = (bf16[16,34,1]{2,1,0:T(8,128)(2,1)S(1)}, bf16[16,34,1]{2,1,0:T(8,128)(2,1)S(1)}, u32[]{:S(2)}, u32[]{:S(2)}) collective-permute-start(bf16[16,34,1]{2,1,0:T(8,128)(2,1)S(1)} %get-tuple-element.87), channel_id=1, source_target_pairs={{0,1},{1,2},{2,3},{3,4},{4,5},{5,6},{6,7},{8,9},{9,10},{10,11},{11... | collective-permute-start | bytes 3272 | tf_op jit(solution)/shard_map/ppermute | solution.py:17
  16.9 6.6 %collective-permute-start.3 = (bf16[16,34,1]{2,1,0:T(8,128)(2,1)S(1)}, bf16[16,34,1]{2,1,0:T(8,128)(2,1)S(1)}, u32[]{:S(2)}, u32[]{:S(2)}) collective-permute-start(bf16[16,34,1]{2,1,0:T(8,128)(2,1)S(1)} %get-tuple-element.88), channel_id=1, source_target_pairs={{1,0},{2,1},{3,2},{4,3},{5,4},{6,5},{7,6},{9,8},{10,9},{11,10},{12... | collective-permute-start | bytes 3272 | tf_op jit(solution)/shard_map/ppermute | solution.py:19
  26.1 1.1 copy-start.20
  26.1 16.2 %copy-start.13 = (bf16[3,3,128,128]{3,2,1,0:T(8,128)(2,1)S(1)}, bf16[3,3,128,128]{3,2,1,0:T(8,128)(2,1)}, u32[]{:S(2)}) copy-start(bf16[3,3,128,128]{3,2,1,0:T(8,128)(2,1)} %param.23) | copy-start | bytes 884740
  28.4 5.3 %collective-permute-start.4 = (bf16[128,1,128]{0,2,1:T(8,128)(2,1)S(1)}, bf16[128,1,128]{0,2,1:T(8,128)(2,1)S(1)}, u32[]{:S(2)}, u32[]{:S(2)}) collective-permute-start(bf16[128,1,128]{0,2,1:T(8,128)(2,1)S(1)} %get-tuple-element.67), channel_id=1, source_target_pairs={{0,8},{8,16},{16,24},{1,9},{9,17},{17,25},{2,10},{10,18},{18,26},{... | collective-permute-start | bytes 98312 | tf_op jit(solution)/shard_map/ppermute | solution.py:17
  32.4 4.7 collective-permute-start.5
  37.1 6.2 %collective-permute-start.6 = (bf16[128,34,1]{0,2,1:T(2,128)(2,1)S(1)}, bf16[128,34,1]{0,2,1:T(2,128)(2,1)}, u32[]{:S(2)}, u32[]{:S(2)}) collective-permute-start(bf16[128,34,1]{0,2,1:T(2,128)(2,1)S(1)} %get-tuple-element.57), channel_id=1, source_target_pairs={{0,1},{1,2},{2,3},{3,4},{4,5},{5,6},{6,7},{8,9},{9,10},{10,11},{11... | collective-permute-start | bytes 26120 | tf_op jit(solution)/shard_map/ppermute | solution.py:17
  40.3 5.2 %collective-permute-start.7 = (bf16[128,34,1]{0,2,1:T(2,128)(2,1)S(1)}, bf16[128,34,1]{0,2,1:T(2,128)(2,1)}, u32[]{:S(2)}, u32[]{:S(2)}) collective-permute-start(bf16[128,34,1]{0,2,1:T(2,128)(2,1)S(1)} %get-tuple-element.58), channel_id=1, source_target_pairs={{1,0},{2,1},{3,2},{4,3},{5,4},{6,5},{7,6},{9,8},{10,9},{11,10},{12... | collective-permute-start | bytes 26120 | tf_op jit(solution)/shard_map/ppermute | solution.py:19
  51.4 1.8 copy-start.12
  56.8 5.1 collective-permute-start.8
  60.6 4.7 collective-permute-start.9
  65.3 5.9 %collective-permute-start.10 = (bf16[128,34,1]{0,2,1:T(2,128)(2,1)S(1)}, bf16[128,34,1]{0,2,1:T(2,128)(2,1)S(1)}, u32[]{:S(2)}, u32[]{:S(2)}) collective-permute-start(bf16[128,34,1]{0,2,1:T(2,128)(2,1)S(1)} %get-tuple-element.55), channel_id=1, source_target_pairs={{0,1},{1,2},{2,3},{3,4},{4,5},{5,6},{6,7},{8,9},{9,10},{10,11},{11... | collective-permute-start | bytes 26120 | tf_op jit(solution)/shard_map/ppermute | solution.py:17
  68.5 5.1 collective-permute-start.11
  78.7 1.8 copy-start.16
  81.4 1.9 copy-start.11
  84.0 19.6 %copy-start.9 = (f32[8,32,128]{2,1,0:T(8,128)}, f32[8,32,128]{2,1,0:T(8,128)S(1)}, u32[]{:S(2)}) copy-start(f32[8,32,128]{2,1,0:T(8,128)S(1)} %get-tuple-element.26) | copy-start | bytes 393220
  84.0 3.8 collective-permute-start.12
  86.5 4.4 collective-permute-start.13
  91.0 5.6 %collective-permute-start.14 = (f32[8,34,1]{2,1,0:T(8,128)S(1)}, f32[8,34,1]{2,1,0:T(8,128)S(1)}, u32[]{:S(2)}, u32[]{:S(2)}) collective-permute-start(f32[8,34,1]{2,1,0:T(8,128)S(1)} %get-tuple-element.85), channel_id=1, source_target_pairs={{0,1},{1,2},{2,3},{3,4},{4,5},{5,6},{6,7},{8,9},{9,10},{10,11},{11... | collective-permute-start | bytes 3272 | tf_op jit(solution)/shard_map/ppermute | solution.py:17
  94.4 6.6 %collective-permute-start.15 = (f32[8,34,1]{2,1,0:T(8,128)S(1)}, f32[8,34,1]{2,1,0:T(8,128)S(1)}, u32[]{:S(2)}, u32[]{:S(2)}) collective-permute-start(f32[8,34,1]{2,1,0:T(8,128)S(1)} %get-tuple-element.86), channel_id=1, source_target_pairs={{1,0},{2,1},{3,2},{4,3},{5,4},{6,5},{7,6},{9,8},{10,9},{11,10},{12... | collective-permute-start | bytes 3272 | tf_op jit(solution)/shard_map/ppermute | solution.py:19
  102.7 10.2 %copy-start.7 = (f32[8,16,4096]{2,1,0:T(8,128)S(1)}, f32[8,16,4096]{2,1,0:T(8,128)}, u32[]{:S(2)}) copy-start(f32[8,16,4096]{2,1,0:T(8,128)} %param.18) | copy-start | bytes 6291460
  103.0 10.7 %copy-start.15 = (bf16[3,3,32,17]{2,1,3,0:T(4,128)(2,1)S(1)}, bf16[3,3,32,17]{2,1,3,0:T(4,128)(2,1)}, u32[]{:S(2)}) copy-start(bf16[3,3,32,17]{2,1,3,0:T(4,128)(2,1)} %param.25) | copy-start | bytes 29380
  108.6 39.4 %copy-start.18 = (bf16[128,32]{0,1:T(8,128)(2,1)S(1)}, bf16[128,32]{0,1:T(8,128)(2,1)}, u32[]{:S(2)}) copy-start(bf16[128,32]{0,1:T(8,128)(2,1)} %param.26) | copy-start | bytes 24580
  108.6 30.3 %all-to-all-start = ((bf16[8,128,512]{2,0,1:T(8,128)(2,1)}), bf16[8,128,512]{2,0,1:T(8,128)(2,1)}, u32[]{:S(2)}, u32[]{:S(2)}) async-start(bf16[8,128,512]{2,0,1:T(8,128)(2,1)} %copy.89), calls=%async_computation | async-start | bytes 2097152 | tf_op jit(solution)/shard_map/all_to_all | solution.py:153
  143.4 5.7 %collective-permute-start.16 = (bf16[17,1,4096]{2,1,0:T(2,128)(2,1)}, bf16[17,1,4096]{2,1,0:T(2,128)(2,1)S(1)}, u32[]{:S(2)}, u32[]{:S(2)}) collective-permute-start(bf16[17,1,4096]{2,1,0:T(2,128)(2,1)} %get-tuple-element.53), channel_id=1, source_target_pairs={{0,1},{1,2},{2,3},{3,4},{4,5},{5,6},{6,7},{7,8},{8,9},{9,10},{10,1... | collective-permute-start | bytes 417800 | tf_op jit(solution)/shard_map/ppermute | solution.py:17
  145.4 10.9 %collective-permute-start.17 = (bf16[17,1,4096]{2,1,0:T(2,128)(2,1)S(1)}, bf16[17,1,4096]{2,1,0:T(2,128)(2,1)S(1)}, u32[]{:S(2)}, u32[]{:S(2)}) collective-permute-start(bf16[17,1,4096]{2,1,0:T(2,128)(2,1)S(1)} %get-tuple-element.54), channel_id=1, source_target_pairs={{1,0},{2,1},{3,2},{4,3},{5,4},{6,5},{7,6},{8,7},{9,8},{10,9},{11,1... | collective-permute-start | bytes 417800 | tf_op jit(solution)/shard_map/ppermute | solution.py:19
  163.9 1.7 copy-start.10
  242.2 4.9 copy-start.19
  247.0 4.5 copy-start.2
  247.1 9.6 %copy-start.14 = (bf16[3,3,32,32]{3,2,1,0:T(8,128)(2,1)S(1)}, bf16[3,3,32,32]{3,2,1,0:T(8,128)(2,1)}, u32[]{:S(2)}) copy-start(bf16[3,3,32,32]{3,2,1,0:T(8,128)(2,1)} %param.28) | copy-start | bytes 55300
  250.4 2.0 copy-start.3
  252.3 8.0 %collective-permute-start.18 = (bf16[32,1,4096]{2,1,0:T(2,128)(2,1)S(1)}, bf16[32,1,4096]{2,1,0:T(2,128)(2,1)S(1)}, u32[]{:S(2)}, u32[]{:S(2)}) collective-permute-start(bf16[32,1,4096]{2,1,0:T(2,128)(2,1)S(1)} %get-tuple-element.43), channel_id=1, source_target_pairs={{0,1},{1,2},{2,3},{3,4},{4,5},{5,6},{6,7},{7,8},{8,9},{9,10},{10,1... | collective-permute-start | bytes 786440 | tf_op jit(solution)/shard_map/ppermute | solution.py:17
  254.3 16.1 %collective-permute-start.19 = (bf16[32,1,4096]{2,1,0:T(2,128)(2,1)S(1)}, bf16[32,1,4096]{2,1,0:T(2,128)(2,1)S(1)}, u32[]{:S(2)}, u32[]{:S(2)}) collective-permute-start(bf16[32,1,4096]{2,1,0:T(2,128)(2,1)S(1)} %get-tuple-element.44), channel_id=1, source_target_pairs={{1,0},{2,1},{3,2},{4,3},{5,4},{6,5},{7,6},{8,7},{9,8},{10,9},{11,1... | collective-permute-start | bytes 786440 | tf_op jit(solution)/shard_map/ppermute | solution.py:19
  282.1 6.1 %copy-start.4 = (bf16[32,16,4096]{2,1,0:T(8,128)(2,1)S(1)}, bf16[32,16,4096]{2,1,0:T(8,128)(2,1)}, u32[]{:S(2)}) copy-start(bf16[32,16,4096]{2,1,0:T(8,128)(2,1)} %copy-done.3) | copy-start | bytes 12582916
  311.3 16.8 %slice-start.5 = ((s8[12582912]{0:T(1024)(128)(4,1)}), s8[4194304]{0:T(1024)(128)(4,1)S(1)}, s32[]{:S(2)}) async-start(s8[12582912]{0:T(1024)(128)(4,1)} %bitcast.250), calls=%async_computation.6 | async-start | bytes 8388608
  311.3 16.8 %slice-start.6 = ((s8[12582912]{0:T(1024)(128)(4,1)}), s8[4194304]{0:T(1024)(128)(4,1)S(1)}, s32[]{:S(2)}) async-start(s8[12582912]{0:T(1024)(128)(4,1)} %bitcast.250), calls=%async_computation.7 | async-start | bytes 8388608
  311.3 16.8 %slice-start.7 = ((s8[12582912]{0:T(1024)(128)(4,1)}), s8[4194304]{0:T(1024)(128)(4,1)S(1)}, s32[]{:S(2)}) async-start(s8[12582912]{0:T(1024)(128)(4,1)} %bitcast.250), calls=%async_computation.8 | async-start | bytes 8388608
  328.1 8.8 %slice-start.2 = ((s8[12582912]{0:T(1024)(128)(4,1)}), s8[4194304]{0:T(1024)(128)(4,1)S(1)}, s32[]{:S(2)}) async-start(s8[12582912]{0:T(1024)(128)(4,1)} %bitcast.246), calls=%async_computation.3 | async-start | bytes 8388608
  328.2 8.8 %slice-start.3 = ((s8[12582912]{0:T(1024)(128)(4,1)}), s8[4194304]{0:T(1024)(128)(4,1)S(1)}, s32[]{:S(2)}) async-start(s8[12582912]{0:T(1024)(128)(4,1)} %bitcast.246), calls=%async_computation.4 | async-start | bytes 8388608
  328.2 8.8 %slice-start.4 = ((s8[12582912]{0:T(1024)(128)(4,1)}), s8[4194304]{0:T(1024)(128)(4,1)S(1)}, s32[]{:S(2)}) async-start(s8[12582912]{0:T(1024)(128)(4,1)} %bitcast.246), calls=%async_computation.5 | async-start | bytes 8388608
  363.6 27.2 %slice-start = ((s8[8388608]{0:T(1024)(128)(4,1)}), s8[4194304]{0:T(1024)(128)(4,1)S(1)}, s32[]{:S(2)}) async-start(s8[8388608]{0:T(1024)(128)(4,1)} %bitcast.239), calls=%async_computation.1 | async-start | bytes 8388608
  375.8 15.1 %slice-start.1 = ((s8[8388608]{0:T(1024)(128)(4,1)}), s8[4194304]{0:T(1024)(128)(4,1)S(1)}, s32[]{:S(2)}) async-start(s8[8388608]{0:T(1024)(128)(4,1)} %bitcast.239), calls=%async_computation.2 | async-start | bytes 8388608
  390.9 11.9 %copy-start.17 = (bf16[3,3,8,32]{3,2,1,0:T(8,128)(2,1)S(1)}, bf16[3,3,8,32]{3,2,1,0:T(8,128)(2,1)}, u32[]{:S(2)}) copy-start(bf16[3,3,8,32]{3,2,1,0:T(8,128)(2,1)} %param.29) | copy-start | bytes 13828
  395.0 2.0 copy-start.5
  398.1 8.0 %collective-permute-start.20 = (bf16[32,1,4096]{2,1,0:T(2,128)(2,1)S(1)}, bf16[32,1,4096]{2,1,0:T(2,128)(2,1)S(1)}, u32[]{:S(2)}, u32[]{:S(2)}) collective-permute-start(bf16[32,1,4096]{2,1,0:T(2,128)(2,1)S(1)} %get-tuple-element.41), channel_id=1, source_target_pairs={{0,1},{1,2},{2,3},{3,4},{4,5},{5,6},{6,7},{7,8},{8,9},{9,10},{10,1... | collective-permute-start | bytes 786440 | tf_op jit(solution)/shard_map/ppermute | solution.py:17
  400.0 14.7 %collective-permute-start.21 = (bf16[32,1,4096]{2,1,0:T(2,128)(2,1)S(1)}, bf16[32,1,4096]{2,1,0:T(2,128)(2,1)S(1)}, u32[]{:S(2)}, u32[]{:S(2)}) collective-permute-start(bf16[32,1,4096]{2,1,0:T(2,128)(2,1)S(1)} %get-tuple-element.42), channel_id=1, source_target_pairs={{1,0},{2,1},{3,2},{4,3},{5,4},{6,5},{7,6},{8,7},{9,8},{10,9},{11,1... | collective-permute-start | bytes 786440 | tf_op jit(solution)/shard_map/ppermute | solution.py:19
  426.5 6.1 %copy-start.6 = (bf16[32,16,4096]{2,1,0:T(8,128)(2,1)S(1)}, bf16[32,16,4096]{2,1,0:T(8,128)(2,1)}, u32[]{:S(2)}) copy-start(bf16[32,16,4096]{2,1,0:T(8,128)(2,1)} %copy-done.5) | copy-start | bytes 12582916
  455.7 16.7 %slice-start.8 = ((s8[12582912]{0:T(1024)(128)(4,1)}), s8[4194304]{0:T(1024)(128)(4,1)S(1)}, s32[]{:S(2)}) async-start(s8[12582912]{0:T(1024)(128)(4,1)} %bitcast.253), calls=%async_computation.9 | async-start | bytes 8388608
  455.7 16.7 %slice-start.9 = ((s8[12582912]{0:T(1024)(128)(4,1)}), s8[4194304]{0:T(1024)(128)(4,1)S(1)}, s32[]{:S(2)}) async-start(s8[12582912]{0:T(1024)(128)(4,1)} %bitcast.253), calls=%async_computation.10 | async-start | bytes 8388608
  455.7 16.7 %slice-start.10 = ((s8[12582912]{0:T(1024)(128)(4,1)}), s8[4194304]{0:T(1024)(128)(4,1)S(1)}, s32[]{:S(2)}) async-start(s8[12582912]{0:T(1024)(128)(4,1)} %bitcast.253), calls=%async_computation.11 | async-start | bytes 8388608
  508.0 1.7 copy-start.8
  508.0 5.2 %copy-start.1 = (bf16[128,128]{1,0:T(8,128)(2,1)S(1)}, bf16[128,128]{1,0:T(8,128)(2,1)}, u32[]{:S(2)}) copy-start(bf16[128,128]{1,0:T(8,128)(2,1)} %param.21) | copy-start | bytes 98308
where the time goes:
time: 518 us; the launch traced here: 513 us
  local copies, waits for them, and re-layouts  224 us (43%)
  other arithmetic  88.6 us (17%)
  waiting for transfers between devices  80.2 us (15%)
  starting transfers between devices  59.8 us (12%)
  matrix products  56.5 us (11%)
    unnamed x81, local copies, waits for them, and re-layouts  151 us
    dot_general x18, matrix products, conv_valid(): jnp.dot(tap_matrix, window, preferred_element_type=jnp.float32)  56.2 us
    ppermute x11, waiting for transfers between devices, with_halo(): lax.ppermute(head, axis, [((i + 1) % count, i) for i in range(ends)])  49.1 us
    slice x6, local copies, waits for them, and re-layouts, conv_valid(): stacked[:, offset:offset + out_rows, :]  45.8 us
    concatenate x6, other arithmetic, conv_valid(): jnp.concatenate([padded[:, :, offset:offset + out_cols] for offset in ran...  35.7 us
    ppermute x11, starting transfers between devices, with_halo(): lax.ppermute(tail, axis, [(i, (i + 1) % count) for i in range(ends)])  35 us
    concatenate x6, other arithmetic, with_halo(): jnp.concatenate([lax.ppermute(tail, axis, [(i, (i + 1) % count) for i in...  32.3 us
    all_to_all x1, waiting for transfers between devices, body(): lax.all_to_all(refined.astype(jnp.bfloat16), 'col', split_axis=1, concat_...  23.5 us
  transfers between devices with their start and end apart: 23, of which 17 were waited for; matrix products, arithmetic and copies ran while one was open for 1% of the time, Pallas kernels for 0%

commit v1 on v0

v1 whole, which is shorter than its diff:
```python
import functools
import math

import jax
import jax.numpy as jnp
import numpy as np
from jax import lax
from jax.experimental import pallas as pl
from jax.experimental.pallas import tpu as pltpu
from jax.sharding import PartitionSpec as P

BF = jnp.bfloat16
F32 = jnp.float32
VMEM = pl.BlockSpec(memory_space=pltpu.VMEM)
SMEM = pl.BlockSpec(memory_space=pltpu.SMEM)
EDGE = 16
ROWS1 = 5
ROWS2 = 6
ROWS3 = 8
LANES = 128


def params(mib):
    return pltpu.CompilerParams(vmem_limit_bytes=mib << 20)


def silu(v):
    return v * (0.5 * jnp.tanh(0.5 * v) + 0.5)


def starts_of(rows, height):
    return [min(s, rows - height) for s in range(0, rows, height)]


def shift_pairs(count, by):
    return [(i, i + by) for i in range(count) if 0 <= i + by < count]


def alpha_bar(moment):
    return jnp.cos((moment / 1000.0 + 0.008) / 1.008 * (math.pi / 2.0)) ** 2


def plan(step_value):
    current_time = step_value.astype(F32)
    current = alpha_bar(current_time)
    earlier = alpha_bar(current_time - 50.0)
    keeping = jnp.sqrt(earlier / current)
    blending = jnp.sqrt(1.0 - earlier) - jnp.sqrt(earlier) * jnp.sqrt(1.0 - current) / jnp.sqrt(
        current
    )
    return (keeping, blending)


def embedding(step_value, timing):
    half_width = timing.shape[0] // 2
    ladder = jnp.arange(half_width, dtype=F32)
    frequency = jnp.exp(-math.log(10000.0) * ladder / float(half_width))
    angles = step_value.astype(F32) * frequency
    feature = jnp.concatenate([jnp.sin(angles), jnp.cos(angles)])
    return jnp.dot(feature[None, :], timing.astype(F32), precision=lax.Precision.HIGHEST)[0]


def pack_kernel(tile_rows, chunk, state, forcing, fine, land, pick, comb, to_next, to_prev, wide):
    wide[...] = forcing[...].astype(F32)
    for y in range(tile_rows):
        comb[y] = jnp.concatenate(
            [state[pl.ds(y, 8, stride=tile_rows), :], wide[pl.ds(y, 8, stride=tile_rows), :]], axis=0
        ).astype(BF)
    for c in range(0, fine.shape[1], chunk):
        cols = slice(c, c + chunk)
        operand = jnp.concatenate([fine[:, cols], land[:, cols].astype(F32)], axis=0).astype(BF)
        made = jnp.dot(pick[...], operand, preferred_element_type=F32).astype(BF)
        to_next[:, cols] = made[0:32]
        to_prev[:, cols] = made[32:64]


def weight_kernel(
    band, inlet_one, middle_one, outlet_one, inlet_two, middle_two, outlet_two, bias_two, land_bias,
    first_one, mid_one, last_one, first_two, mid_two, last_two, wide1, wide2, wide3,
):
    first_one[...] = jnp.zeros_like(first_one)
    for dx in range(3):
        for i in range(2):
            for dy in range(3):
                at = 192 + (i + dy) * 16
                first_one[dx, at : at + 16, i * 128 : (i + 1) * 128] = (
                    inlet_one[dy, dx].astype(F32).T.astype(BF)
                )
    mid_one[...] = jnp.zeros_like(mid_one)
    last_one[...] = jnp.zeros_like(last_one)
    for dx in range(3):
        for dy in range(3):
            turned = middle_one[dy, dx].astype(F32).T.astype(BF)
            for i in range(2):
                at = dx * 512 + (i + dy) * 128
                mid_one[at : at + 128, i * 128 : (i + 1) * 128] = turned
    for dx in range(3):
        for slot in range(2):
            pieces = []
            for i in range(2):
                halves = []
                for par in range(2):
                    dy = 2 * slot + par - i
                    halves.append(
                        outlet_one[dy, dx].astype(F32) if 0 <= dy <= 2 else jnp.zeros((8, 128), F32)
                    )
                pieces.append(jnp.concatenate(halves, axis=1))
            at = dx * 32 + slot * 16
            last_one[at : at + 16, :] = jnp.concatenate(pieces, axis=0).astype(BF)

    wide1[...] = jnp.zeros_like(wide1)
    wide2[...] = jnp.zeros_like(wide2)
    wide3[...] = jnp.zeros_like(wide3)
    span = (ROWS1 + 2) * 16
    for dx in range(3):
        for dy in range(3):
            w1 = inlet_two[dy, dx].astype(F32)[:, :16]
            w2 = middle_two[dy, dx].astype(F32)
            for i in range(ROWS1):
                at = dx * span + (i + dy) * 16
                wide1[32 * i : 32 * i + 32, at : at + 16] = w1
            for i in range(ROWS2):
                at = dx * 256 + (i + dy) * 32
                wide2[32 * i : 32 * i + 32, at : at + 32] = w2
    columns = lax.broadcasted_iota(jnp.int32, (ROWS3, 32 * (ROWS3 + 2)), 1)
    offset = columns // 32 - lax.broadcasted_iota(jnp.int32, columns.shape, 0)
    for dx in range(3):
        for o in range(8):
            value = jnp.zeros(columns.shape, F32)
            for dy in range(3):
                line = outlet_two[dy, dx].astype(F32)[o : o + 1]
                line = jnp.concatenate([line] * (ROWS3 + 2), axis=1)
                value = jnp.where(offset == dy, line, value)
            row = (dx * 8 + o) * ROWS3
            wide3[row : row + ROWS3, :] = value
    mid_two[...] = wide2[...].astype(BF)
    last_two[...] = wide3[...].astype(BF)
    lane = lax.broadcasted_iota(jnp.int32, (32, LANES), 1)

    def spread(column):
        return jnp.broadcast_to(column, (32, LANES))

    def split(value):
        high = value.astype(BF).astype(F32)
        return high, (value - high).astype(BF).astype(F32)

    taps = [[spread(inlet_two[dy, dx].astype(F32)[:, 16:17]) for dx in range(3)] for dy in range(3)]
    centre_high, centre_low = split(taps[1][1] + spread(land_bias[...]))
    taps[1][1] = centre_high
    bias_high, bias_low = split(spread(bias_two[...]))
    starts = starts_of(band + 4, ROWS1)
    for b, s in enumerate(starts):
        for i in range(ROWS1):
            value = jnp.where(lane == 32, bias_high, 0.0)
            value = jnp.where(lane == 33, bias_low, value)
            for dx in range(3):
                for dy in range(3):
                    value = jnp.where(lane == dx * 32 + 5 + s + i + dy, taps[dy][dx], value)
            value = jnp.where(lane == 96 + 5 + s + i + 1, centre_low, value)
            first_two[b, 32 * i : 32 * i + 32, 0:LANES] = value.astype(BF)
        first_two[b, :, LANES:] = wide1[...].astype(BF)


def coarse_kernel(
    tile_rows, cols, dests, place, rates, own, west, east, state, first_one, mid_one, last_one,
    bias, scale, coarse_next, noise_one, sends, turned, hidden, active, summed, taps,
):
    px = cols + 2 * EDGE
    rows_before, rows_total, cols_before, cols_total = (place[k] for k in range(4))
    keep, blend = rates[0], rates[1]
    ext = tile_rows + 10
    pairs = (tile_rows + 8) // 2
    windows = [min(14 * k, ext - 16) for k in range(-(-pairs // 7))]
    for k, at in enumerate(windows):
        parts = [
            ref[at : at + 16].reshape(256, cols).astype(F32).T for ref in (west, own, east)
        ]
        whole = jnp.concatenate([parts[0][cols - EDGE :], parts[1], parts[2][:EDGE]], axis=0)
        turned[k, 0] = pltpu.roll(whole, 1, 0).astype(BF)
        turned[k, 1] = whole.astype(BF)
        turned[k, 2] = pltpu.roll(whole, px - 1, 0).astype(BF)

    column = cols_before - EDGE + lax.broadcasted_iota(jnp.int32, (px, 256), 0)
    half = lax.broadcasted_iota(jnp.int32, (px, 256), 1) // 128
    inside = jnp.where((column >= 0) & (column < cols_total), 1.0, 0.0)

    def mask(first_row):
        row = rows_before - 5 + first_row + half
        return jnp.where((row >= 0) & (row < rows_total), inside, 0.0)

    for p in range(pairs):
        k = p // 7
        off = 192 - (2 * p - windows[k]) * 16
        acc = jnp.dot(turned[k, 0], first_one[0, off : off + 256], preferred_element_type=F32)
        for dx in (1, 2):
            acc += jnp.dot(turned[k, dx], first_one[dx, off : off + 256], preferred_element_type=F32)
        low = silu(acc + bias[...]).astype(BF)
        hidden[p] = low
        value = low.astype(F32)
        square = value * value
        scaled = []
        for h in range(2):
            mean = jnp.mean(square[:, h * 128 : (h + 1) * 128], axis=1, keepdims=True)
            scaled.append(value[:, h * 128 : (h + 1) * 128] * lax.rsqrt(mean + 1e-06))
        act = silu(jnp.concatenate(scaled, axis=1) * scale[...]) * mask(1 + 2 * p)
        active[p, :, 0:256] = pltpu.roll(act, 1, 0).astype(BF)
        active[p, :, 256:512] = act.astype(BF)
        active[p, :, 512:768] = pltpu.roll(act, px - 1, 0).astype(BF)

    for p in range(pairs - 1):
        acc = None
        for dx in range(3):
            for q in range(2):
                at = dx * 512 + q * 256
                term = jnp.dot(
                    active[p + q, :, dx * 256 : (dx + 1) * 256], mid_one[at : at + 256],
                    preferred_element_type=F32,
                )
                acc = term if acc is None else acc + term
        rest = jnp.concatenate([hidden[p, :, 128:256], hidden[p + 1, :, 0:128]], axis=1)
        summed[p] = ((acc + rest.astype(F32)) * mask(2 + 2 * p)).astype(BF)

    for p in range(pairs - 1):
        taps[p] = lax.dot_general(
            last_one[...], summed[p], (((1,), (1,)), ((), ())), preferred_element_type=F32
        )
    each = tile_rows // dests
    for p in range(pairs - 2):
        noise = None
        for dx in range(3):
            at = EDGE - 1 + dx
            term = (
                taps[p, dx * 32 : dx * 32 + 16, at : at + cols]
                + taps[p + 1, dx * 32 + 16 : dx * 32 + 32, at : at + cols]
            )
            noise = term if noise is None else noise + term
        made = []
        for i in range(2):
            y = 2 * p - 2 + i
            part = noise[8 * i : 8 * i + 8]
            if 0 <= y < tile_rows:
                rows = pl.ds(y, 8, stride=tile_rows)
                after = keep * state[rows, :] + blend * part
                noise_one[rows, :] = part
                coarse_next[rows, :] = after
            else:
                after = keep * own[y + 5].astype(F32)[0:8] + blend * part
            made.append(after)
        made = jnp.concatenate(made, axis=0).astype(BF)
        for d in range(dests):
            slot = 2 * p - each * d
            if 0 <= slot < each + 4:
                sends[d, slot * 8 : slot * 8 + 16, :] = made


def fine_kernel(
    band, width, chunk, place, rates, coarse, fine, land, above, below, spread, order, first_two, mid_two,
    last_two, fine_next, noise_two, lifted, inputs, ground, hidden, summed,
):
    keep, blend = rates[2], rates[3]
    top = jnp.where(place[4] > 0, 1.0, 0.0)
    bottom = jnp.where(place[4] < place[5] - 1, 1.0, 0.0)
    ext = band + 6
    own = band // 4
    sources = width // (4 * LANES)
    zeros = lambda rows: jnp.zeros((rows, LANES), BF)
    for ref in (inputs, ground, hidden, summed):
        ref[:, 0:LANES] = zeros(ref.shape[0])
        ref[:, LANES + width : 2 * LANES + width] = zeros(ref.shape[0])

    for m in range(sources):
        block = coarse[m].astype(F32)
        rows = [block[8 * j : 8 * j + 8] for j in range(own + 4)]
        rows[1] = top * rows[1] + (1.0 - top) * rows[2]
        rows[own + 2] = bottom * rows[own + 2] + (1.0 - bottom) * rows[own + 1]
        made = []
        for e in range(ext):
            k, phase = divmod(e - 3, 4)
            j = k + 2
            other, near, far = (
                (j - 1, 0.625, 0.375), (j - 1, 0.875, 0.125), (j + 1, 0.875, 0.125), (j + 1, 0.625, 0.375),
            )[phase]
            value = near * rows[j] + far * rows[other]
            if e < 3:
                value = value * top
            if e >= band + 3:
                value = value * bottom
            made.append(value)
        made = jnp.concatenate(made, axis=0)
        lifted[:, (m + 1) * LANES : (m + 2) * LANES] = made
        if m == 0:
            lifted[:, 0:LANES] = jnp.broadcast_to(made[:, 0:1], (ext * 8, LANES))
        if m == sources - 1:
            lifted[:, (m + 2) * LANES : (m + 3) * LANES] = jnp.broadcast_to(
                made[:, LANES - 1 : LANES], (ext * 8, LANES)
            )

    lane = lax.broadcasted_iota(jnp.int32, (ext * 8, LANES), 1)
    pad_rows = ground.shape[0] - band - 16

    def fill(m, _):
        c = pl.multiple_of(m * LANES, LANES)
        main = lifted[:, pl.ds(c + LANES, LANES)]
        side = jnp.where(
            lane == LANES - 1, lifted[:, pl.ds(c, LANES)], lifted[:, pl.ds(c + 2 * LANES, LANES)]
        )
        fields = jnp.dot(
            jnp.concatenate([main, side], axis=1).astype(BF), spread[...], preferred_element_type=F32
        )
        x = pl.multiple_of(m * 4 * LANES, LANES)
        cols = pl.ds(x, 4 * LANES)
        upper = above[:, cols].astype(F32)
        lower = below[:, cols].astype(F32)
        held = jnp.dot(order[...], fine[:, cols].astype(BF), preferred_element_type=F32)
        for e in range(ext):
            if e < 3:
                state = upper[8 * e : 8 * e + 8]
            elif e < band + 3:
                state = held[8 * (e - 3) : 8 * (e - 3) + 8]
            else:
                state = lower[8 * (e - band - 3) : 8 * (e - band - 3) + 8]
            inputs[16 * e : 16 * e + 16, pl.ds(x + LANES, 4 * LANES)] = jnp.concatenate(
                [state, fields[8 * e : 8 * e + 8]], axis=0
            ).astype(BF)
        pieces = [upper[24:32], land[:, cols].astype(F32), lower[24:32]]
        if pad_rows:
            pieces.append(jnp.zeros((pad_rows, 4 * LANES), F32))
        covered = jnp.concatenate(pieces, axis=0)
        ground[:, pl.ds(x + LANES, 4 * LANES)] = covered.astype(BF)
        return 0

    lax.fori_loop(0, sources, fill, 0)

    def three(block):
        return [block[:, LANES - 1 + k : LANES - 1 + k + chunk] for k in range(3)]

    ones_row = lax.broadcasted_iota(jnp.int32, (ground.shape[0], chunk), 0) < 2

    def first(n, _):
        c = pl.multiple_of(n * chunk, chunk)
        span = pl.ds(c, chunk + 2 * LANES)
        west, here, east = three(ground[:, span])
        marked = jnp.where(ones_row, 1.0, here.astype(F32)).astype(BF)
        base = [west, marked, east, here]
        for b, s in enumerate(starts_of(band + 4, ROWS1)):
            block = inputs[16 * s : 16 * (s + ROWS1 + 2), span]
            operand = jnp.concatenate(base + three(block), axis=0)
            value = silu(jnp.dot(first_two[b], operand, preferred_element_type=F32))
            for i in range(ROWS1):
                part = value[32 * i : 32 * i + 32]
                if s + i < 2:
                    part = part * top
                if s + i >= band + 2:
                    part = part * bottom
                at = 32 * (s + i)
                hidden[at : at + 32, pl.ds(c + LANES, chunk)] = part.astype(BF)
        return 0

    lax.fori_loop(0, width // chunk, first, 0)

    def second(n, _):
        c = pl.multiple_of(n * chunk, chunk)
        span = pl.ds(c, chunk + 2 * LANES)
        for s in starts_of(band + 2, ROWS2):
            block = hidden[32 * s : 32 * (s + ROWS2 + 2), span]
            value = jnp.dot(
                mid_two[...], jnp.concatenate(three(block), axis=0), preferred_element_type=F32
            )
            for i in range(ROWS2):
                part = value[32 * i : 32 * i + 32] + block[
                    32 * i + 32 : 32 * i + 64, LANES : LANES + chunk
                ].astype(F32)
                if s + i < 1:
                    part = part * top
                if s + i >= band + 1:
                    part = part * bottom
                at = 32 * (s + i)
                summed[at : at + 32, pl.ds(c + LANES, chunk)] = part.astype(BF)
        return 0

    lax.fori_loop(0, width // chunk, second, 0)

    def third(n, _):
        c = pl.multiple_of(n * chunk, chunk)
        cols = pl.ds(c, chunk)
        for s in range(0, band, ROWS3):
            value = jnp.dot(
                last_two[...],
                summed[32 * s : 32 * (s + ROWS3 + 2), pl.ds(c, chunk + 2 * LANES)],
                preferred_element_type=F32,
            )
            high = 8 * ROWS3
            parts = [
                value[k * high : (k + 1) * high, LANES - 1 + k : LANES - 1 + k + chunk] for k in range(3)
            ]
            noise = parts[0] + parts[1] + parts[2]
            for o in range(8):
                rows = slice(o * band + s, o * band + s + ROWS3)
                part = noise[ROWS3 * o : ROWS3 * o + ROWS3]
                noise_two[rows, cols] = part
                fine_next[rows, cols] = keep * fine[rows, cols] + blend * part
        return 0

    lax.fori_loop(0, width // chunk, third, 0)


def spread_matrix():
    near = np.array([0.625, 0.875, 0.875, 0.625])
    far = np.array([0.375, 0.125, 0.125, 0.375])
    made = np.zeros((2 * LANES, 4 * LANES))
    for n in range(4 * LANES):
        k, phase = divmod(n, 4)
        made[k, n] = near[phase]
        other = k - 1 if phase < 2 else k + 1
        if other < 0:
            made[2 * LANES - 1, n] = far[phase]
        elif other == LANES:
            made[LANES, n] = far[phase]
        else:
            made[other, n] = far[phase]
    return jnp.asarray(made, BF)


def order_matrix(band):
    made = np.zeros((8 * band, 8 * band))
    for y in range(band):
        for o in range(8):
            made[8 * y + o, o * band + y] = 1
    return jnp.asarray(made, BF)


def pick_matrix(band):
    made = np.zeros((64, 9 * band))
    for k, (first, low) in enumerate(((band - 3, band - 8), (0, 0))):
        for y in range(3):
            for o in range(8):
                made[32 * k + 8 * y + o, o * band + first + y] = 1
        for y in range(8):
            made[32 * k + 24 + y, 8 * band + low + y] = 1
    return jnp.asarray(made, BF)


def body(
    step_index, coarse_state, coarse_forcing, fine_state, land_mask, inlet_one, timing_one, scale_one,
    middle_one, outlet_one, inlet_two, timing_two, land_bias, middle_two, outlet_two,
):
    fields, tile_rows, cols = coarse_state.shape
    _, band, width = fine_state.shape
    row_count, col_count = lax.axis_size("row"), lax.axis_size("col")
    row_at, col_at = lax.axis_index("row"), lax.axis_index("col")
    count = row_count * col_count
    state = coarse_state.reshape(fields * tile_rows, cols)
    forcing = coarse_forcing.reshape(fields * tile_rows, cols)
    fine = fine_state.reshape(fields * band, width)

    keep_one, blend_one = plan(step_index[0])
    keep_two, blend_two = plan(step_index[1])
    rates = jnp.stack([keep_one, blend_one, keep_two, blend_two])
    bias_one = embedding(step_index[0], timing_one)
    bias_two = embedding(step_index[1], timing_two)
    place = jnp.stack(
        [
            row_at * tile_rows, jnp.int32(row_count * tile_rows), col_at * cols,
            jnp.int32(col_count * cols), row_at * col_count + col_at, jnp.int32(count),
        ]
    ).astype(jnp.int32)

    comb, to_next, to_prev = pl.pallas_call(
        functools.partial(pack_kernel, tile_rows, 1024),
        out_shape=(
            jax.ShapeDtypeStruct((tile_rows, 2 * fields, cols), BF),
            jax.ShapeDtypeStruct((32, width), BF),
            jax.ShapeDtypeStruct((32, width), BF),
        ),
        in_specs=[VMEM] * 5,
        out_specs=[VMEM] * 3,
        scratch_shapes=[pltpu.VMEM((fields * tile_rows, cols), F32)],
        compiler_params=params(24),
        name="pack",
    )(state, forcing, fine, land_mask, pick_matrix(band))

    north = lax.ppermute(comb[tile_rows - 5 :], "row", shift_pairs(row_count, 1))
    south = lax.ppermute(comb[:5], "row", shift_pairs(row_count, -1))
    tall = jnp.concatenate([north, comb, south], axis=0)
    west = lax.ppermute(tall, "col", shift_pairs(col_count, 1))
    east = lax.ppermute(tall, "col", shift_pairs(col_count, -1))
    above = lax.ppermute(to_next, ("row", "col"), shift_pairs(count, 1))
    below = lax.ppermute(to_prev, ("row", "col"), shift_pairs(count, -1))

    blocks = len(starts_of(band + 4, ROWS1))
    deep = LANES + 3 * 16 * (ROWS1 + 2)
    weights = pl.pallas_call(
        functools.partial(weight_kernel, band),
        out_shape=(
            jax.ShapeDtypeStruct((3, 448, 256), BF),
            jax.ShapeDtypeStruct((1536, 256), BF),
            jax.ShapeDtypeStruct((96, 256), BF),
            jax.ShapeDtypeStruct((blocks, 32 * ROWS1, deep), BF),
            jax.ShapeDtypeStruct((32 * ROWS2, 768), BF),
            jax.ShapeDtypeStruct((24 * ROWS3, 32 * (ROWS3 + 2)), BF),
        ),
        in_specs=[VMEM] * 8,
        out_specs=[VMEM] * 6,
        scratch_shapes=[
            pltpu.VMEM((32 * ROWS1, deep - LANES), F32),
            pltpu.VMEM((32 * ROWS2, 768), F32),
            pltpu.VMEM((24 * ROWS3, 32 * (ROWS3 + 2)), F32),
        ],
        compiler_params=params(24),
        name="weights",
    )(
        inlet_one, middle_one, outlet_one, inlet_two, middle_two, outlet_two, bias_two[:, None],
        land_bias[:, None],
    )
    first_one, mid_one, last_one, first_two, mid_two, last_two = weights

    px = cols + 2 * EDGE
    pairs = (tile_rows + 8) // 2
    each = tile_rows // col_count
    coarse_next, noise_one, sends = pl.pallas_call(
        functools.partial(coarse_kernel, tile_rows, cols, col_count),
        out_shape=(
            jax.ShapeDtypeStruct((fields * tile_rows, cols), F32),
            jax.ShapeDtypeStruct((fields * tile_rows, cols), F32),
            jax.ShapeDtypeStruct((col_count, (each + 4) * fields, cols), BF),
        ),
        in_specs=[SMEM] * 2 + [VMEM] * 9,
        out_specs=[VMEM] * 3,
        scratch_shapes=[
            pltpu.VMEM((-(-pairs // 7), 3, px, 256), BF),
            pltpu.VMEM((pairs, px, 256), BF),
            pltpu.VMEM((pairs, px, 768), BF),
            pltpu.VMEM((pairs - 1, px, 256), BF),
            pltpu.VMEM((pairs - 1, 96, px), F32),
        ],
        compiler_params=params(40),
        name="coarse",
    )(
        place, rates, tall, west, east, state, first_one, mid_one, last_one,
        jnp.tile(bias_one, 2)[None, :], jnp.tile(scale_one, 2)[None, :],
    )

    arrived = lax.all_to_all(sends, "col", split_axis=0, concat_axis=0, tiled=True)

    ground_rows = -(-(band + 16) // 32) * 32
    fine_next, noise_two = pl.pallas_call(
        functools.partial(fine_kernel, band, width, 512),
        out_shape=(
            jax.ShapeDtypeStruct((fields * band, width), F32),
            jax.ShapeDtypeStruct((fields * band, width), F32),
        ),
        in_specs=[SMEM] * 2 + [VMEM] * 10,
        out_specs=[VMEM] * 2,
        scratch_shapes=[
            pltpu.VMEM(((band + 6) * 8, width // 4 + 2 * LANES), F32),
            pltpu.VMEM(((band + 6) * 16, width + 2 * LANES), BF),
            pltpu.VMEM((ground_rows, width + 2 * LANES), BF),
            pltpu.VMEM(((band + 4) * 32, width + 2 * LANES), BF),
            pltpu.VMEM(((band + 2) * 32, width + 2 * LANES), BF),
        ],
        compiler_params=params(56),
        name="fine",
    )(
        place, rates, arrived, fine, land_mask, above, below, spread_matrix(), order_matrix(band),
        first_two, mid_two, last_two,
    )

    return (
        coarse_next.reshape(coarse_state.shape),
        noise_one.reshape(coarse_state.shape),
        fine_next.reshape(fine_state.shape),
        noise_two.reshape(fine_state.shape),
    )


def solution(mesh):
    return jax.shard_map(
        body,
        mesh=mesh,
        in_specs=(
            P(), P(None, "row", "col"), P(None, "row", "col"), P(None, ("row", "col"), None),
            P(("row", "col"), None), P(), P(), P(), P(), P(), P(), P(), P(), P(), P(),
        ),
        out_specs=(
            P(None, "row", "col"), P(None, "row", "col"), P(None, ("row", "col"), None),
            P(None, ("row", "col"), None),
        ),
        check_vma=False,
    )
```

time: 518 us -> 86.7 us (0.17)
  the two profiles are of different devices: /device:TPU:1 before, /device:TPU:0 now
where the time goes in v1:
time: 86.7 us; the launch traced here: 85.8 us
  Pallas kernels  43.9 us (51%)
  starting transfers between devices  22.2 us (26%)
  local copies, waits for them, and re-layouts  9.18 us (11%)
  waiting for transfers between devices  6.76 us (8%)
  between operations  3.12 us (4%)
    pallas_call x1, Pallas kernels, body(): pl.pallas_call(functools.partial(fine_kernel, band, width, 512), out_shap...  35.2 us
    unnamed x54, local copies, waits for them, and re-layouts  8.39 us
    pallas_call x1, Pallas kernels, body(): pl.pallas_call(functools.partial(coarse_kernel, tile_rows, cols, col_coun...  7.32 us
    all_to_all x1, waiting for transfers between devices, body(): lax.all_to_all(sends, 'col', split_axis=0, concat_axis=0, tiled=True)  6.74 us
    ppermute x1, starting transfers between devices, body(): west = lax.ppermute(tall, 'col', shift_pairs(col_count, 1))  5.82 us
    all_to_all x1, starting transfers between devices, body(): lax.all_to_all(sends, 'col', split_axis=0, concat_axis=0, tiled=True)  5.59 us
    ppermute x1, starting transfers between devices, body(): north = lax.ppermute(comb[tile_rows - 5:], 'row', shift_pairs(row_count, 1))  5.47 us
  transfers between devices with their start and end apart: 7, of which 1 were waited for; matrix products, arithmetic and copies ran while one was open for 2% of the time, Pallas kernels for 10%

profile of v1, /device:TPU:0, one launch (start us, length us, event | category | flops | bytes accessed | tf_op | source)
XLA Modules:
  0.0 85.8 jit_solution(495295822712649628)
XLA Ops:
  0.6 0.0 copy-start
  0.7 0.0 copy-start.22
  0.7 0.0 copy-start.23
  0.7 0.0 copy-start.1
  0.7 1.6 %copy-done.1 = f32[8,16,4096]{2,1,0:T(8,128)S(1)} copy-done((f32[8,16,4096]{2,1,0:T(8,128)S(1)}, f32[8,16,4096]{2,1,0:T(8,128)}, u32[]{:S(2)}) %copy-start.1) | copy-done | bytes 2097176
  2.3 0.9 %copy-done.2 = s32[16,4096]{1,0:T(8,128)S(1)} copy-done((s32[16,4096]{1,0:T(8,128)S(1)}, s32[16,4096]{1,0:T(8,128)}, u32[]{:S(2)}) %copy-start.2) | copy-done | bytes 262168
  3.2 0.9 %copy-done.4 = f32[8,32,128]{2,1,0:T(8,128)S(1)} copy-done((f32[8,32,128]{2,1,0:T(8,128)S(1)}, f32[8,32,128]{2,1,0:T(8,128)}, u32[]{:S(2)}) %copy-start.4) | copy-done | bytes 131096
  4.1 0.8 copy-done.10
  5.0 0.8 copy-done.11
  5.7 0.0 copy-start.9
  5.8 0.0 copy-start.12
  5.8 0.0 copy-start.13
  5.8 0.0 copy-start.24
  5.8 0.0 copy-start.5
  5.8 0.5 pack.1
  6.3 1.3 %collective-permute-start.1 = (bf16[5,16,128]{2,1,0:T(8,128)(2,1)S(1)}, bf16[5,16,128]{2,1,0:T(8,128)(2,1)S(1)}, u32[]{:S(2)}, u32[]{:S(2)}) collective-permute-start(bf16[5,16,128]{2,1,0:T(8,128)(2,1)S(1)} %get-tuple-element.32), channel_id=1, source_target_pairs={{8,0},{16,8},{24,16},{9,1},{17,9},{25,17},{10,2},{18,10},{26,18},{... | collective-permute-start | bytes 61448 | tf_op jit(solution)/shard_map/ppermute | solution.py:483
  7.6 5.5 %collective-permute-start = (bf16[5,16,128]{2,1,0:T(8,128)(2,1)S(1)}, bf16[5,16,128]{2,1,0:T(8,128)(2,1)S(1)}, u32[]{:S(2)}, u32[]{:S(2)}) collective-permute-start(bf16[5,16,128]{2,1,0:T(8,128)(2,1)S(1)} %get-tuple-element.33), channel_id=1, source_target_pairs={{0,8},{8,16},{16,24},{1,9},{9,17},{17,25},{2,10},{10,18},{18,26},{... | collective-permute-start | bytes 61448 | tf_op jit(solution)/shard_map/ppermute | solution.py:482
  13.1 1.5 %collective-permute-start.4 = (bf16[32,4096]{1,0:T(8,128)(2,1)S(1)}, bf16[32,4096]{1,0:T(8,128)(2,1)S(1)}, u32[]{:S(2)}, u32[]{:S(2)}) collective-permute-start(bf16[32,4096]{1,0:T(8,128)(2,1)S(1)} %get-tuple-element.25), channel_id=1, source_target_pairs={{0,1},{1,2},{2,3},{3,4},{4,5},{5,6},{6,7},{7,8},{8,9},{9,10},{10,1... | collective-permute-start | bytes 786440 | tf_op jit(solution)/shard_map/ppermute | solution.py:487
  14.5 1.3 %collective-permute-start.5 = (bf16[32,4096]{1,0:T(8,128)(2,1)S(1)}, bf16[32,4096]{1,0:T(8,128)(2,1)S(1)}, u32[]{:S(2)}, u32[]{:S(2)}) collective-permute-start(bf16[32,4096]{1,0:T(8,128)(2,1)S(1)} %get-tuple-element.26), channel_id=1, source_target_pairs={{1,0},{2,1},{3,2},{4,3},{5,4},{6,5},{7,6},{8,7},{9,8},{10,9},{11,1... | collective-permute-start | bytes 786440 | tf_op jit(solution)/shard_map/ppermute | solution.py:488
  15.8 0.0 copy-done.22
  15.8 0.6 fusion.13
  17.8 0.0 copy-done.21
  17.8 0.2 convolution_bitcast_fusion.bias_two
  18.0 0.1 fusion.6
  18.9 0.0 collective-permute-done
  18.9 0.0 collective-permute-done.1
  19.0 1.3 %collective-permute-start.3 = (bf16[42,16,128]{2,1,0:T(8,128)(2,1)S(1)}, bf16[42,16,128]{2,1,0:T(8,128)(2,1)S(1)}, u32[]{:S(2)}, u32[]{:S(2)}) collective-permute-start(bf16[42,16,128]{2,1,0:T(8,128)(2,1)S(1)} %constant_dynamic-update-slice_fusion.own), channel_id=1, source_target_pairs={{1,0},{2,1},{3,2},{4,3},{5,4},{6,5},{7,6},{9,8},{10,9},{11,10},{12... | collective-permute-start | bytes 516104 | tf_op jit(solution)/shard_map/ppermute | solution.py:486
  20.3 5.8 %collective-permute-start.2 = (bf16[42,16,128]{2,1,0:T(8,128)(2,1)S(1)}, bf16[42,16,128]{2,1,0:T(8,128)(2,1)S(1)}, u32[]{:S(2)}, u32[]{:S(2)}) collective-permute-start(bf16[42,16,128]{2,1,0:T(8,128)(2,1)S(1)} %constant_dynamic-update-slice_fusion.own), channel_id=1, source_target_pairs={{0,1},{1,2},{2,3},{3,4},{4,5},{5,6},{6,7},{8,9},{9,10},{10,11},{11... | collective-permute-start | bytes 516104 | tf_op jit(solution)/shard_map/ppermute | solution.py:485
  26.1 0.0 copy-done
  26.1 0.2 convolution_bitcast_fusion.1
  26.3 0.1 pad_maximum_fusion.rates
  26.4 0.0 copy-done.23
  26.4 0.1 copy.25.land_bias
  26.5 0.0 copy-done.19
  26.5 0.2 copy.23.inlet_two
  26.6 0.0 copy-done.20
  26.6 0.2 copy.22.inlet_one
  26.9 0.1 stack.30.place
  27.0 0.0 copy-done.7
  27.0 0.0 copy-done.9
  27.0 0.0 copy-done.12
  27.0 0.0 copy-done.13
  27.0 0.0 copy-start.15
  27.0 0.9 %weights.1 = (bf16[3,448,256]{2,1,0:T(8,128)(2,1)S(1)}, bf16[1536,256]{1,0:T(8,128)(2,1)S(1)}, bf16[96,256]{1,0:T(8,128)(2,1)S(1)}, bf16[4,160,464]{2,1,0:T(8,12...) custom-call(bf16[3,3,128,16]{3,2,1,0:T(8,128)(2,1)S(1)} %copy.22.inlet_one, ...), custom_call_target="tpu_custom_call" | custom-call | tf_op jit(solution)/shard_map/weights/pallas_call | solution.py:492
  27.9 0.0 copy-start.3
  28.0 0.8 copy-done.3
  28.8 0.7 copy-done.6
  29.5 0.7 copy-done.8
  30.2 0.0 collective-permute-done.3.east
  30.2 0.0 collective-permute-done.2.west
  30.2 0.0 copy-done.24
  30.2 0.0 copy-done.5
  30.2 7.3 %coarse.1 = (f32[256,128]{1,0:T(8,128)}, f32[256,128]{1,0:T(8,128)}, bf16[8,64,128]{2,1,0:T(8,128)(2,1)}) custom-call(s32[6]{0:T(128)S(1)} %stack.30.place, f32[4]{0:T(128)S(1)} %pad_maximum_fusion.rates, bf16[42,16,128]{2,1,0:T(8,128)(2,1)S(1)} %constant_dynamic-update-slice_fusion.own, bf16[42,16,128]{2,1,0:T(8,128)(2,1)S(1)} %collective-permute-done.2.west, ...), custom_call_target="tpu_custom_call" | custom-call | tf_op jit(solution)/shard_map/coarse/pallas_call | solution.py:520
  37.6 5.6 %all-to-all-start = ((bf16[8,64,128]{2,1,0:T(8,128)(2,1)}), bf16[8,64,128]{2,1,0:T(8,128)(2,1)S(1)}, u32[]{:S(2)}, u32[]{:S(2)}) async-start(bf16[8,64,128]{2,1,0:T(8,128)(2,1)} %get-tuple-element.24), calls=%async_computation | async-start | bytes 262144 | tf_op jit(solution)/shard_map/all_to_all | solution.py:543
  43.1 0.0 collective-permute-done.4.above
  43.2 0.0 copy-start.17
  43.2 0.0 collective-permute-done.5.below
  43.2 0.0 copy-start.18
  43.2 6.7 %all-to-all-done.coarse = bf16[8,64,128]{2,1,0:T(8,128)(2,1)S(1)} async-done(((bf16[8,64,128]{2,1,0:T(8,128)(2,1)}), bf16[8,64,128]{2,1,0:T(8,128)(2,1)S(1)}, u32[]{:S(2)}, u32[]{:S(2)}) %all-to-all-start) | async-done | bytes 131104 | tf_op jit(solution)/shard_map/all_to_all | solution.py:543
  49.9 0.0 copy-done.14
  49.9 0.0 copy-done.15
  49.9 0.0 copy-done.17
  50.0 0.6 copy-done.16
  50.6 35.2 %fine.1 = (f32[128,4096]{1,0:T(8,128)}, f32[128,4096]{1,0:T(8,128)}) custom-call(s32[6]{0:T(128)} %copy-done.15, f32[4]{0:T(128)} %copy-done.14, bf16[8,64,128]{2,1,0:T(8,128)(2,1)} %copy-done.16, f32[128,4096]{1,0:T(8,128)} %bitcast.33, s32[16,4096]{1,0:T(8,128)} %land.3, bf16[32,4096]{1,0:T(8,128)(2,1)} %copy-done.17, bf16[32,4096]{1,0:T(8,128)(2,1)} %copy-done.18, ...), custom_call_target="tpu_custom_call" | custom-call | tf_op jit(solution)/shard_map/fine/pallas_call | solution.py:546
  (20 shorter events, 0.1 us)
Async XLA Ops:
  0.6 25.5 %copy-start = (bf16[128,128]{1,0:T(8,128)(2,1)S(1)}, bf16[128,128]{1,0:T(8,128)(2,1)}, u32[]{:S(2)}) copy-start(bf16[128,128]{1,0:T(8,128)(2,1)} %param.24) | copy-start | bytes 98308
  0.7 15.2 %copy-start.22 = (s32[2]{0:T(128)S(1)}, s32[2]{0:T(128)}, u32[]{:S(2)}) copy-start(s32[2]{0:T(128)} %param.18) | copy-start | bytes 28
  0.7 25.7 %copy-start.23 = (f32[32]{0:T(128)S(1)}, f32[32]{0:T(128)}, u32[]{:S(2)}) copy-start(f32[32]{0:T(128)} %param.30) | copy-start | bytes 388
  0.7 1.6 %copy-start.1 = (f32[8,16,4096]{2,1,0:T(8,128)S(1)}, f32[8,16,4096]{2,1,0:T(8,128)}, u32[]{:S(2)}) copy-start(f32[8,16,4096]{2,1,0:T(8,128)} %param.21) | copy-start | bytes 6291460
  2.3 0.9 %copy-start.2 = (s32[16,4096]{1,0:T(8,128)S(1)}, s32[16,4096]{1,0:T(8,128)}, u32[]{:S(2)}) copy-start(s32[16,4096]{1,0:T(8,128)} %land.3) | copy-start | bytes 786436
  3.2 0.9 %copy-start.4 = (f32[8,32,128]{2,1,0:T(8,128)S(1)}, f32[8,32,128]{2,1,0:T(8,128)}, u32[]{:S(2)}) copy-start(f32[8,32,128]{2,1,0:T(8,128)} %param.19) | copy-start | bytes 393220
  4.1 0.8 copy-start.10
  5.0 0.8 copy-start.11
  5.7 12.1 %copy-start.21 = (bf16[128,32]{0,1:T(8,128)(2,1)S(1)}, bf16[128,32]{0,1:T(8,128)(2,1)}, u32[]{:S(2)}) copy-start(bf16[128,32]{0,1:T(8,128)(2,1)} %param.29) | copy-start | bytes 24580
  5.7 20.7 %copy-start.19 = (bf16[3,3,32,17]{2,1,3,0:T(4,128)(2,1)S(1)}, bf16[3,3,32,17]{2,1,3,0:T(4,128)(2,1)}, u32[]{:S(2)}) copy-start(bf16[3,3,32,17]{2,1,3,0:T(4,128)(2,1)} %param.28) | copy-start | bytes 29380
  5.7 20.9 %copy-start.20 = (bf16[3,3,128,16]{2,3,1,0:T(8,128)(2,1)S(1)}, bf16[3,3,128,16]{2,3,1,0:T(8,128)(2,1)}, u32[]{:S(2)}) copy-start(bf16[3,3,128,16]{2,3,1,0:T(8,128)(2,1)} %param.23) | copy-start | bytes 110596
  5.7 21.2 %copy-start.7 = (bf16[3,3,128,128]{3,2,1,0:T(8,128)(2,1)S(1)}, bf16[3,3,128,128]{3,2,1,0:T(8,128)(2,1)}, u32[]{:S(2)}) copy-start(bf16[3,3,128,128]{3,2,1,0:T(8,128)(2,1)} %middle_one.1) | copy-start | bytes 884740
  5.7 21.2 %copy-start.9 = (bf16[3,3,32,32]{3,2,1,0:T(8,128)(2,1)S(1)}, bf16[3,3,32,32]{3,2,1,0:T(8,128)(2,1)}, u32[]{:S(2)}) copy-start(bf16[3,3,32,32]{3,2,1,0:T(8,128)(2,1)} %middle_two.1) | copy-start | bytes 55300
  5.8 21.2 %copy-start.12 = (bf16[3,3,8,128]{3,2,1,0:T(8,128)(2,1)S(1)}, bf16[3,3,8,128]{3,2,1,0:T(8,128)(2,1)}, u32[]{:S(2)}) copy-start(bf16[3,3,8,128]{3,2,1,0:T(8,128)(2,1)} %outlet_one.1) | copy-start | bytes 55300
  5.8 21.2 %copy-start.13 = (bf16[3,3,8,32]{3,2,1,0:T(8,128)(2,1)S(1)}, bf16[3,3,8,32]{3,2,1,0:T(8,128)(2,1)}, u32[]{:S(2)}) copy-start(bf16[3,3,8,32]{3,2,1,0:T(8,128)(2,1)} %outlet_two.1) | copy-start | bytes 13828
  5.8 24.4 %copy-start.24 = (f32[128]{0:T(128)S(1)}, f32[128]{0:T(128)}, u32[]{:S(2)}) copy-start(f32[128]{0:T(128)} %param.25) | copy-start | bytes 1540
  5.8 24.4 %copy-start.5 = (f32[8,32,128]{2,1,0:T(8,128)S(1)}, f32[8,32,128]{2,1,0:T(8,128)}, u32[]{:S(2)}) copy-start(f32[8,32,128]{2,1,0:T(8,128)} %param.19) | copy-start | bytes 393220
  6.3 12.7 %collective-permute-start.1 = (bf16[5,16,128]{2,1,0:T(8,128)(2,1)S(1)}, bf16[5,16,128]{2,1,0:T(8,128)(2,1)S(1)}, u32[]{:S(2)}, u32[]{:S(2)}) collective-permute-start(bf16[5,16,128]{2,1,0:T(8,128)(2,1)S(1)} %get-tuple-element.32), channel_id=1, source_target_pairs={{8,0},{16,8},{24,16},{9,1},{17,9},{25,17},{10,2},{18,10},{26,18},{... | collective-permute-start | bytes 61448 | tf_op jit(solution)/shard_map/ppermute | solution.py:483
  7.6 11.3 %collective-permute-start = (bf16[5,16,128]{2,1,0:T(8,128)(2,1)S(1)}, bf16[5,16,128]{2,1,0:T(8,128)(2,1)S(1)}, u32[]{:S(2)}, u32[]{:S(2)}) collective-permute-start(bf16[5,16,128]{2,1,0:T(8,128)(2,1)S(1)} %get-tuple-element.33), channel_id=1, source_target_pairs={{0,8},{8,16},{16,24},{1,9},{9,17},{17,25},{2,10},{10,18},{18,26},{... | collective-permute-start | bytes 61448 | tf_op jit(solution)/shard_map/ppermute | solution.py:482
  13.1 30.1 %collective-permute-start.4 = (bf16[32,4096]{1,0:T(8,128)(2,1)S(1)}, bf16[32,4096]{1,0:T(8,128)(2,1)S(1)}, u32[]{:S(2)}, u32[]{:S(2)}) collective-permute-start(bf16[32,4096]{1,0:T(8,128)(2,1)S(1)} %get-tuple-element.25), channel_id=1, source_target_pairs={{0,1},{1,2},{2,3},{3,4},{4,5},{5,6},{6,7},{7,8},{8,9},{9,10},{10,1... | collective-permute-start | bytes 786440 | tf_op jit(solution)/shard_map/ppermute | solution.py:487
  14.5 28.6 %collective-permute-start.5 = (bf16[32,4096]{1,0:T(8,128)(2,1)S(1)}, bf16[32,4096]{1,0:T(8,128)(2,1)S(1)}, u32[]{:S(2)}, u32[]{:S(2)}) collective-permute-start(bf16[32,4096]{1,0:T(8,128)(2,1)S(1)} %get-tuple-element.26), channel_id=1, source_target_pairs={{1,0},{2,1},{3,2},{4,3},{5,4},{6,5},{7,6},{8,7},{9,8},{10,9},{11,1... | collective-permute-start | bytes 786440 | tf_op jit(solution)/shard_map/ppermute | solution.py:488
  19.0 11.2 %collective-permute-start.3 = (bf16[42,16,128]{2,1,0:T(8,128)(2,1)S(1)}, bf16[42,16,128]{2,1,0:T(8,128)(2,1)S(1)}, u32[]{:S(2)}, u32[]{:S(2)}) collective-permute-start(bf16[42,16,128]{2,1,0:T(8,128)(2,1)S(1)} %constant_dynamic-update-slice_fusion.own), channel_id=1, source_target_pairs={{1,0},{2,1},{3,2},{4,3},{5,4},{6,5},{7,6},{9,8},{10,9},{11,10},{12... | collective-permute-start | bytes 516104 | tf_op jit(solution)/shard_map/ppermute | solution.py:486
  20.3 9.9 %collective-permute-start.2 = (bf16[42,16,128]{2,1,0:T(8,128)(2,1)S(1)}, bf16[42,16,128]{2,1,0:T(8,128)(2,1)S(1)}, u32[]{:S(2)}, u32[]{:S(2)}) collective-permute-start(bf16[42,16,128]{2,1,0:T(8,128)(2,1)S(1)} %constant_dynamic-update-slice_fusion.own), channel_id=1, source_target_pairs={{0,1},{1,2},{2,3},{3,4},{4,5},{5,6},{6,7},{8,9},{9,10},{10,11},{11... | collective-permute-start | bytes 516104 | tf_op jit(solution)/shard_map/ppermute | solution.py:485
  26.4 23.6 %copy-start.14 = (f32[4]{0:T(128)}, f32[4]{0:T(128)S(1)}, u32[]{:S(2)}) copy-start(f32[4]{0:T(128)S(1)} %pad_maximum_fusion.rates) | copy-start | bytes 52
  27.0 23.0 %copy-start.15 = (s32[6]{0:T(128)}, s32[6]{0:T(128)S(1)}, u32[]{:S(2)}) copy-start(s32[6]{0:T(128)S(1)} %stack.30.place) | copy-start | bytes 76
  27.9 0.9 copy-start.3
  28.8 0.7 copy-start.6
  29.5 0.7 copy-start.8
  37.6 12.4 %all-to-all-start = ((bf16[8,64,128]{2,1,0:T(8,128)(2,1)}), bf16[8,64,128]{2,1,0:T(8,128)(2,1)S(1)}, u32[]{:S(2)}, u32[]{:S(2)}) async-start(bf16[8,64,128]{2,1,0:T(8,128)(2,1)} %get-tuple-element.24), calls=%async_computation | async-start | bytes 262144 | tf_op jit(solution)/shard_map/all_to_all | solution.py:543
  43.2 6.8 %copy-start.17 = (bf16[32,4096]{1,0:T(8,128)(2,1)}, bf16[32,4096]{1,0:T(8,128)(2,1)S(1)}, u32[]{:S(2)}) copy-start(bf16[32,4096]{1,0:T(8,128)(2,1)S(1)} %collective-permute-done.4.above) | copy-start | bytes 786436
  43.2 6.8 %copy-start.18 = (bf16[32,4096]{1,0:T(8,128)(2,1)}, bf16[32,4096]{1,0:T(8,128)(2,1)S(1)}, u32[]{:S(2)}) copy-start(bf16[32,4096]{1,0:T(8,128)(2,1)S(1)} %collective-permute-done.5.below) | copy-start | bytes 786436
  49.9 0.7 copy-start.16

commit v2 on v1

v2 whole, which is shorter than its diff:
```python
import functools
import math

import jax
import jax.numpy as jnp
import numpy as np
from jax import lax
from jax.experimental import pallas as pl
from jax.experimental.pallas import tpu as pltpu
from jax.sharding import PartitionSpec as P

BF = jnp.bfloat16
F32 = jnp.float32
VMEM = pl.BlockSpec(memory_space=pltpu.VMEM)
SMEM = pl.BlockSpec(memory_space=pltpu.SMEM)
ANY = pl.BlockSpec(memory_space=pl.ANY)
WHOLE = pl.BlockSpec()
EDGE = 16
ROWS1 = 6
ROWS2 = 6
ROWS3 = 8
LANES = 128


def params(mib):
    return pltpu.CompilerParams(vmem_limit_bytes=mib << 20)


def silu(v):
    return v * (0.5 * jnp.tanh(0.5 * v) + 0.5)


def starts_of(rows, height):
    return [min(s, rows - height) for s in range(0, rows, height)]


def shift_pairs(count, by):
    return [(i, (i + by) % count) for i in range(count)]


def alpha_bar(moment):
    return jnp.cos((moment / 1000.0 + 0.008) / 1.008 * (math.pi / 2.0)) ** 2


def plan(step, shape):
    current_time = jnp.full(shape, step.astype(F32), F32)
    current = alpha_bar(current_time)
    earlier = alpha_bar(current_time - 50.0)
    keeping = jnp.sqrt(earlier / current)
    blending = jnp.sqrt(1.0 - earlier) - jnp.sqrt(earlier) * jnp.sqrt(1.0 - current) / jnp.sqrt(
        current
    )
    return (keeping, blending)


def embed(step, ladder, timing):
    half = ladder.shape[1] // 2
    angles = step.astype(F32) * ladder[...]
    lane = lax.broadcasted_iota(jnp.int32, angles.shape, 1)
    feature = jnp.where(lane < half, jnp.sin(angles), jnp.cos(angles))
    parts = []
    for _ in range(3):
        part = feature.astype(BF)
        feature = feature - part.astype(F32)
        parts.append(part)
    return sum(jnp.dot(part, timing, preferred_element_type=F32) for part in parts)


def ladder_rows(width):
    steps = np.exp(-math.log(10000.0) * np.arange(width // 2) / (width // 2))
    return jnp.asarray(np.tile(np.concatenate([steps, steps]), (8, 1)), F32)


def pack_kernel(tile_rows, state, forcing, comb, top, bottom, near, wide, narrow, sems):
    copies = [
        pltpu.make_async_copy(state, near, sems.at[0]),
        pltpu.make_async_copy(forcing, narrow, sems.at[1]),
    ]
    for copy in copies:
        copy.start()
    for copy in copies:
        copy.wait()
    wide[...] = narrow[...].astype(F32)
    for y in range(tile_rows):
        made = jnp.concatenate(
            [near[pl.ds(y, 8, stride=tile_rows), :], wide[pl.ds(y, 8, stride=tile_rows), :]], axis=0
        ).astype(BF)
        comb[y] = made
        if y < 5:
            top[y] = made
        if y >= tile_rows - 5:
            bottom[y - tile_rows + 5] = made


def sort_kernel(fine, land, turn, order, own, ground, to_next, to_prev):
    for m in range(fine.shape[1] // (4 * LANES)):
        cols = slice(4 * LANES * m, 4 * LANES * (m + 1))
        block = jnp.concatenate([fine[:, cols], land[:, cols].astype(F32)], axis=0).astype(BF)
        block = jnp.dot(block, turn[...], preferred_element_type=F32).astype(BF)
        made = jnp.dot(order[...], block, preferred_element_type=F32).astype(BF)
        at = slice(m * LANES, (m + 1) * LANES)
        for j in range(4):
            part = made[:, j * LANES : (j + 1) * LANES]
            to_next[j, :, at] = part[0:32]
            to_prev[j, :, at] = part[32:64]
            ground[j, :, at] = part[64:80]
            own[j, :, at] = part[80:]


def ground_row(band, e):
    if e < 3:
        return 21 + e
    return e - 3 if e < band + 3 else 24 + e - band - 3


def coarse_weights(
    steps, ladder, timing, inlet_one, middle_one, outlet_one, first_one, mid_one, last_one, bias,
):
    made = embed(steps[0], ladder, timing[...])
    bias[...] = jnp.concatenate([made, made], axis=1)
    first_one[...] = jnp.zeros_like(first_one)
    for dx in range(3):
        for i in range(2):
            for dy in range(3):
                at = 192 + (i + dy) * 16
                first_one[dx, at : at + 16, i * 128 : (i + 1) * 128] = (
                    inlet_one[dy, dx].astype(F32).T.astype(BF)
                )
    mid_one[...] = jnp.zeros_like(mid_one)
    last_one[...] = jnp.zeros_like(last_one)
    for dx in range(3):
        for dy in range(3):
            turned = middle_one[dy, dx].astype(F32).T.astype(BF)
            for i in range(2):
                at = dx * 512 + (i + dy) * 128
                mid_one[at : at + 128, i * 128 : (i + 1) * 128] = turned
    for dx in range(3):
        for slot in range(2):
            pieces = []
            for i in range(2):
                halves = []
                for par in range(2):
                    dy = 2 * slot + par - i
                    halves.append(
                        outlet_one[dy, dx].astype(F32) if 0 <= dy <= 2 else jnp.zeros((8, 128), F32)
                    )
                pieces.append(jnp.concatenate(halves, axis=1))
            at = dx * 32 + slot * 16
            last_one[at : at + 16, :] = jnp.concatenate(pieces, axis=0).astype(BF)


def fine_weights(
    band, steps, ladder, timing, inlet_two, middle_two, outlet_two, land_bias, first_two, mid_two, last_two,
    wide1, wide2, wide3,
):
    bias_two = embed(steps[1], ladder, timing[...])[0:1].T
    wide1[...] = jnp.zeros_like(wide1)
    wide2[...] = jnp.zeros_like(wide2)
    wide3[...] = jnp.zeros_like(wide3)
    span = (ROWS1 + 2) * 8
    for dx in range(3):
        for dy in range(3):
            w1 = inlet_two[dy, dx].astype(F32)[:, :16]
            w2 = middle_two[dy, dx].astype(F32)
            for i in range(ROWS1):
                for half in range(2):
                    at = (3 * half + dx) * span + (i + dy) * 8
                    wide1[32 * i : 32 * i + 32, at : at + 8] = w1[:, 8 * half : 8 * half + 8]
            for i in range(ROWS2):
                at = dx * 256 + (i + dy) * 32
                wide2[32 * i : 32 * i + 32, at : at + 32] = w2
    columns = lax.broadcasted_iota(jnp.int32, (ROWS3, 32 * (ROWS3 + 2)), 1)
    offset = columns // 32 - lax.broadcasted_iota(jnp.int32, columns.shape, 0)
    for dx in range(3):
        for o in range(8):
            value = jnp.zeros(columns.shape, F32)
            for dy in range(3):
                line = outlet_two[dy, dx].astype(F32)[o : o + 1]
                line = jnp.concatenate([line] * (ROWS3 + 2), axis=1)
                value = jnp.where(offset == dy, line, value)
            row = (dx * 8 + o) * ROWS3
            wide3[row : row + ROWS3, :] = value
    mid_two[...] = wide2[...].astype(BF)
    last_two[...] = wide3[...].astype(BF)
    lane = lax.broadcasted_iota(jnp.int32, (32, LANES), 1)

    def spread(column):
        return jnp.broadcast_to(column, (32, LANES))

    def split(value):
        high = value.astype(BF).astype(F32)
        return high, (value - high).astype(BF).astype(F32)

    taps = [[spread(inlet_two[dy, dx].astype(F32)[:, 16:17]) for dx in range(3)] for dy in range(3)]
    centre_high, centre_low = split(taps[1][1] + spread(land_bias[...]))
    taps[1][1] = centre_high
    bias_high, bias_low = split(spread(bias_two))
    starts = starts_of(band + 4, ROWS1)
    for b, s in enumerate(starts):
        for i in range(ROWS1):
            value = jnp.where(lane == 48, bias_high, 0.0)
            value = jnp.where(lane == 49, bias_low, value)
            for dx in range(3):
                for dy in range(3):
                    value = jnp.where(lane == dx * 32 + ground_row(band, s + i + dy), taps[dy][dx], value)
            value = jnp.where(lane == 96 + ground_row(band, s + i + 1), centre_low, value)
            first_two[b, 32 * i : 32 * i + 32, 0:LANES] = value.astype(BF)
        first_two[b, :, LANES:] = wide1[...].astype(BF)


def coarse_kernel(
    tile_rows, cols, dests, place, steps, own, west, east, state, first_one, mid_one, last_one,
    bias, scale, coarse_next, noise_one, sends, turned, hidden, active, summed, taps,
):
    px = cols + 2 * EDGE
    rows_before, rows_total, cols_before, cols_total = (place[k] for k in range(4))
    keep, blend = plan(steps[0], (8, cols))
    ext = tile_rows + 10
    pairs = (tile_rows + 8) // 2
    column = cols_before - EDGE + lax.broadcasted_iota(jnp.int32, (px, 256), 0)
    half = lax.broadcasted_iota(jnp.int32, (px, 256), 1) // 128
    inside = jnp.where((column >= 0) & (column < cols_total), 1.0, 0.0)

    windows = [min(14 * k, ext - 16) for k in range(-(-pairs // 7))]
    for k, at in enumerate(windows):
        parts = [
            ref[at : at + 16].reshape(256, cols).astype(F32).T for ref in (west, own, east)
        ]
        whole = jnp.concatenate([parts[0][cols - EDGE :], parts[1], parts[2][:EDGE]], axis=0)
        row = rows_before - 5 + at + lax.broadcasted_iota(jnp.int32, (px, 256), 1) // 16
        whole = jnp.where((row >= 0) & (row < rows_total) & (inside > 0), whole, 0.0)
        turned[k, 0] = pltpu.roll(whole, 1, 0).astype(BF)
        turned[k, 1] = whole.astype(BF)
        turned[k, 2] = pltpu.roll(whole, px - 1, 0).astype(BF)

    def mask(first_row):
        row = rows_before - 5 + first_row + half
        return jnp.where((row >= 0) & (row < rows_total), inside, 0.0)

    for p in range(pairs):
        k = p // 7
        off = 192 - (2 * p - windows[k]) * 16
        acc = jnp.dot(turned[k, 0], first_one[0, off : off + 256], preferred_element_type=F32)
        for dx in (1, 2):
            acc += jnp.dot(turned[k, dx], first_one[dx, off : off + 256], preferred_element_type=F32)
        low = silu(acc + bias[0:1, :]).astype(BF)
        hidden[p] = low
        value = low.astype(F32)
        square = value * value
        scaled = []
        for h in range(2):
            mean = jnp.mean(square[:, h * 128 : (h + 1) * 128], axis=1, keepdims=True)
            scaled.append(value[:, h * 128 : (h + 1) * 128] * lax.rsqrt(mean + 1e-06))
        act = silu(jnp.concatenate(scaled, axis=1) * scale[...]) * mask(1 + 2 * p)
        active[p, :, 0:256] = pltpu.roll(act, 1, 0).astype(BF)
        active[p, :, 256:512] = act.astype(BF)
        active[p, :, 512:768] = pltpu.roll(act, px - 1, 0).astype(BF)

    for p in range(pairs - 1):
        acc = None
        for dx in range(3):
            for q in range(2):
                at = dx * 512 + q * 256
                term = jnp.dot(
                    active[p + q, :, dx * 256 : (dx + 1) * 256], mid_one[at : at + 256],
                    preferred_element_type=F32,
                )
                acc = term if acc is None else acc + term
        rest = jnp.concatenate([hidden[p, :, 128:256], hidden[p + 1, :, 0:128]], axis=1)
        summed[p] = ((acc + rest.astype(F32)) * mask(2 + 2 * p)).astype(BF)

    for p in range(pairs - 1):
        taps[p] = lax.dot_general(
            last_one[...], summed[p], (((1,), (1,)), ((), ())), preferred_element_type=F32
        )
    each = tile_rows // dests
    for p in range(pairs - 2):
        noise = None
        for dx in range(3):
            at = EDGE - 1 + dx
            term = (
                taps[p, dx * 32 : dx * 32 + 16, at : at + cols]
                + taps[p + 1, dx * 32 + 16 : dx * 32 + 32, at : at + cols]
            )
            noise = term if noise is None else noise + term
        made = []
        for i in range(2):
            y = 2 * p - 2 + i
            part = noise[8 * i : 8 * i + 8]
            if 0 <= y < tile_rows:
                rows = pl.ds(y, 8, stride=tile_rows)
                after = keep * state[rows, :] + blend * part
                noise_one[rows, :] = part
                coarse_next[rows, :] = after
            else:
                after = keep * own[y + 5].astype(F32)[0:8] + blend * part
            made.append(after)
        made = jnp.concatenate(made, axis=0).astype(BF)
        for d in range(dests):
            slot = 2 * p - each * d
            if 0 <= slot < each + 4:
                sends[d, slot * 8 : slot * 8 + 16, :] = made


def fine_kernel(
    band, quarter, place, steps, coarse, fine_far, own, land, above, below, back, first_two, mid_two, last_two,
    fine_far_next, noise_far, rows_of, states, lifted, ground, hidden, summed, fine, fine_next, noise_two, sems,
):
    bring = pltpu.make_async_copy(fine_far, fine, sems.at[0])
    bring.start()
    keep, blend = plan(steps[1], (8, LANES))
    keep, blend = (jnp.concatenate([v] * 4, axis=1) for v in (keep, blend))
    top = jnp.where(place[4] > 0, 1.0, 0.0)
    bottom = jnp.where(place[4] < place[5] - 1, 1.0, 0.0)
    ext = band + 6
    quota = band // 4
    sources = quarter // LANES
    tall = ext * 8

    def edge(value, by):
        lane = lax.broadcasted_iota(jnp.int32, value.shape, 1)
        if by > 0:
            return jnp.where(lane == 0, 0.0, pltpu.roll(value, 1, 1))
        return jnp.where(lane == quarter - 1, 0.0, pltpu.roll(value, quarter - 1, 1))

    def keep_phase(ref, j, rows, value):
        ref[j + 1, rows, :] = value.astype(BF)
        if j == 0:
            ref[5, rows, :] = edge(value, -1).astype(BF)
        if j == 3:
            ref[0, rows, :] = edge(value, 1).astype(BF)

    field = lax.broadcasted_iota(jnp.int32, (16, quarter), 0)
    for j in range(4):
        upper = above[j].astype(F32) * top
        lower = below[j].astype(F32) * bottom
        mine = own[j].astype(F32)
        high = jnp.where(field < 8, upper[16:32], mine[0:16])
        low = jnp.where(field < 8, mine[tall - 48 :], lower[0:16])
        keep_phase(
            states, j, slice(0, tall),
            jnp.concatenate([upper[0:16], high, mine[16 : tall - 48], low, lower[16:32]], axis=0),
        )
        tail = jnp.concatenate([upper[24:32], lower[0:8]], axis=0)
        tail = jnp.where(field < 2, 1.0, tail)
        keep_phase(
            ground, j, slice(0, 32), jnp.concatenate([land[j].astype(F32), tail], axis=0)
        )

    for m in range(sources):
        block = coarse[m].astype(F32)
        rows = [block[8 * j : 8 * j + 8] for j in range(quota + 4)]
        rows[1] = top * rows[1] + (1.0 - top) * rows[2]
        rows[quota + 2] = bottom * rows[quota + 2] + (1.0 - bottom) * rows[quota + 1]
        for e in range(ext):
            k, phase = divmod(e - 3, 4)
            j = k + 2
            other, near, far = (
                (j - 1, 0.625, 0.375), (j - 1, 0.875, 0.125), (j + 1, 0.875, 0.125), (j + 1, 0.625, 0.375),
            )[phase]
            value = near * rows[j] + far * rows[other]
            if e < 3:
                value = value * top
            if e >= band + 3:
                value = value * bottom
            rows_of[8 * e : 8 * e + 8, m * LANES : (m + 1) * LANES] = value
    centre = rows_of[...]
    lane = lax.broadcasted_iota(jnp.int32, centre.shape, 1)
    before = jnp.where(lane == 0, centre, pltpu.roll(centre, 1, 1))
    after = jnp.where(lane == quarter - 1, centre, pltpu.roll(centre, quarter - 1, 1))
    for j, (side, near, far) in enumerate(
        ((before, 0.625, 0.375), (before, 0.875, 0.125), (after, 0.875, 0.125), (after, 0.625, 0.375))
    ):
        keep_phase(lifted, j, slice(0, tall), near * centre + far * side)

    done = 0
    for b, s in enumerate(starts_of(band + 4, ROWS1)):
        for j in range(4):
            window = slice(8 * s, 8 * (s + ROWS1 + 2))
            operand = [ground[j], ground[j + 1], ground[j + 2], ground[j + 1]]
            operand += [states[j + k, window] for k in range(3)]
            operand += [lifted[j + k, window] for k in range(3)]
            value = jnp.dot(
                first_two[b], jnp.concatenate(operand, axis=0), preferred_element_type=F32
            )[32 * (done - s) :]
            value = silu(value)
            parts = []
            for i in range(done, s + ROWS1):
                part = value[32 * (i - done) : 32 * (i - done) + 32]
                if i < 2:
                    part = part * top
                if i >= band + 2:
                    part = part * bottom
                parts.append(part)
            keep_phase(hidden, j, slice(32 * done, 32 * (s + ROWS1)), jnp.concatenate(parts, axis=0))
        done = s + ROWS1

    done = 0
    for s in starts_of(band + 2, ROWS2):
        for j in range(4):
            window = slice(32 * s, 32 * (s + ROWS2 + 2))
            value = jnp.dot(
                mid_two[...], jnp.concatenate([hidden[j + k, window] for k in range(3)], axis=0),
                preferred_element_type=F32,
            )
            for i in range(done, s + ROWS2):
                rows = slice(32 * (i + 1), 32 * (i + 2))
                part = value[32 * (i - s) : 32 * (i - s) + 32] + hidden[j + 1, rows].astype(F32)
                if i < 1:
                    part = part * top
                if i >= band + 1:
                    part = part * bottom
                summed[j, 32 * i : 32 * i + 32] = part.astype(BF)
        done = s + ROWS2

    high = 8 * ROWS3
    bring.wait()
    sends = []
    for s in range(0, band, ROWS3):
        made = [
            jnp.dot(last_two[...], summed[j, 32 * s : 32 * (s + ROWS3 + 2)], preferred_element_type=F32)
            for j in range(4)
        ]
        west = [edge(made[3][0:high], 1)] + [made[j][0:high] for j in range(3)]
        east = [made[j][2 * high :] for j in range(1, 4)] + [edge(made[0][2 * high :], -1)]
        phases = [west[j] + made[j][high : 2 * high] + east[j] for j in range(4)]
        for m in range(sources):
            value = jnp.concatenate([p[:, m * LANES : (m + 1) * LANES] for p in phases], axis=1)
            rough = value.astype(BF)
            fine_part = (value - rough.astype(F32)).astype(BF)
            noise = jnp.dot(
                jnp.concatenate([rough, fine_part], axis=0), back[...], preferred_element_type=F32
            )
            noise = noise[0:high] + noise[high:]
            cols = slice(4 * LANES * m, 4 * LANES * (m + 1))
            for o in range(8):
                rows = slice(s, s + ROWS3)
                part = noise[ROWS3 * o : ROWS3 * o + ROWS3]
                noise_two[o, rows, cols] = part
                fine_next[o, rows, cols] = keep * fine[o, rows, cols] + blend * part
        rows = pl.ds(s, ROWS3)
        for k, (near, far) in enumerate(((noise_two, noise_far), (fine_next, fine_far_next))):
            sem = sems.at[1 + 2 * (s // ROWS3) + k]
            sends.append(pltpu.make_async_copy(near.at[:, rows], far.at[:, rows], sem))
            sends[-1].start()
    for send in sends:
        send.wait()


def turn_matrix():
    made = np.zeros((4 * LANES, 4 * LANES))
    for n in range(4 * LANES):
        made[n, (n % 4) * LANES + n // 4] = 1
    return made


def order_matrix(band):
    made = np.zeros((80 + 8 * (band + 2), 9 * band))
    for o in range(8):
        for y in range(3):
            made[8 * y + o, o * band + band - 3 + y] = 1
            made[32 + 8 * (y + 1) + o, o * band + y] = 1
        for y in range(band):
            made[80 + 8 * (y + 1) + o, o * band + y] = 1
    for y in range(8):
        made[24 + y, 8 * band + band - 8 + y] = 1
        made[32 + y, 8 * band + y] = 1
    for y in range(band):
        made[64 + y, 8 * band + y] = 1
    return made


def body(
    step_index, coarse_state, coarse_forcing, fine_state, land_mask, inlet_one, timing_one, scale_one,
    middle_one, outlet_one, inlet_two, timing_two, land_bias, middle_two, outlet_two,
):
    fields, tile_rows, cols = coarse_state.shape
    _, band, width = fine_state.shape
    row_count, col_count = lax.axis_size("row"), lax.axis_size("col")
    row_at, col_at = lax.axis_index("row"), lax.axis_index("col")
    count = row_count * col_count
    state = coarse_state.reshape(fields * tile_rows, cols)
    forcing = coarse_forcing.reshape(fields * tile_rows, cols)
    fine = fine_state.reshape(fields * band, width)
    quarter = width // 4
    place = jnp.stack(
        [
            row_at * tile_rows, jnp.int32(row_count * tile_rows), col_at * cols,
            jnp.int32(col_count * cols), row_at * col_count + col_at, jnp.int32(count),
        ]
    ).astype(jnp.int32)
    ladder = ladder_rows(timing_one.shape[0])

    comb, first_rows, last_rows = pl.pallas_call(
        functools.partial(pack_kernel, tile_rows),
        out_shape=(
            jax.ShapeDtypeStruct((tile_rows, 2 * fields, cols), BF),
            jax.ShapeDtypeStruct((5, 2 * fields, cols), BF),
            jax.ShapeDtypeStruct((5, 2 * fields, cols), BF),
        ),
        in_specs=[ANY] * 2,
        out_specs=[VMEM] * 3,
        scratch_shapes=[
            pltpu.VMEM((fields * tile_rows, cols), F32),
            pltpu.VMEM((fields * tile_rows, cols), F32),
            pltpu.VMEM((fields * tile_rows, cols), BF),
            pltpu.SemaphoreType.DMA((2,)),
        ],
        compiler_params=params(8),
        name="pack",
    )(state, forcing)
    north = lax.ppermute(last_rows, "row", shift_pairs(row_count, 1))
    south = lax.ppermute(first_rows, "row", shift_pairs(row_count, -1))

    turn = turn_matrix()
    split = 1024
    part = split // 4
    shapes = (8 * (band + 2), 16, 32, 32)
    own, ground, to_next, to_prev = pl.pallas_call(
        sort_kernel,
        grid=(width // split,),
        out_shape=[jax.ShapeDtypeStruct((4, rows, quarter), BF) for rows in shapes],
        in_specs=[
            pl.BlockSpec((fields * band, split), lambda n: (0, n)),
            pl.BlockSpec((band, split), lambda n: (0, n)),
            pl.BlockSpec((4 * LANES, 4 * LANES), lambda n: (0, 0)),
            pl.BlockSpec((80 + 8 * (band + 2), 9 * band), lambda n: (0, 0)),
        ],
        out_specs=[pl.BlockSpec((4, rows, part), lambda n: (0, 0, n)) for rows in shapes],
        compiler_params=params(24),
        name="sort",
    )(fine, land_mask, jnp.asarray(turn, BF), jnp.asarray(order_matrix(band), BF))
    above = lax.ppermute(to_next, ("row", "col"), shift_pairs(count, 1))
    below = lax.ppermute(to_prev, ("row", "col"), shift_pairs(count, -1))

    tall = jnp.concatenate([north, comb, south], axis=0)
    west = lax.ppermute(tall, "col", shift_pairs(col_count, 1))
    east = lax.ppermute(tall, "col", shift_pairs(col_count, -1))

    first_one, mid_one, last_one, bias = pl.pallas_call(
        coarse_weights,
        out_shape=(
            jax.ShapeDtypeStruct((3, 448, 256), BF),
            jax.ShapeDtypeStruct((1536, 256), BF),
            jax.ShapeDtypeStruct((96, 256), BF),
            jax.ShapeDtypeStruct((8, 256), F32),
        ),
        in_specs=[SMEM] + [WHOLE] * 5,
        out_specs=[VMEM] * 4,
        compiler_params=params(8),
        name="coarse_weights",
    )(step_index, ladder, timing_one, inlet_one, middle_one, outlet_one)
    blocks = len(starts_of(band + 4, ROWS1))
    deep = LANES + 6 * 8 * (ROWS1 + 2)
    first_two, mid_two, last_two = pl.pallas_call(
        functools.partial(fine_weights, band),
        out_shape=(
            jax.ShapeDtypeStruct((blocks, 32 * ROWS1, deep), BF),
            jax.ShapeDtypeStruct((32 * ROWS2, 768), BF),
            jax.ShapeDtypeStruct((24 * ROWS3, 32 * (ROWS3 + 2)), BF),
        ),
        in_specs=[SMEM] + [WHOLE] * 6,
        out_specs=[VMEM] * 3,
        scratch_shapes=[
            pltpu.VMEM((32 * ROWS1, deep - LANES), F32),
            pltpu.VMEM((32 * ROWS2, 768), F32),
            pltpu.VMEM((24 * ROWS3, 32 * (ROWS3 + 2)), F32),
        ],
        compiler_params=params(8),
        name="fine_weights",
    )(step_index, ladder, timing_two, inlet_two, middle_two, outlet_two, land_bias[:, None])

    px = cols + 2 * EDGE
    pairs = (tile_rows + 8) // 2
    each = tile_rows // col_count
    coarse_next, noise_one, sends = pl.pallas_call(
        functools.partial(coarse_kernel, tile_rows, cols, col_count),
        out_shape=(
            jax.ShapeDtypeStruct((fields * tile_rows, cols), F32),
            jax.ShapeDtypeStruct((fields * tile_rows, cols), F32),
            jax.ShapeDtypeStruct((col_count, (each + 4) * fields, cols), BF),
        ),
        in_specs=[SMEM] * 2 + [VMEM] * 9,
        out_specs=[VMEM] * 3,
        scratch_shapes=[
            pltpu.VMEM((-(-pairs // 7), 3, px, 256), BF),
            pltpu.VMEM((pairs, px, 256), BF),
            pltpu.VMEM((pairs, px, 768), BF),
            pltpu.VMEM((pairs - 1, px, 256), BF),
            pltpu.VMEM((pairs - 1, 96, px), F32),
        ],
        compiler_params=params(40),
        name="coarse",
    )(
        place, step_index, tall, west, east, state, first_one, mid_one, last_one, bias,
        jnp.tile(scale_one, 2)[None, :],
    )

    arrived = lax.all_to_all(sends, "col", split_axis=0, concat_axis=0, tiled=True)

    fine_next, noise_two = pl.pallas_call(
        functools.partial(fine_kernel, band, quarter),
        out_shape=(
            jax.ShapeDtypeStruct((fields, band, width), F32),
            jax.ShapeDtypeStruct((fields, band, width), F32),
        ),
        in_specs=[SMEM] * 2 + [VMEM, ANY] + [VMEM] * 8,
        out_specs=[ANY] * 2,
        scratch_shapes=[
            pltpu.VMEM(((band + 6) * 8, quarter), F32),
            pltpu.VMEM((6, (band + 6) * 8, quarter), BF),
            pltpu.VMEM((6, (band + 6) * 8, quarter), BF),
            pltpu.VMEM((6, 32, quarter), BF),
            pltpu.VMEM((6, (band + 4) * 32, quarter), BF),
            pltpu.VMEM((4, (band + 2) * 32, quarter), BF),
            pltpu.VMEM((fields, band, width), F32),
            pltpu.VMEM((fields, band, width), F32),
            pltpu.VMEM((fields, band, width), F32),
            pltpu.SemaphoreType.DMA((1 + 2 * (band // ROWS3),)),
        ],
        compiler_params=params(56),
        name="fine",
    )(
        place, step_index, arrived, fine_state, own, ground, above, below, jnp.asarray(turn.T, BF),
        first_two, mid_two, last_two,
    )

    return (
        coarse_next.reshape(coarse_state.shape),
        noise_one.reshape(coarse_state.shape),
        fine_next,
        noise_two,
    )


def solution(mesh):
    return jax.shard_map(
        body,
        mesh=mesh,
        in_specs=(
            P(), P(None, "row", "col"), P(None, "row", "col"), P(None, ("row", "col"), None),
            P(("row", "col"), None), P(), P(), P(), P(), P(), P(), P(), P(), P(), P(),
        ),
        out_specs=(
            P(None, "row", "col"), P(None, "row", "col"), P(None, ("row", "col"), None),
            P(None, ("row", "col"), None),
        ),
        check_vma=False,
    )
```

time: 86.7 us -> 61.4 us (0.71)
  Pallas kernels: 43.9 us -> 28.4 us
  starting transfers between devices: 22.2 us -> 14.8 us
  local copies, waits for them, and re-layouts: 9.18 us -> 11.5 us
  between operations: 3.12 us -> 1.04 us
  waiting for transfers between devices: 6.76 us -> 5.21 us
    pallas_call x3 -> x5, Pallas kernels: 36.6 us -> 20.7 us  [the longest x1 14.8 us: body(): pl.pallas_call(functools.partial(fine_kernel, band, quarter), out_shape=(...]
    ppermute x1, starting transfers between devices: 5.82 us -> 0.01 us  [body(): west = lax.ppermute(tall, 'col', shift_pairs(col_count, 1))]
    all_to_all x1, waiting for transfers between devices: 6.74 us -> 2.46 us  [body(): lax.all_to_all(sends, 'col', split_axis=0, concat_axis=0, tiled=True)]
    ppermute x1, starting transfers between devices: 1.29 us -> 5.44 us  [body(): below = lax.ppermute(to_prev, ('row', 'col'), shift_pairs(count, -1))]
    unnamed x54 -> x61, local copies, waits for them, and re-layouts: 8.39 us -> 11.4 us
    ppermute x2, starting transfers between devices: 6.76 us -> 4.01 us  [the longest x1 2.99 us: body(): north = lax.ppermute(last_rows, 'row', shift_pairs(row_count, 1))]
    ppermute x2, waiting for transfers between devices: 0.01 us -> 2.73 us  [the longest x1 1.7 us: body(): north = lax.ppermute(last_rows, 'row', shift_pairs(row_count, 1))]
    all_to_all x1, starting transfers between devices: 5.59 us -> 3.55 us  [body(): lax.all_to_all(sends, 'col', split_axis=0, concat_axis=0, tiled=True)]
  transfers between devices with their start and end apart: 7 -> 7, of which waited for: 1 -> 3; matrix products, arithmetic and copies ran while one was open for 2% -> 1% of each run, Pallas kernels for 10% -> 22%
where the time goes in v2:
time: 61.4 us; the launch traced here: 61 us
  Pallas kernels  28.4 us (46%)
  starting transfers between devices  14.8 us (24%)
  local copies, waits for them, and re-layouts  11.5 us (19%)
  waiting for transfers between devices  5.21 us (8%)
  between operations  1.04 us (2%)
    pallas_call x1, Pallas kernels, body(): pl.pallas_call(functools.partial(fine_kernel, band, quarter), out_shape=(...  14.8 us
    unnamed x61, local copies, waits for them, and re-layouts  11.4 us
    pallas_call x1, Pallas kernels, body(): pl.pallas_call(functools.partial(coarse_kernel, tile_rows, cols, col_coun...  7.66 us
    ppermute x1, starting transfers between devices, body(): below = lax.ppermute(to_prev, ('row', 'col'), shift_pairs(count, -1))  5.44 us
    all_to_all x1, starting transfers between devices, body(): lax.all_to_all(sends, 'col', split_axis=0, concat_axis=0, tiled=True)  3.55 us
    pallas_call x1, Pallas kernels, body(): pl.pallas_call(sort_kernel, grid=(width // split,), out_shape=[jax.ShapeD...  3.2 us
    ppermute x1, starting transfers between devices, body(): north = lax.ppermute(last_rows, 'row', shift_pairs(row_count, 1))  2.99 us
    all_to_all x1, waiting for transfers between devices, body(): lax.all_to_all(sends, 'col', split_axis=0, concat_axis=0, tiled=True)  2.46 us
  transfers between devices with their start and end apart: 7, of which 3 were waited for; matrix products, arithmetic and copies ran while one was open for 1% of the time, Pallas kernels for 22%

profile of v2, /device:TPU:0, one launch (start us, length us, event | category | flops | bytes accessed | tf_op | source)
XLA Modules:
  0.0 61.0 jit_solution(10196281607654126360)
XLA Ops:
  0.6 0.0 copy-start.17
  0.6 0.0 copy-start.18
  0.7 0.0 copy-start.3
  0.7 0.9 %copy-done.3 = f32[8,32,128]{2,1,0:T(8,128)S(1)} copy-done((f32[8,32,128]{2,1,0:T(8,128)S(1)}, f32[8,32,128]{2,1,0:T(8,128)}, u32[]{:S(2)}) %copy-start.3) | copy-done | bytes 131096
  1.6 0.0 copy-start.13
  1.6 0.8 %copy-done.13 = bf16[8,32,128]{2,1,0:T(8,128)(2,1)S(1)} copy-done((bf16[8,32,128]{2,1,0:T(8,128)(2,1)S(1)}, bf16[8,32,128]{2,1,0:T(8,128)(2,1)}, u32[]{:S(2)}) %copy-start.13) | copy-done | bytes 65560
  2.4 0.0 copy-start.24
  2.4 0.0 copy-start.7
  2.4 0.4 pack.1
  2.9 3.0 %collective-permute-start = (bf16[5,16,128]{2,1,0:T(8,128)(2,1)S(1)}, bf16[5,16,128]{2,1,0:T(8,128)(2,1)S(1)}, u32[]{:S(2)}, u32[]{:S(2)}) collective-permute-start(bf16[5,16,128]{2,1,0:T(8,128)(2,1)S(1)} %get-tuple-element.23), channel_id=1, source_target_pairs={{0,8},{8,16},{16,24},{24,0},{1,9},{9,17},{17,25},{25,1},{2,10},{10... | collective-permute-start | bytes 61448 | tf_op jit(solution)/shard_map/ppermute | solution.py:512
  5.9 1.0 %collective-permute-start.1 = (bf16[5,16,128]{2,1,0:T(8,128)(2,1)S(1)}, bf16[5,16,128]{2,1,0:T(8,128)(2,1)S(1)}, u32[]{:S(2)}, u32[]{:S(2)}) collective-permute-start(bf16[5,16,128]{2,1,0:T(8,128)(2,1)S(1)} %get-tuple-element.25), channel_id=1, source_target_pairs={{0,24},{8,0},{16,8},{24,16},{1,25},{9,1},{17,9},{25,17},{2,26},{10... | collective-permute-start | bytes 61448 | tf_op jit(solution)/shard_map/ppermute | solution.py:513
  6.9 1.7 %collective-permute-done = bf16[5,16,128]{2,1,0:T(8,128)(2,1)S(1)} collective-permute-done((bf16[5,16,128]{2,1,0:T(8,128)(2,1)S(1)}, bf16[5,16,128]{2,1,0:T(8,128)(2,1)S(1)}, u32[]{:S(2)}, u32[]{:S(2)}) %collective-permute-start) | collective-permute-done | bytes 20512 | tf_op jit(solution)/shard_map/ppermute | solution.py:512
  8.6 1.0 %collective-permute-done.1 = bf16[5,16,128]{2,1,0:T(8,128)(2,1)S(1)} collective-permute-done((bf16[5,16,128]{2,1,0:T(8,128)(2,1)S(1)}, bf16[5,16,128]{2,1,0:T(8,128)(2,1)S(1)}, u32[]{:S(2)}, u32[]{:S(2)}) %collective-permute-start.1) | collective-permute-done | bytes 20512 | tf_op jit(solution)/shard_map/ppermute | solution.py:513
  9.6 1.6 %collective-permute-start.3 = (bf16[42,16,128]{2,1,0:T(8,128)(2,1)S(1)}, bf16[42,16,128]{2,1,0:T(8,128)(2,1)S(1)}, u32[]{:S(2)}, u32[]{:S(2)}) collective-permute-start(bf16[42,16,128]{2,1,0:T(8,128)(2,1)S(1)} %constant_dynamic-update-slice_fusion.own), channel_id=1, source_target_pairs={{0,7},{1,0},{2,1},{3,2},{4,3},{5,4},{6,5},{7,6},{8,15},{9,8},{10,9... | collective-permute-start | bytes 516104 | tf_op jit(solution)/shard_map/ppermute | solution.py:538
  11.3 0.0 collective-permute-start.2
  11.3 1.6 %copy-done = f32[8,16,4096]{2,1,0:T(8,128)S(1)} copy-done((f32[8,16,4096]{2,1,0:T(8,128)S(1)}, f32[8,16,4096]{2,1,0:T(8,128)}, u32[]{:S(2)}) %copy-start) | copy-done | bytes 2097176
  12.9 1.0 %copy-done.5 = bf16[512,512]{1,0:T(8,128)(2,1)S(1)} copy-done((bf16[512,512]{1,0:T(8,128)(2,1)S(1)}, bf16[512,512]{1,0:T(8,128)(2,1)}, u32[]{:S(2)}) %copy-start.5) | copy-done | bytes 524312
  13.9 0.9 %copy-done.8 = s32[16,4096]{1,0:T(8,128)S(1)} copy-done((s32[16,4096]{1,0:T(8,128)S(1)}, s32[16,4096]{1,0:T(8,128)}, u32[]{:S(2)}) %copy-start.8) | copy-done | bytes 262168
  14.8 0.9 %copy-done.11 = bf16[224,144]{1,0:T(8,128)(2,1)S(1)} copy-done((bf16[224,144]{1,0:T(8,128)(2,1)S(1)}, bf16[224,144]{1,0:T(8,128)(2,1)}, u32[]{:S(2)}) %copy-start.11) | copy-done | bytes 64536
  15.7 3.2 %sort.1 = (bf16[4,144,1024]{2,1,0:T(8,128)(2,1)S(1)}, bf16[4,16,1024]{2,1,0:T(8,128)(2,1)S(1)}, bf16[4,32,1024]{2,1,0:T(8,128)(2,1)S(1)}, bf16[4,32,1024]{2,1,0:T(8,128)(2,1)S(1)}) custom-call(f32[128,4096]{1,0:T(8,128)S(1)} %bitcast.10, s32[16,4096]{1,0:T(8,128)S(1)} %copy-done.8, bf16[512,512]{1,0:T(8,128)(2,1)S(1)} %copy-done.5, ...), custom_call_target="tpu_custom_call" | custom-call | tf_op jit(solution)/shard_map/sort/pallas_call | solution.py:519
  19.0 0.0 copy-start.1
  19.0 1.0 %copy-done.1 = bf16[4,144,1024]{2,1,0:T(8,128)(2,1)} copy-done((bf16[4,144,1024]{2,1,0:T(8,128)(2,1)}, bf16[4,144,1024]{2,1,0:T(8,128)(2,1)S(1)}, u32[]{:S(2)}) %copy-start.1) | copy-done | bytes 1179672
  20.0 0.7 %copy-done.10 = bf16[4,16,1024]{2,1,0:T(8,128)(2,1)} copy-done((bf16[4,16,1024]{2,1,0:T(8,128)(2,1)}, bf16[4,16,1024]{2,1,0:T(8,128)(2,1)S(1)}, u32[]{:S(2)}) %copy-start.10) | copy-done | bytes 131096
  20.7 0.0 copy-start.16
  20.7 0.2 collective-permute-start.4
  20.9 5.4 %collective-permute-start.5 = (bf16[4,32,1024]{2,1,0:T(8,128)(2,1)S(1)}, bf16[4,32,1024]{2,1,0:T(8,128)(2,1)S(1)}, u32[]{:S(2)}, u32[]{:S(2)}) collective-permute-start(bf16[4,32,1024]{2,1,0:T(8,128)(2,1)S(1)} %get-tuple-element.36), channel_id=1, source_target_pairs={{0,31},{1,0},{2,1},{3,2},{4,3},{5,4},{6,5},{7,6},{8,7},{9,8},{10,9... | collective-permute-start | bytes 786440 | tf_op jit(solution)/shard_map/ppermute | solution.py:534
  26.3 0.0 copy-done.24
  26.3 0.2 copy.23.inlet_one
  26.5 0.1 stack.15.place
  26.6 0.0 copy-done.17
  26.6 0.0 copy-done.18
  26.6 0.0 copy-done.7
  26.6 0.0 copy-done.14
  26.6 0.0 copy-done.15
  26.7 0.0 copy-start.19
  26.7 0.9 %coarse_weights.1 = (bf16[3,448,256]{2,1,0:T(8,128)(2,1)S(1)}, bf16[1536,256]{1,0:T(8,128)(2,1)S(1)}, bf16[96,256]{1,0:T(8,128)(2,1)S(1)}, f32[8,256]{1,0:T(8,128)S(1)}) custom-call(s32[2]{0:T(128)S(1)} %copy-done.18, f32[8,128]{1,0:T(8,128)S(1)} %copy-done.17, bf16[128,128]{1,0:T(8,128)(2,1)S(1)} %copy-done.14, bf16[3,3,128,16]{3,2,1,0:T(8,128)(2,1)S(1)} %copy.23.inlet_one, ...), custom_call_target="tpu_custom_call" | custom-call | tf_op jit(solution)/shard_map/coarse_weights/pallas_call | solution.py:540
  27.6 0.0 collective-permute-done.3.east
  27.6 0.0 collective-permute-done.2.west
  27.6 0.0 copy-done.27
  27.7 0.0 copy-done.4
  27.7 7.7 %coarse.1 = (f32[256,128]{1,0:T(8,128)}, f32[256,128]{1,0:T(8,128)}, bf16[8,64,128]{2,1,0:T(8,128)(2,1)}) custom-call(s32[6]{0:T(128)S(1)} %stack.15.place, s32[2]{0:T(128)S(1)} %copy-done.18, bf16[42,16,128]{2,1,0:T(8,128)(2,1)S(1)} %constant_dynamic-update-slice_fusion.own, bf16[42,16,128]{2,1,0:T(8,128)(2,1)S(1)} %collective-permute-done.2.west, ...), custom_call_target="tpu_custom_call" | custom-call | tf_op jit(solution)/shard_map/coarse/pallas_call | solution.py:576
  35.3 3.6 %all-to-all-start = ((bf16[8,64,128]{2,1,0:T(8,128)(2,1)}), bf16[8,64,128]{2,1,0:T(8,128)(2,1)S(1)}, u32[]{:S(2)}, u32[]{:S(2)}) async-start(bf16[8,64,128]{2,1,0:T(8,128)(2,1)} %get-tuple-element.32), calls=%async_computation | async-start | bytes 262144 | tf_op jit(solution)/shard_map/all_to_all | solution.py:599
  38.9 0.0 copy-done.26
  38.9 0.1 copy.26.land_bias
  39.0 0.0 copy-done.25
  39.0 0.1 copy.24.timing
  39.1 0.0 copy-done.23
  39.1 0.1 copy.25.inlet_two
  39.3 0.0 copy-done.12
  39.3 0.0 copy-done.16
  39.3 1.4 %fine_weights.1 = (bf16[4,192,512]{2,1,0:T(8,128)(2,1)S(1)}, bf16[192,768]{1,0:T(8,128)(2,1)S(1)}, bf16[192,320]{1,0:T(8,128)(2,1)S(1)}) custom-call(s32[2]{0:T(128)S(1)} %copy-done.18, f32[8,128]{1,0:T(8,128)S(1)} %copy-done.17, bf16[128,32]{1,0:T(8,128)(2,1)S(1)} %copy.24.timing, bf16[3,3,32,17]{3,2,1,0:T(8,128)(2,1)S(1)} %copy.25.inlet_two, ...), custom_call_target="tpu_custom_call" | custom-call | tf_op jit(solution)/shard_map/fine_weights/pallas_call | solution.py:555
  40.7 0.0 copy-start.2
  40.7 0.9 %copy-done.2 = bf16[4,192,512]{2,1,0:T(8,128)(2,1)} copy-done((bf16[4,192,512]{2,1,0:T(8,128)(2,1)}, bf16[4,192,512]{2,1,0:T(8,128)(2,1)S(1)}, u32[]{:S(2)}) %copy-start.2) | copy-done | bytes 786456
  41.6 0.7 %copy-done.6 = bf16[192,768]{1,0:T(8,128)(2,1)} copy-done((bf16[192,768]{1,0:T(8,128)(2,1)}, bf16[192,768]{1,0:T(8,128)(2,1)S(1)}, u32[]{:S(2)}) %copy-start.6) | copy-done | bytes 294936
  42.3 0.6 %copy-done.9 = bf16[192,320]{1,0:T(8,128)(2,1)} copy-done((bf16[192,320]{1,0:T(8,128)(2,1)}, bf16[192,320]{1,0:T(8,128)(2,1)S(1)}, u32[]{:S(2)}) %copy-start.9) | copy-done | bytes 122904
  42.9 0.0 collective-permute-done.4.above
  42.9 0.0 collective-permute-done.5.below
  42.9 0.0 copy-start.22
  42.9 2.5 %all-to-all-done.coarse = bf16[8,64,128]{2,1,0:T(8,128)(2,1)S(1)} async-done(((bf16[8,64,128]{2,1,0:T(8,128)(2,1)}), bf16[8,64,128]{2,1,0:T(8,128)(2,1)S(1)}, u32[]{:S(2)}, u32[]{:S(2)}) %all-to-all-start) | async-done | bytes 131104 | tf_op jit(solution)/shard_map/all_to_all | solution.py:599
  45.4 0.0 copy-done.19
  45.4 0.0 copy-done.21
  45.4 0.0 copy-done.22
  45.4 0.6 %copy-done.20 = bf16[8,64,128]{2,1,0:T(8,128)(2,1)} copy-done((bf16[8,64,128]{2,1,0:T(8,128)(2,1)}, bf16[8,64,128]{2,1,0:T(8,128)(2,1)S(1)}, u32[]{:S(2)}) %copy-start.20) | copy-done | bytes 131096
  46.1 14.8 %fine.1 = (f32[8,16,4096]{2,1,0:T(8,128)}, f32[8,16,4096]{2,1,0:T(8,128)}) custom-call(s32[6]{0:T(128)} %copy-done.19, s32[2]{0:T(128)} %steps.7, bf16[8,64,128]{2,1,0:T(8,128)(2,1)} %copy-done.20, f32[8,16,4096]{2,1,0:T(8,128)} %fine_far.1, bf16[4,144,1024]{2,1,0:T(8,128)(2,1)} %copy-done.1, bf16[4,16,1024]{2,1,0:T(8,128)(2,1)} %copy-done.10, ...), custom_call_target="tpu_custom_call" | custom-call | tf_op jit(solution)/shard_map/fine/pallas_call | solution.py:601
  (21 shorter events, 0.1 us)
Async XLA Ops:
  0.6 26.0 %copy-start.17 = (f32[8,128]{1,0:T(8,128)S(1)}, f32[8,128]{1,0:T(8,128)}, u32[]{:S(2)}) copy-start(f32[8,128]{1,0:T(8,128)} %constant.28.clone.ladder) | copy-start | bytes 12292
  0.6 26.0 %copy-start.18 = (s32[2]{0:T(128)S(1)}, s32[2]{0:T(128)}, u32[]{:S(2)}) copy-start(s32[2]{0:T(128)} %steps.7) | copy-start | bytes 28
  0.7 0.9 %copy-start.3 = (f32[8,32,128]{2,1,0:T(8,128)S(1)}, f32[8,32,128]{2,1,0:T(8,128)}, u32[]{:S(2)}) copy-start(f32[8,32,128]{2,1,0:T(8,128)} %param.20) | copy-start | bytes 393220
  1.6 0.8 %copy-start.13 = (bf16[8,32,128]{2,1,0:T(8,128)(2,1)S(1)}, bf16[8,32,128]{2,1,0:T(8,128)(2,1)}, u32[]{:S(2)}) copy-start(bf16[8,32,128]{2,1,0:T(8,128)(2,1)} %param.21) | copy-start | bytes 196612
  2.4 23.9 %copy-start.24 = (bf16[3,3,128,16]{2,3,1,0:T(8,128)(2,1)S(1)}, bf16[3,3,128,16]{2,3,1,0:T(8,128)(2,1)}, u32[]{:S(2)}) copy-start(bf16[3,3,128,16]{2,3,1,0:T(8,128)(2,1)} %param.24) | copy-start | bytes 110596
  2.4 24.2 %copy-start.7 = (bf16[3,3,128,128]{3,2,1,0:T(8,128)(2,1)S(1)}, bf16[3,3,128,128]{3,2,1,0:T(8,128)(2,1)}, u32[]{:S(2)}) copy-start(bf16[3,3,128,128]{3,2,1,0:T(8,128)(2,1)} %middle_one.1) | copy-start | bytes 884740
  2.4 24.2 %copy-start.14 = (bf16[128,128]{1,0:T(8,128)(2,1)S(1)}, bf16[128,128]{1,0:T(8,128)(2,1)}, u32[]{:S(2)}) copy-start(bf16[128,128]{1,0:T(8,128)(2,1)} %timing.2) | copy-start | bytes 98308
  2.4 24.2 %copy-start.15 = (bf16[3,3,8,128]{3,2,1,0:T(8,128)(2,1)S(1)}, bf16[3,3,8,128]{3,2,1,0:T(8,128)(2,1)}, u32[]{:S(2)}) copy-start(bf16[3,3,8,128]{3,2,1,0:T(8,128)(2,1)} %outlet_one.1) | copy-start | bytes 55300
  2.9 5.7 %collective-permute-start = (bf16[5,16,128]{2,1,0:T(8,128)(2,1)S(1)}, bf16[5,16,128]{2,1,0:T(8,128)(2,1)S(1)}, u32[]{:S(2)}, u32[]{:S(2)}) collective-permute-start(bf16[5,16,128]{2,1,0:T(8,128)(2,1)S(1)} %get-tuple-element.23), channel_id=1, source_target_pairs={{0,8},{8,16},{16,24},{24,0},{1,9},{9,17},{17,25},{25,1},{2,10},{10... | collective-permute-start | bytes 61448 | tf_op jit(solution)/shard_map/ppermute | solution.py:512
  5.9 3.8 %collective-permute-start.1 = (bf16[5,16,128]{2,1,0:T(8,128)(2,1)S(1)}, bf16[5,16,128]{2,1,0:T(8,128)(2,1)S(1)}, u32[]{:S(2)}, u32[]{:S(2)}) collective-permute-start(bf16[5,16,128]{2,1,0:T(8,128)(2,1)S(1)} %get-tuple-element.25), channel_id=1, source_target_pairs={{0,24},{8,0},{16,8},{24,16},{1,25},{9,1},{17,9},{25,17},{2,26},{10... | collective-permute-start | bytes 61448 | tf_op jit(solution)/shard_map/ppermute | solution.py:513
  8.6 19.1 %copy-start.27 = (f32[128]{0:T(128)S(1)}, f32[128]{0:T(128)}, u32[]{:S(2)}) copy-start(f32[128]{0:T(128)} %param.26) | copy-start | bytes 1540
  8.6 19.1 %copy-start.4 = (f32[8,32,128]{2,1,0:T(8,128)S(1)}, f32[8,32,128]{2,1,0:T(8,128)}, u32[]{:S(2)}) copy-start(f32[8,32,128]{2,1,0:T(8,128)} %param.20) | copy-start | bytes 393220
  9.6 18.0 %collective-permute-start.3 = (bf16[42,16,128]{2,1,0:T(8,128)(2,1)S(1)}, bf16[42,16,128]{2,1,0:T(8,128)(2,1)S(1)}, u32[]{:S(2)}, u32[]{:S(2)}) collective-permute-start(bf16[42,16,128]{2,1,0:T(8,128)(2,1)S(1)} %constant_dynamic-update-slice_fusion.own), channel_id=1, source_target_pairs={{0,7},{1,0},{2,1},{3,2},{4,3},{5,4},{6,5},{7,6},{8,15},{9,8},{10,9... | collective-permute-start | bytes 516104 | tf_op jit(solution)/shard_map/ppermute | solution.py:538
  11.3 16.4 %collective-permute-start.2 = (bf16[42,16,128]{2,1,0:T(8,128)(2,1)S(1)}, bf16[42,16,128]{2,1,0:T(8,128)(2,1)S(1)}, u32[]{:S(2)}, u32[]{:S(2)}) collective-permute-start(bf16[42,16,128]{2,1,0:T(8,128)(2,1)S(1)} %constant_dynamic-update-slice_fusion.own), channel_id=1, source_target_pairs={{0,1},{1,2},{2,3},{3,4},{4,5},{5,6},{6,7},{7,0},{8,9},{9,10},{10,1... | collective-permute-start | bytes 516104 | tf_op jit(solution)/shard_map/ppermute | solution.py:537
  11.3 1.6 %copy-start = (f32[8,16,4096]{2,1,0:T(8,128)S(1)}, f32[8,16,4096]{2,1,0:T(8,128)}, u32[]{:S(2)}) copy-start(f32[8,16,4096]{2,1,0:T(8,128)} %fine_far.1) | copy-start | bytes 6291460
  12.9 1.0 %copy-start.5 = (bf16[512,512]{1,0:T(8,128)(2,1)S(1)}, bf16[512,512]{1,0:T(8,128)(2,1)}, u32[]{:S(2)}) copy-start(bf16[512,512]{1,0:T(8,128)(2,1)} %constant.29.clone.turn) | copy-start | bytes 1572868
  13.9 0.9 %copy-start.8 = (s32[16,4096]{1,0:T(8,128)S(1)}, s32[16,4096]{1,0:T(8,128)}, u32[]{:S(2)}) copy-start(s32[16,4096]{1,0:T(8,128)} %land.1) | copy-start | bytes 786436
  14.8 0.9 %copy-start.11 = (bf16[224,144]{1,0:T(8,128)(2,1)S(1)}, bf16[224,144]{1,0:T(8,128)(2,1)}, u32[]{:S(2)}) copy-start(bf16[224,144]{1,0:T(8,128)(2,1)} %constant.30.clone.order) | copy-start | bytes 193540
  19.0 1.0 %copy-start.1 = (bf16[4,144,1024]{2,1,0:T(8,128)(2,1)}, bf16[4,144,1024]{2,1,0:T(8,128)(2,1)S(1)}, u32[]{:S(2)}) copy-start(bf16[4,144,1024]{2,1,0:T(8,128)(2,1)S(1)} %get-tuple-element.33.own) | copy-start | bytes 3538948
  20.0 0.7 %copy-start.10 = (bf16[4,16,1024]{2,1,0:T(8,128)(2,1)}, bf16[4,16,1024]{2,1,0:T(8,128)(2,1)S(1)}, u32[]{:S(2)}) copy-start(bf16[4,16,1024]{2,1,0:T(8,128)(2,1)S(1)} %get-tuple-element.34.land) | copy-start | bytes 393220
  20.6 18.2 %copy-start.26 = (f32[32]{0:T(128)S(1)}, f32[32]{0:T(128)}, u32[]{:S(2)}) copy-start(f32[32]{0:T(128)} %param.31) | copy-start | bytes 388
  20.6 18.3 %copy-start.25 = (bf16[128,32]{0,1:T(8,128)(2,1)S(1)}, bf16[128,32]{0,1:T(8,128)(2,1)}, u32[]{:S(2)}) copy-start(bf16[128,32]{0,1:T(8,128)(2,1)} %param.30) | copy-start | bytes 24580
  20.7 18.5 %copy-start.23 = (bf16[3,3,32,17]{2,1,3,0:T(4,128)(2,1)S(1)}, bf16[3,3,32,17]{2,1,3,0:T(4,128)(2,1)}, u32[]{:S(2)}) copy-start(bf16[3,3,32,17]{2,1,3,0:T(4,128)(2,1)} %param.29) | copy-start | bytes 29380
  20.7 18.6 %copy-start.12 = (bf16[3,3,32,32]{3,2,1,0:T(8,128)(2,1)S(1)}, bf16[3,3,32,32]{3,2,1,0:T(8,128)(2,1)}, u32[]{:S(2)}) copy-start(bf16[3,3,32,32]{3,2,1,0:T(8,128)(2,1)} %middle_two.1) | copy-start | bytes 55300
  20.7 18.6 %copy-start.16 = (bf16[3,3,8,32]{3,2,1,0:T(8,128)(2,1)S(1)}, bf16[3,3,8,32]{3,2,1,0:T(8,128)(2,1)}, u32[]{:S(2)}) copy-start(bf16[3,3,8,32]{3,2,1,0:T(8,128)(2,1)} %outlet_two.1) | copy-start | bytes 13828
  20.7 22.3 %collective-permute-start.4 = (bf16[4,32,1024]{2,1,0:T(8,128)(2,1)S(1)}, bf16[4,32,1024]{2,1,0:T(8,128)(2,1)S(1)}, u32[]{:S(2)}, u32[]{:S(2)}) collective-permute-start(bf16[4,32,1024]{2,1,0:T(8,128)(2,1)S(1)} %get-tuple-element.35), channel_id=1, source_target_pairs={{0,1},{1,2},{2,3},{3,4},{4,5},{5,6},{6,7},{7,8},{8,9},{9,10},{10,1... | collective-permute-start | bytes 786440 | tf_op jit(solution)/shard_map/ppermute | solution.py:533
  20.9 22.1 %collective-permute-start.5 = (bf16[4,32,1024]{2,1,0:T(8,128)(2,1)S(1)}, bf16[4,32,1024]{2,1,0:T(8,128)(2,1)S(1)}, u32[]{:S(2)}, u32[]{:S(2)}) collective-permute-start(bf16[4,32,1024]{2,1,0:T(8,128)(2,1)S(1)} %get-tuple-element.36), channel_id=1, source_target_pairs={{0,31},{1,0},{2,1},{3,2},{4,3},{5,4},{6,5},{7,6},{8,7},{9,8},{10,9... | collective-permute-start | bytes 786440 | tf_op jit(solution)/shard_map/ppermute | solution.py:534
  26.7 18.8 %copy-start.19 = (s32[6]{0:T(128)}, s32[6]{0:T(128)S(1)}, u32[]{:S(2)}) copy-start(s32[6]{0:T(128)S(1)} %stack.15.place) | copy-start | bytes 76
  35.3 10.1 %all-to-all-start = ((bf16[8,64,128]{2,1,0:T(8,128)(2,1)}), bf16[8,64,128]{2,1,0:T(8,128)(2,1)S(1)}, u32[]{:S(2)}, u32[]{:S(2)}) async-start(bf16[8,64,128]{2,1,0:T(8,128)(2,1)} %get-tuple-element.32), calls=%async_computation | async-start | bytes 262144 | tf_op jit(solution)/shard_map/all_to_all | solution.py:599
  40.7 0.9 %copy-start.2 = (bf16[4,192,512]{2,1,0:T(8,128)(2,1)}, bf16[4,192,512]{2,1,0:T(8,128)(2,1)S(1)}, u32[]{:S(2)}) copy-start(bf16[4,192,512]{2,1,0:T(8,128)(2,1)S(1)} %get-tuple-element.37.first_two) | copy-start | bytes 2359300
  41.6 0.7 %copy-start.6 = (bf16[192,768]{1,0:T(8,128)(2,1)}, bf16[192,768]{1,0:T(8,128)(2,1)S(1)}, u32[]{:S(2)}) copy-start(bf16[192,768]{1,0:T(8,128)(2,1)S(1)} %get-tuple-element.38.mid_two) | copy-start | bytes 884740
  42.3 0.7 %copy-start.9 = (bf16[192,320]{1,0:T(8,128)(2,1)}, bf16[192,320]{1,0:T(8,128)(2,1)S(1)}, u32[]{:S(2)}) copy-start(bf16[192,320]{1,0:T(8,128)(2,1)S(1)} %get-tuple-element.39.last_two) | copy-start | bytes 368644
  42.9 2.5 %copy-start.21 = (bf16[4,32,1024]{2,1,0:T(8,128)(2,1)}, bf16[4,32,1024]{2,1,0:T(8,128)(2,1)S(1)}, u32[]{:S(2)}) copy-start(bf16[4,32,1024]{2,1,0:T(8,128)(2,1)S(1)} %collective-permute-done.4.above) | copy-start | bytes 786436
  42.9 2.5 %copy-start.22 = (bf16[4,32,1024]{2,1,0:T(8,128)(2,1)}, bf16[4,32,1024]{2,1,0:T(8,128)(2,1)S(1)}, u32[]{:S(2)}) copy-start(bf16[4,32,1024]{2,1,0:T(8,128)(2,1)S(1)} %collective-permute-done.5.below) | copy-start | bytes 786436
  45.4 0.6 %copy-start.20 = (bf16[8,64,128]{2,1,0:T(8,128)(2,1)}, bf16[8,64,128]{2,1,0:T(8,128)(2,1)S(1)}, u32[]{:S(2)}) copy-start(bf16[8,64,128]{2,1,0:T(8,128)(2,1)S(1)} %all-to-all-done.coarse) | copy-start | bytes 393220

commit v3 on v2

--- a/solution.py
+++ b/solution.py
@@ -92,11 +92,34 @@
             bottom[y - tile_rows + 5] = made
 
 
+def edge_kernel(tile_rows, north, comb, south, tile, first_cols, last_cols):
+    cols = comb.shape[2]
+
+    def row(e):
+        if e < 5:
+            return north[e]
+        return comb[e - 5] if e < tile_rows + 5 else south[min(e - tile_rows - 5, 4)]
+
+    for g in range(tile.shape[1] // LANES):
+        block = jnp.concatenate([row(6 * g + i).astype(F32) for i in range(8)], axis=0)
+        turned = block.T.astype(BF)
+        at = slice(g * LANES, (g + 1) * LANES)
+        tile[:, at] = turned
+        first_cols[:, at] = turned[0:EDGE]
+        last_cols[:, at] = turned[cols - EDGE :]
+
+
 def sort_kernel(fine, land, turn, order, own, ground, to_next, to_prev):
+    blocks = []
     for m in range(fine.shape[1] // (4 * LANES)):
         cols = slice(4 * LANES * m, 4 * LANES * (m + 1))
-        block = jnp.concatenate([fine[:, cols], land[:, cols].astype(F32)], axis=0).astype(BF)
-        block = jnp.dot(block, turn[...], preferred_element_type=F32).astype(BF)
+        blocks += [fine[:, cols], land[:, cols].astype(F32)]
+    high = fine.shape[0] + land.shape[0]
+    sorted_all = jnp.dot(
+        jnp.concatenate(blocks, axis=0).astype(BF), turn[...], preferred_element_type=F32
+    )
+    for m in range(fine.shape[1] // (4 * LANES)):
+        block = sorted_all[m * high : (m + 1) * high].astype(BF)
         made = jnp.dot(order[...], block, preferred_element_type=F32).astype(BF)
         at = slice(m * LANES, (m + 1) * LANES)
         for j in range(4):
@@ -119,13 +142,12 @@
     made = embed(steps[0], ladder, timing[...])
     bias[...] = jnp.concatenate([made, made], axis=1)
     first_one[...] = jnp.zeros_like(first_one)
-    for dx in range(3):
-        for i in range(2):
-            for dy in range(3):
-                at = 192 + (i + dy) * 16
-                first_one[dx, at : at + 16, i * 128 : (i + 1) * 128] = (
-                    inlet_one[dy, dx].astype(F32).T.astype(BF)
-                )
+    for t in range(3):
+        for dx in range(3):
+            for i in range(2):
+                for dy in range(3):
+                    at = dx * LANES + (2 * t + i + dy) * 16
+                    first_one[t, at : at + 16, i * 128 : (i + 1) * 128] = inlet_one[dy, dx]
     mid_one[...] = jnp.zeros_like(mid_one)
     last_one[...] = jnp.zeros_like(last_one)
     for dx in range(3):
@@ -209,11 +231,12 @@
 
 
 def coarse_kernel(
-    tile_rows, cols, dests, place, steps, own, west, east, state, first_one, mid_one, last_one,
+    tile_rows, cols, dests, steps, north, south, own, west, east, state, first_one, mid_one, last_one,
     bias, scale, coarse_next, noise_one, sends, turned, hidden, active, summed, taps,
 ):
     px = cols + 2 * EDGE
-    rows_before, rows_total, cols_before, cols_total = (place[k] for k in range(4))
+    rows_before, cols_before = lax.axis_index("row") * tile_rows, lax.axis_index("col") * cols
+    rows_total, cols_total = lax.axis_size("row") * tile_rows, lax.axis_size("col") * cols
     keep, blend = plan(steps[0], (8, cols))
     ext = tile_rows + 10
     pairs = (tile_rows + 8) // 2
@@ -221,28 +244,22 @@
     half = lax.broadcasted_iota(jnp.int32, (px, 256), 1) // 128
     inside = jnp.where((column >= 0) & (column < cols_total), 1.0, 0.0)
 
-    windows = [min(14 * k, ext - 16) for k in range(-(-pairs // 7))]
-    for k, at in enumerate(windows):
-        parts = [
-            ref[at : at + 16].reshape(256, cols).astype(F32).T for ref in (west, own, east)
-        ]
-        whole = jnp.concatenate([parts[0][cols - EDGE :], parts[1], parts[2][:EDGE]], axis=0)
-        row = rows_before - 5 + at + lax.broadcasted_iota(jnp.int32, (px, 256), 1) // 16
-        whole = jnp.where((row >= 0) & (row < rows_total) & (inside > 0), whole, 0.0)
-        turned[k, 0] = pltpu.roll(whole, 1, 0).astype(BF)
-        turned[k, 1] = whole.astype(BF)
-        turned[k, 2] = pltpu.roll(whole, px - 1, 0).astype(BF)
+    gains = jnp.concatenate([scale[...], scale[...]], axis=1)
+    for g in range(-(-pairs // 3)):
+        lanes = slice(g * LANES, (g + 1) * LANES)
+        whole = jnp.concatenate([west[:, lanes], own[:, lanes], east[:, lanes]], axis=0).astype(F32)
+        row = rows_before - 5 + 6 * g + lax.broadcasted_iota(jnp.int32, (px, LANES), 1) // 16
+        whole = jnp.where((row >= 0) & (row < rows_total) & (inside[:, 0:LANES] > 0), whole, 0.0)
+        turned[g, :, 0:LANES] = pltpu.roll(whole, 1, 0).astype(BF)
+        turned[g, :, LANES : 2 * LANES] = whole.astype(BF)
+        turned[g, :, 2 * LANES :] = pltpu.roll(whole, px - 1, 0).astype(BF)
 
     def mask(first_row):
         row = rows_before - 5 + first_row + half
         return jnp.where((row >= 0) & (row < rows_total), inside, 0.0)
 
     for p in range(pairs):
-        k = p // 7
-        off = 192 - (2 * p - windows[k]) * 16
-        acc = jnp.dot(turned[k, 0], first_one[0, off : off + 256], preferred_element_type=F32)
-        for dx in (1, 2):
-            acc += jnp.dot(turned[k, dx], first_one[dx, off : off + 256], preferred_element_type=F32)
+        acc = jnp.dot(turned[p // 3], first_one[p % 3], preferred_element_type=F32)
         low = silu(acc + bias[0:1, :]).astype(BF)
         hidden[p] = low
         value = low.astype(F32)
@@ -251,23 +268,24 @@
         for h in range(2):
             mean = jnp.mean(square[:, h * 128 : (h + 1) * 128], axis=1, keepdims=True)
             scaled.append(value[:, h * 128 : (h + 1) * 128] * lax.rsqrt(mean + 1e-06))
-        act = silu(jnp.concatenate(scaled, axis=1) * scale[...]) * mask(1 + 2 * p)
+        act = silu(jnp.concatenate(scaled, axis=1) * gains) * mask(1 + 2 * p)
         active[p, :, 0:256] = pltpu.roll(act, 1, 0).astype(BF)
         active[p, :, 256:512] = act.astype(BF)
         active[p, :, 512:768] = pltpu.roll(act, px - 1, 0).astype(BF)
 
-    for p in range(pairs - 1):
-        acc = None
-        for dx in range(3):
-            for q in range(2):
-                at = dx * 512 + q * 256
-                term = jnp.dot(
-                    active[p + q, :, dx * 256 : (dx + 1) * 256], mid_one[at : at + 256],
-                    preferred_element_type=F32,
-                )
-                acc = term if acc is None else acc + term
-        rest = jnp.concatenate([hidden[p, :, 128:256], hidden[p + 1, :, 0:128]], axis=1)
-        summed[p] = ((acc + rest.astype(F32)) * mask(2 + 2 * p)).astype(BF)
+    for p in range(0, pairs - 1, 2):
+        size = min(2, pairs - 1 - p)
+        parts = [
+            active[p + q : p + q + size, :, dx * 256 : (dx + 1) * 256].reshape(size * px, 256)
+            for dx in range(3)
+            for q in range(2)
+        ]
+        acc = jnp.dot(jnp.concatenate(parts, axis=1), mid_one[...], preferred_element_type=F32)
+        for k in range(size):
+            n = p + k
+            rest = jnp.concatenate([hidden[n, :, 128:256], hidden[n + 1, :, 0:128]], axis=1)
+            value = acc[k * px : (k + 1) * px] + rest.astype(F32)
+            summed[n] = (value * mask(2 + 2 * n)).astype(BF)
 
     for p in range(pairs - 1):
         taps[p] = lax.dot_general(
@@ -293,7 +311,8 @@
                 noise_one[rows, :] = part
                 coarse_next[rows, :] = after
             else:
-                after = keep * own[y + 5].astype(F32)[0:8] + blend * part
+                edge = north[y + 5] if y < 0 else south[y - tile_rows]
+                after = keep * edge.astype(F32)[0:8] + blend * part
             made.append(after)
         made = jnp.concatenate(made, axis=0).astype(BF)
         for d in range(dests):
@@ -303,15 +322,17 @@
 
 
 def fine_kernel(
-    band, quarter, place, steps, coarse, fine_far, own, land, above, below, back, first_two, mid_two, last_two,
+    band, quarter, steps, coarse, fine_far, own, land, above, below, back, first_two, mid_two, last_two,
     fine_far_next, noise_far, rows_of, states, lifted, ground, hidden, summed, fine, fine_next, noise_two, sems,
 ):
     bring = pltpu.make_async_copy(fine_far, fine, sems.at[0])
     bring.start()
     keep, blend = plan(steps[1], (8, LANES))
     keep, blend = (jnp.concatenate([v] * 4, axis=1) for v in (keep, blend))
-    top = jnp.where(place[4] > 0, 1.0, 0.0)
-    bottom = jnp.where(place[4] < place[5] - 1, 1.0, 0.0)
+    position = lax.axis_index("row") * lax.axis_size("col") + lax.axis_index("col")
+    count = lax.axis_size("row") * lax.axis_size("col")
+    top = jnp.where(position > 0, 1.0, 0.0)
+    bottom = jnp.where(position < count - 1, 1.0, 0.0)
     ext = band + 6
     quota = band // 4
     sources = quarter // LANES
@@ -424,14 +445,16 @@
         west = [edge(made[3][0:high], 1)] + [made[j][0:high] for j in range(3)]
         east = [made[j][2 * high :] for j in range(1, 4)] + [edge(made[0][2 * high :], -1)]
         phases = [west[j] + made[j][high : 2 * high] + east[j] for j in range(4)]
+        value = jnp.concatenate(
+            [
+                jnp.concatenate([p[:, m * LANES : (m + 1) * LANES] for p in phases], axis=1)
+                for m in range(sources)
+            ],
+            axis=0,
+        )
+        back_all = jnp.dot(value.astype(BF), back[...], preferred_element_type=F32)
         for m in range(sources):
-            value = jnp.concatenate([p[:, m * LANES : (m + 1) * LANES] for p in phases], axis=1)
-            rough = value.astype(BF)
-            fine_part = (value - rough.astype(F32)).astype(BF)
-            noise = jnp.dot(
-                jnp.concatenate([rough, fine_part], axis=0), back[...], preferred_element_type=F32
-            )
-            noise = noise[0:high] + noise[high:]
+            noise = back_all[m * high : (m + 1) * high]
             cols = slice(4 * LANES * m, 4 * LANES * (m + 1))
             for o in range(8):
                 rows = slice(s, s + ROWS3)
@@ -477,18 +500,11 @@
     fields, tile_rows, cols = coarse_state.shape
     _, band, width = fine_state.shape
     row_count, col_count = lax.axis_size("row"), lax.axis_size("col")
-    row_at, col_at = lax.axis_index("row"), lax.axis_index("col")
     count = row_count * col_count
     state = coarse_state.reshape(fields * tile_rows, cols)
     forcing = coarse_forcing.reshape(fields * tile_rows, cols)
     fine = fine_state.reshape(fields * band, width)
     quarter = width // 4
-    place = jnp.stack(
-        [
-            row_at * tile_rows, jnp.int32(row_count * tile_rows), col_at * cols,
-            jnp.int32(col_count * cols), row_at * col_count + col_at, jnp.int32(count),
-        ]
-    ).astype(jnp.int32)
     ladder = ladder_rows(timing_one.shape[0])
 
     comb, first_rows, last_rows = pl.pallas_call(
@@ -506,14 +522,14 @@
             pltpu.VMEM((fields * tile_rows, cols), BF),
             pltpu.SemaphoreType.DMA((2,)),
         ],
-        compiler_params=params(8),
+        compiler_params=params(60),
         name="pack",
     )(state, forcing)
     north = lax.ppermute(last_rows, "row", shift_pairs(row_count, 1))
     south = lax.ppermute(first_rows, "row", shift_pairs(row_count, -1))
 
     turn = turn_matrix()
-    split = 1024
+    split = 2048
     part = split // 4
     shapes = (8 * (band + 2), 16, 32, 32)
     own, ground, to_next, to_prev = pl.pallas_call(
@@ -527,29 +543,44 @@
             pl.BlockSpec((80 + 8 * (band + 2), 9 * band), lambda n: (0, 0)),
         ],
         out_specs=[pl.BlockSpec((4, rows, part), lambda n: (0, 0, n)) for rows in shapes],
-        compiler_params=params(24),
+        compiler_params=params(60),
         name="sort",
     )(fine, land_mask, jnp.asarray(turn, BF), jnp.asarray(order_matrix(band), BF))
-    above = lax.ppermute(to_next, ("row", "col"), shift_pairs(count, 1))
-    below = lax.ppermute(to_prev, ("row", "col"), shift_pairs(count, -1))
-
-    tall = jnp.concatenate([north, comb, south], axis=0)
-    west = lax.ppermute(tall, "col", shift_pairs(col_count, 1))
-    east = lax.ppermute(tall, "col", shift_pairs(col_count, -1))
-
+    north, to_next, to_prev = lax.optimization_barrier((north, to_next, to_prev))
+    deep_rows = -(-(tile_rows + 8) // 6) * LANES
+    tile, first_cols, last_cols = pl.pallas_call(
+        functools.partial(edge_kernel, tile_rows),
+        out_shape=(
+            jax.ShapeDtypeStruct((cols, deep_rows), BF),
+            jax.ShapeDtypeStruct((EDGE, deep_rows), BF),
+            jax.ShapeDtypeStruct((EDGE, deep_rows), BF),
+        ),
+        in_specs=[VMEM] * 3,
+        out_specs=[VMEM] * 3,
+        compiler_params=params(8),
+        name="edges",
+    )(north, comb, south)
+    west = lax.ppermute(last_cols, "col", shift_pairs(col_count, 1))
+    east = lax.ppermute(first_cols, "col", shift_pairs(col_count, -1))
+    turned_inlet, first_cols = lax.optimization_barrier(
+        (jnp.transpose(inlet_one, (0, 1, 3, 2)), first_cols)
+    )
     first_one, mid_one, last_one, bias = pl.pallas_call(
         coarse_weights,
         out_shape=(
-            jax.ShapeDtypeStruct((3, 448, 256), BF),
+            jax.ShapeDtypeStruct((3, 3 * LANES, 256), BF),
             jax.ShapeDtypeStruct((1536, 256), BF),
             jax.ShapeDtypeStruct((96, 256), BF),
             jax.ShapeDtypeStruct((8, 256), F32),
         ),
         in_specs=[SMEM] + [WHOLE] * 5,
         out_specs=[VMEM] * 4,
-        compiler_params=params(8),
+        compiler_params=params(60),
         name="coarse_weights",
-    )(step_index, ladder, timing_one, inlet_one, middle_one, outlet_one)
+    )(step_index, ladder, timing_one, turned_inlet, middle_one, outlet_one)
+    to_next, to_prev, west, east, bias = lax.optimization_barrier((to_next, to_prev, west, east, bias))
+    above = lax.ppermute(to_next, ("row", "col"), shift_pairs(count, 1))
+    below = lax.ppermute(to_prev, ("row", "col"), shift_pairs(count, -1))
     blocks = len(starts_of(band + 4, ROWS1))
     deep = LANES + 6 * 8 * (ROWS1 + 2)
     first_two, mid_two, last_two = pl.pallas_call(
@@ -566,7 +597,7 @@
             pltpu.VMEM((32 * ROWS2, 768), F32),
             pltpu.VMEM((24 * ROWS3, 32 * (ROWS3 + 2)), F32),
         ],
-        compiler_params=params(8),
+        compiler_params=params(60),
         name="fine_weights",
     )(step_index, ladder, timing_two, inlet_two, middle_two, outlet_two, land_bias[:, None])
 
@@ -580,20 +611,20 @@
             jax.ShapeDtypeStruct((fields * tile_rows, cols), F32),
             jax.ShapeDtypeStruct((col_count, (each + 4) * fields, cols), BF),
         ),
-        in_specs=[SMEM] * 2 + [VMEM] * 9,
+        in_specs=[SMEM] + [VMEM] * 11,
         out_specs=[VMEM] * 3,
         scratch_shapes=[
-            pltpu.VMEM((-(-pairs // 7), 3, px, 256), BF),
+            pltpu.VMEM((-(-pairs // 3), px, 3 * LANES), BF),
             pltpu.VMEM((pairs, px, 256), BF),
             pltpu.VMEM((pairs, px, 768), BF),
             pltpu.VMEM((pairs - 1, px, 256), BF),
             pltpu.VMEM((pairs - 1, 96, px), F32),
         ],
-        compiler_params=params(40),
+        compiler_params=params(60),
         name="coarse",
     )(
-        place, step_index, tall, west, east, state, first_one, mid_one, last_one, bias,
-        jnp.tile(scale_one, 2)[None, :],
+        step_index, north, south, tile, west, east, state, first_one, mid_one, last_one, bias,
+        scale_one[None, :],
     )
 
     arrived = lax.all_to_all(sends, "col", split_axis=0, concat_axis=0, tiled=True)
@@ -604,7 +635,7 @@
             jax.ShapeDtypeStruct((fields, band, width), F32),
             jax.ShapeDtypeStruct((fields, band, width), F32),
         ),
-        in_specs=[SMEM] * 2 + [VMEM, ANY] + [VMEM] * 8,
+        in_specs=[SMEM] + [VMEM, ANY] + [VMEM] * 8,
         out_specs=[ANY] * 2,
         scratch_shapes=[
             pltpu.VMEM(((band + 6) * 8, quarter), F32),
@@ -618,10 +649,10 @@
             pltpu.VMEM((fields, band, width), F32),
             pltpu.SemaphoreType.DMA((1 + 2 * (band // ROWS3),)),
         ],
-        compiler_params=params(56),
+        compiler_params=params(60),
         name="fine",
     )(
-        place, step_index, arrived, fine_state, own, ground, above, below, jnp.asarray(turn.T, BF),
+        step_index, arrived, fine_state, own, ground, above, below, jnp.asarray(turn.T, BF),
         first_two, mid_two, last_two,
     )
 

time: 61.4 us -> 56.4 us (0.919)
  local copies, waits for them, and re-layouts: 11.5 us -> 3.74 us
  Pallas kernels: 28.4 us -> 33.2 us
  waiting for transfers between devices: 5.21 us -> 1.63 us
  starting transfers between devices: 14.8 us -> 16.5 us
    unnamed x61 -> x26, local copies, waits for them, and re-layouts: 11.4 us -> 3.06 us
    ppermute x2, starting transfers between devices: 1.61 us -> 3.54 us  [the longest x1 3.54 us: body(): east = lax.ppermute(first_cols, 'col', shift_pairs(col_count, -1))]
    ppermute x1, waiting for transfers between devices: 1.7 us -> 0.01 us  [body(): north = lax.ppermute(last_rows, 'row', shift_pairs(row_count, 1))]
    pallas_call x1 -> x2, Pallas kernels: 0.94 us -> 2.39 us  [the longest x1 2.25 us: body(): pl.pallas_call(coarse_weights, out_shape=(jax.ShapeDtypeStruct((3, 3 * LA...]
    pallas_call x1, Pallas kernels: 1.39 us -> 2.72 us  [body(): pl.pallas_call(functools.partial(fine_weights, band), out_shape=(jax.Shap...]
    pallas_call x1, Pallas kernels: 0.43 us -> 1.74 us  [body(): pl.pallas_call(functools.partial(pack_kernel, tile_rows), out_shape=(jax....]
    ppermute x1, waiting for transfers between devices: 1.03 us -> 0.01 us  [body(): south = lax.ppermute(first_rows, 'row', shift_pairs(row_count, -1))]
    all_to_all x1, waiting for transfers between devices: 2.46 us -> 1.62 us  [body(): lax.all_to_all(sends, 'col', split_axis=0, concat_axis=0, tiled=True)]
  transfers between devices with their start and end apart: 7 -> 7, of which waited for: 3 -> 1; matrix products, arithmetic and copies ran while one was open for 1% -> 4% of each run, Pallas kernels for 22% -> 30%
where the time goes in v3:
time: 56.4 us; the launch traced here: 56 us
  Pallas kernels  33.2 us (59%)
  starting transfers between devices  16.5 us (29%)
  local copies, waits for them, and re-layouts  3.74 us (7%)
  waiting for transfers between devices  1.63 us (3%)
  between operations  0.96 us (2%)
    pallas_call x1, Pallas kernels, body(): pl.pallas_call(functools.partial(fine_kernel, band, quarter), out_shape=(...  14.5 us
    pallas_call x1, Pallas kernels, body(): pl.pallas_call(functools.partial(coarse_kernel, tile_rows, cols, col_coun...  8.06 us
    ppermute x1, starting transfers between devices, body(): below = lax.ppermute(to_prev, ('row', 'col'), shift_pairs(count, -1))  5.33 us
    pallas_call x1, Pallas kernels, body(): pl.pallas_call(sort_kernel, grid=(width // split,), out_shape=[jax.ShapeD...  3.78 us
    all_to_all x1, starting transfers between devices, body(): lax.all_to_all(sends, 'col', split_axis=0, concat_axis=0, tiled=True)  3.55 us
    ppermute x1, starting transfers between devices, body(): east = lax.ppermute(first_cols, 'col', shift_pairs(col_count, -1))  3.54 us
    unnamed x26, local copies, waits for them, and re-layouts  3.06 us
    ppermute x1, starting transfers between devices, body(): north = lax.ppermute(last_rows, 'row', shift_pairs(row_count, 1))  2.99 us
  transfers between devices with their start and end apart: 7, of which 1 were waited for; matrix products, arithmetic and copies ran while one was open for 4% of the time, Pallas kernels for 30%

profile of v3, /device:TPU:0, one launch (start us, length us, event | category | flops | bytes accessed | tf_op | source)
XLA Modules:
  0.0 56.0 jit_solution(15817001823580882868)
XLA Ops:
  0.6 1.7 %pack.1 = (bf16[32,16,128]{2,1,0:T(8,128)(2,1)}, bf16[5,16,128]{2,1,0:T(8,128)(2,1)}, bf16[5,16,128]{2,1,0:T(8,128)(2,1)}) custom-call(f32[256,128]{1,0:T(8,128)} %bitcast.9, bf16[256,128]{1,0:T(8,128)(2,1)} %bitcast.11), custom_call_target="tpu_custom_call" | custom-call | tf_op jit(solution)/shard_map/pack/pallas_call | solution.py:510
  2.4 0.0 copy-start.1
  2.4 3.0 %collective-permute-start = (bf16[5,16,128]{2,1,0:T(8,128)(2,1)}, bf16[5,16,128]{2,1,0:T(8,128)(2,1)S(1)}, u32[]{:S(2)}, u32[]{:S(2)}) collective-permute-start(bf16[5,16,128]{2,1,0:T(8,128)(2,1)} %get-tuple-element.35), channel_id=1, source_target_pairs={{0,8},{8,16},{16,24},{24,0},{1,9},{9,17},{17,25},{25,1},{2,10},{10... | collective-permute-start | bytes 61448 | tf_op jit(solution)/shard_map/ppermute | solution.py:528
  5.4 1.0 %collective-permute-start.1 = (bf16[5,16,128]{2,1,0:T(8,128)(2,1)}, bf16[5,16,128]{2,1,0:T(8,128)(2,1)S(1)}, u32[]{:S(2)}, u32[]{:S(2)}) collective-permute-start(bf16[5,16,128]{2,1,0:T(8,128)(2,1)} %get-tuple-element.39), channel_id=1, source_target_pairs={{0,24},{8,0},{16,8},{24,16},{1,25},{9,1},{17,9},{25,17},{2,26},{10... | collective-permute-start | bytes 61448 | tf_op jit(solution)/shard_map/ppermute | solution.py:529
  6.4 3.8 %sort.1 = (bf16[4,144,1024]{2,1,0:T(8,128)(2,1)}, bf16[4,16,1024]{2,1,0:T(8,128)(2,1)}, bf16[4,32,1024]{2,1,0:T(8,128)(2,1)}, bf16[4,32,1024]{2,1,0:T(8,128)(2,1)}) custom-call(f32[128,4096]{1,0:T(8,128)} %bitcast.8, s32[16,4096]{1,0:T(8,128)} %land.1, bf16[512,512]{1,0:T(8,128)(2,1)} %constant.9.clone.turn, bf16[224,144]{1,0:T(8,128)(2,1)} %constant.10.clone.order), custom_call_target="tpu_custom_call" | custom-call | tf_op jit(solution)/shard_map/sort/pallas_call | solution.py:535
  10.2 0.0 copy-start.11
  10.2 0.0 copy-start.10
  10.2 0.0 copy-start.7
  10.2 0.0 collective-permute-done.north
  10.2 0.0 copy-start.2
  10.2 0.0 collective-permute-done.1.south
  10.2 0.0 copy-start.3
  10.3 0.0 copy-done.1
  10.3 0.1 edges.1
  10.4 0.0 copy-start
  10.4 0.7 %copy-done = bf16[128,896]{1,0:T(8,128)(2,1)} copy-done((bf16[128,896]{1,0:T(8,128)(2,1)}, bf16[128,896]{1,0:T(8,128)(2,1)S(1)}, u32[]{:S(2)}) %copy-start) | copy-done | bytes 229400
  11.1 0.0 collective-permute-start.2
  11.1 3.5 %collective-permute-start.3 = (bf16[16,896]{1,0:T(8,128)(2,1)S(1)}, bf16[16,896]{1,0:T(8,128)(2,1)S(1)}, u32[]{:S(2)}, u32[]{:S(2)}) collective-permute-start(bf16[16,896]{1,0:T(8,128)(2,1)S(1)} %get-tuple-element.45), channel_id=1, source_target_pairs={{0,7},{1,0},{2,1},{3,2},{4,3},{5,4},{6,5},{7,6},{8,15},{9,8},{10,9... | collective-permute-start | bytes 86024 | tf_op jit(solution)/shard_map/ppermute | solution.py:564
  14.7 2.3 %coarse_weights.1 = (bf16[3,384,256]{2,1,0:T(8,128)(2,1)}, bf16[1536,256]{1,0:T(8,128)(2,1)}, bf16[96,256]{1,0:T(8,128)(2,1)}, f32[8,256]{1,0:T(8,128)}) custom-call(s32[2]{0:T(128)} %steps.7, f32[8,128]{1,0:T(8,128)} %constant.8.clone.ladder, bf16[128,128]{1,0:T(8,128)(2,1)} %timing.2, bf16[3,3,16,128]{3,2,1,0:T(8,128)(2,1)} %bitcast.12, ...), custom_call_target="tpu_custom_call" | custom-call | tf_op jit(solution)/shard_map/coarse_weights/pallas_call | solution.py:568
  16.9 0.0 collective-permute-done.2.west
  16.9 0.0 copy-start.8
  16.9 0.0 collective-permute-done.3.east
  16.9 0.0 copy-start.9
  16.9 0.1 collective-permute-start.4
  17.0 5.3 %collective-permute-start.5 = (bf16[4,32,1024]{2,1,0:T(8,128)(2,1)}, bf16[4,32,1024]{2,1,0:T(8,128)(2,1)S(1)}, u32[]{:S(2)}, u32[]{:S(2)}) collective-permute-start(bf16[4,32,1024]{2,1,0:T(8,128)(2,1)} %get-tuple-element.60), channel_id=1, source_target_pairs={{0,31},{1,0},{2,1},{3,2},{4,3},{5,4},{6,5},{7,6},{8,7},{9,8},{10,9... | collective-permute-start | bytes 786440 | tf_op jit(solution)/shard_map/ppermute | solution.py:583
  22.3 0.0 copy-done.2
  22.3 0.0 copy-done.3
  22.3 0.0 copy-done.8
  22.3 0.0 copy-done.9
  22.3 8.1 %coarse.1 = (f32[256,128]{1,0:T(8,128)}, f32[256,128]{1,0:T(8,128)}, bf16[8,64,128]{2,1,0:T(8,128)(2,1)}) custom-call(s32[2]{0:T(128)} %steps.7, bf16[5,16,128]{2,1,0:T(8,128)(2,1)} %copy-done.2, bf16[5,16,128]{2,1,0:T(8,128)(2,1)} %copy-done.3, bf16[128,896]{1,0:T(8,128)(2,1)} %copy-done, bf16[16,896]{1,0:T(8,128)(2,1)} %copy-done.8, ...), custom_call_target="tpu_custom_call" | custom-call | tf_op jit(solution)/shard_map/coarse/pallas_call | solution.py:607
  30.4 3.5 %all-to-all-start = ((bf16[8,64,128]{2,1,0:T(8,128)(2,1)}), bf16[8,64,128]{2,1,0:T(8,128)(2,1)S(1)}, u32[]{:S(2)}, u32[]{:S(2)}) async-start(bf16[8,64,128]{2,1,0:T(8,128)(2,1)} %get-tuple-element.56), calls=%async_computation | async-start | bytes 262144 | tf_op jit(solution)/shard_map/all_to_all | solution.py:630
  34.0 0.0 copy-done.11
  34.0 0.7 %copy.25.land_bias = f32[32,1]{1,0:T(8,128)} copy(f32[32,1]{0,1:T(1,128)S(1)} %bitcast.14) | data formatting | bytes 256 | tf_op jit(solution)/shard_map/broadcast_in_dim | solution.py:602
  34.7 0.0 copy-done.10
  34.7 0.7 %copy.23.timing = bf16[128,32]{1,0:T(8,128)(2,1)} copy(bf16[128,32]{0,1:T(8,128)(2,1)S(1)} %copy-done.10) | data formatting | bytes 16384 | tf_op args[11]
  35.4 0.0 copy-done.7
  35.4 0.8 %copy.24.inlet_two = bf16[3,3,32,17]{3,2,1,0:T(8,128)(2,1)} copy(bf16[3,3,32,17]{2,1,3,0:T(4,128)(2,1)S(1)} %copy-done.7) | data formatting | bytes 19584 | tf_op args[10]
  36.2 2.7 %fine_weights.1 = (bf16[4,192,512]{2,1,0:T(8,128)(2,1)}, bf16[192,768]{1,0:T(8,128)(2,1)}, bf16[192,320]{1,0:T(8,128)(2,1)}) custom-call(s32[2]{0:T(128)} %steps.7, f32[8,128]{1,0:T(8,128)} %constant.8.clone.ladder, bf16[128,32]{1,0:T(8,128)(2,1)} %copy.23.timing, bf16[3,3,32,17]{3,2,1,0:T(8,128)(2,1)} %copy.24.inlet_two, bf16[3,3,32,32]{3,2,1,0:T(8,128)(2,1)} %middle_two.1, ...), custom_call_target="tpu_custom_call" | custom-call | tf_op jit(solution)/shard_map/fine_weights/pallas_call | solution.py:586
  38.9 1.6 %all-to-all-done.coarse = bf16[8,64,128]{2,1,0:T(8,128)(2,1)S(1)} async-done(((bf16[8,64,128]{2,1,0:T(8,128)(2,1)}), bf16[8,64,128]{2,1,0:T(8,128)(2,1)S(1)}, u32[]{:S(2)}, u32[]{:S(2)}) %all-to-all-start) | async-done | bytes 131104 | tf_op jit(solution)/shard_map/all_to_all | solution.py:630
  40.5 0.0 copy-start.4
  40.5 0.0 collective-permute-done.4.above
  40.5 0.0 copy-start.5
  40.5 0.0 collective-permute-done.5.below
  40.5 0.0 copy-start.6
  40.5 0.6 %copy-done.4 = bf16[8,64,128]{2,1,0:T(8,128)(2,1)} copy-done((bf16[8,64,128]{2,1,0:T(8,128)(2,1)}, bf16[8,64,128]{2,1,0:T(8,128)(2,1)S(1)}, u32[]{:S(2)}) %copy-start.4) | copy-done | bytes 131096
  41.1 0.1 copy-done.5
  41.3 0.1 copy-done.6
  41.4 14.5 %fine.1 = (f32[8,16,4096]{2,1,0:T(8,128)}, f32[8,16,4096]{2,1,0:T(8,128)}) custom-call(s32[2]{0:T(128)} %steps.7, bf16[8,64,128]{2,1,0:T(8,128)(2,1)} %copy-done.4, f32[8,16,4096]{2,1,0:T(8,128)} %fine_far.1, bf16[4,144,1024]{2,1,0:T(8,128)(2,1)} %get-tuple-element.57.own, bf16[4,16,1024]{2,1,0:T(8,128)(2,1)} %get-tuple-element.58.land, ...), custom_call_target="tpu_custom_call" | custom-call | tf_op jit(solution)/shard_map/fine/pallas_call | solution.py:632
Async XLA Ops:
  2.4 7.9 %copy-start.1 = (bf16[32,16,128]{2,1,0:T(8,128)(2,1)S(1)}, bf16[32,16,128]{2,1,0:T(8,128)(2,1)}, u32[]{:S(2)}) copy-start(bf16[32,16,128]{2,1,0:T(8,128)(2,1)} %get-tuple-element.40.comb) | copy-start | bytes 393220
  2.4 7.8 %collective-permute-start = (bf16[5,16,128]{2,1,0:T(8,128)(2,1)}, bf16[5,16,128]{2,1,0:T(8,128)(2,1)S(1)}, u32[]{:S(2)}, u32[]{:S(2)}) collective-permute-start(bf16[5,16,128]{2,1,0:T(8,128)(2,1)} %get-tuple-element.35), channel_id=1, source_target_pairs={{0,8},{8,16},{16,24},{24,0},{1,9},{9,17},{17,25},{25,1},{2,10},{10... | collective-permute-start | bytes 61448 | tf_op jit(solution)/shard_map/ppermute | solution.py:528
  5.4 4.9 %collective-permute-start.1 = (bf16[5,16,128]{2,1,0:T(8,128)(2,1)}, bf16[5,16,128]{2,1,0:T(8,128)(2,1)S(1)}, u32[]{:S(2)}, u32[]{:S(2)}) collective-permute-start(bf16[5,16,128]{2,1,0:T(8,128)(2,1)} %get-tuple-element.39), channel_id=1, source_target_pairs={{0,24},{8,0},{16,8},{24,16},{1,25},{9,1},{17,9},{25,17},{2,26},{10... | collective-permute-start | bytes 61448 | tf_op jit(solution)/shard_map/ppermute | solution.py:529
  10.2 23.8 %copy-start.11 = (f32[32]{0:T(128)S(1)}, f32[32]{0:T(128)}, u32[]{:S(2)}) copy-start(f32[32]{0:T(128)} %param.31) | copy-start | bytes 388
  10.2 24.5 %copy-start.10 = (bf16[128,32]{0,1:T(8,128)(2,1)S(1)}, bf16[128,32]{0,1:T(8,128)(2,1)}, u32[]{:S(2)}) copy-start(bf16[128,32]{0,1:T(8,128)(2,1)} %param.30) | copy-start | bytes 24580
  10.2 25.2 %copy-start.7 = (bf16[3,3,32,17]{2,1,3,0:T(4,128)(2,1)S(1)}, bf16[3,3,32,17]{2,1,3,0:T(4,128)(2,1)}, u32[]{:S(2)}) copy-start(bf16[3,3,32,17]{2,1,3,0:T(4,128)(2,1)} %param.29) | copy-start | bytes 29380
  10.2 12.1 %copy-start.2 = (bf16[5,16,128]{2,1,0:T(8,128)(2,1)}, bf16[5,16,128]{2,1,0:T(8,128)(2,1)S(1)}, u32[]{:S(2)}) copy-start(bf16[5,16,128]{2,1,0:T(8,128)(2,1)S(1)} %collective-permute-done.north) | copy-start | bytes 61444
  10.2 12.1 %copy-start.3 = (bf16[5,16,128]{2,1,0:T(8,128)(2,1)}, bf16[5,16,128]{2,1,0:T(8,128)(2,1)S(1)}, u32[]{:S(2)}) copy-start(bf16[5,16,128]{2,1,0:T(8,128)(2,1)S(1)} %collective-permute-done.1.south) | copy-start | bytes 61444
  10.4 0.7 %copy-start = (bf16[128,896]{1,0:T(8,128)(2,1)}, bf16[128,896]{1,0:T(8,128)(2,1)S(1)}, u32[]{:S(2)}) copy-start(bf16[128,896]{1,0:T(8,128)(2,1)S(1)} %get-tuple-element.41.own) | copy-start | bytes 688132
  11.1 5.8 %collective-permute-start.2 = (bf16[16,896]{1,0:T(8,128)(2,1)S(1)}, bf16[16,896]{1,0:T(8,128)(2,1)S(1)}, u32[]{:S(2)}, u32[]{:S(2)}) collective-permute-start(bf16[16,896]{1,0:T(8,128)(2,1)S(1)} %get-tuple-element.44), channel_id=1, source_target_pairs={{0,1},{1,2},{2,3},{3,4},{4,5},{5,6},{6,7},{7,0},{8,9},{9,10},{10,1... | collective-permute-start | bytes 86024 | tf_op jit(solution)/shard_map/ppermute | solution.py:563
  11.1 5.8 %collective-permute-start.3 = (bf16[16,896]{1,0:T(8,128)(2,1)S(1)}, bf16[16,896]{1,0:T(8,128)(2,1)S(1)}, u32[]{:S(2)}, u32[]{:S(2)}) collective-permute-start(bf16[16,896]{1,0:T(8,128)(2,1)S(1)} %get-tuple-element.45), channel_id=1, source_target_pairs={{0,7},{1,0},{2,1},{3,2},{4,3},{5,4},{6,5},{7,6},{8,15},{9,8},{10,9... | collective-permute-start | bytes 86024 | tf_op jit(solution)/shard_map/ppermute | solution.py:564
  16.9 5.4 %copy-start.8 = (bf16[16,896]{1,0:T(8,128)(2,1)}, bf16[16,896]{1,0:T(8,128)(2,1)S(1)}, u32[]{:S(2)}) copy-start(bf16[16,896]{1,0:T(8,128)(2,1)S(1)} %collective-permute-done.2.west) | copy-start | bytes 86020
  16.9 5.4 %copy-start.9 = (bf16[16,896]{1,0:T(8,128)(2,1)}, bf16[16,896]{1,0:T(8,128)(2,1)S(1)}, u32[]{:S(2)}) copy-start(bf16[16,896]{1,0:T(8,128)(2,1)S(1)} %collective-permute-done.3.east) | copy-start | bytes 86020
  16.9 23.6 %collective-permute-start.4 = (bf16[4,32,1024]{2,1,0:T(8,128)(2,1)}, bf16[4,32,1024]{2,1,0:T(8,128)(2,1)S(1)}, u32[]{:S(2)}, u32[]{:S(2)}) collective-permute-start(bf16[4,32,1024]{2,1,0:T(8,128)(2,1)} %get-tuple-element.59), channel_id=1, source_target_pairs={{0,1},{1,2},{2,3},{3,4},{4,5},{5,6},{6,7},{7,8},{8,9},{9,10},{10,1... | collective-permute-start | bytes 786440 | tf_op jit(solution)/shard_map/ppermute | solution.py:582
  17.0 23.5 %collective-permute-start.5 = (bf16[4,32,1024]{2,1,0:T(8,128)(2,1)}, bf16[4,32,1024]{2,1,0:T(8,128)(2,1)S(1)}, u32[]{:S(2)}, u32[]{:S(2)}) collective-permute-start(bf16[4,32,1024]{2,1,0:T(8,128)(2,1)} %get-tuple-element.60), channel_id=1, source_target_pairs={{0,31},{1,0},{2,1},{3,2},{4,3},{5,4},{6,5},{7,6},{8,7},{9,8},{10,9... | collective-permute-start | bytes 786440 | tf_op jit(solution)/shard_map/ppermute | solution.py:583
  30.4 10.1 %all-to-all-start = ((bf16[8,64,128]{2,1,0:T(8,128)(2,1)}), bf16[8,64,128]{2,1,0:T(8,128)(2,1)S(1)}, u32[]{:S(2)}, u32[]{:S(2)}) async-start(bf16[8,64,128]{2,1,0:T(8,128)(2,1)} %get-tuple-element.56), calls=%async_computation | async-start | bytes 262144 | tf_op jit(solution)/shard_map/all_to_all | solution.py:630
  40.5 0.6 %copy-start.4 = (bf16[8,64,128]{2,1,0:T(8,128)(2,1)}, bf16[8,64,128]{2,1,0:T(8,128)(2,1)S(1)}, u32[]{:S(2)}) copy-start(bf16[8,64,128]{2,1,0:T(8,128)(2,1)S(1)} %all-to-all-done.coarse) | copy-start | bytes 393220
  40.5 0.8 %copy-start.5 = (bf16[4,32,1024]{2,1,0:T(8,128)(2,1)}, bf16[4,32,1024]{2,1,0:T(8,128)(2,1)S(1)}, u32[]{:S(2)}) copy-start(bf16[4,32,1024]{2,1,0:T(8,128)(2,1)S(1)} %collective-permute-done.4.above) | copy-start | bytes 786436
  40.5 0.8 %copy-start.6 = (bf16[4,32,1024]{2,1,0:T(8,128)(2,1)}, bf16[4,32,1024]{2,1,0:T(8,128)(2,1)S(1)}, u32[]{:S(2)}) copy-start(bf16[4,32,1024]{2,1,0:T(8,128)(2,1)S(1)} %collective-permute-done.5.below) | copy-start | bytes 786436

commit v4 on v3

--- a/solution.py
+++ b/solution.py
@@ -16,6 +16,7 @@
 ANY = pl.BlockSpec(memory_space=pl.ANY)
 WHOLE = pl.BlockSpec()
 EDGE = 16
+MARGIN = 8
 ROWS1 = 6
 ROWS2 = 6
 ROWS3 = 8
@@ -234,20 +235,23 @@
     tile_rows, cols, dests, steps, north, south, own, west, east, state, first_one, mid_one, last_one,
     bias, scale, coarse_next, noise_one, sends, turned, hidden, active, summed, taps,
 ):
-    px = cols + 2 * EDGE
+    px = cols + 2 * MARGIN
     rows_before, cols_before = lax.axis_index("row") * tile_rows, lax.axis_index("col") * cols
     rows_total, cols_total = lax.axis_size("row") * tile_rows, lax.axis_size("col") * cols
     keep, blend = plan(steps[0], (8, cols))
     ext = tile_rows + 10
     pairs = (tile_rows + 8) // 2
-    column = cols_before - EDGE + lax.broadcasted_iota(jnp.int32, (px, 256), 0)
+    column = cols_before - MARGIN + lax.broadcasted_iota(jnp.int32, (px, 256), 0)
     half = lax.broadcasted_iota(jnp.int32, (px, 256), 1) // 128
     inside = jnp.where((column >= 0) & (column < cols_total), 1.0, 0.0)
 
     gains = jnp.concatenate([scale[...], scale[...]], axis=1)
     for g in range(-(-pairs // 3)):
         lanes = slice(g * LANES, (g + 1) * LANES)
-        whole = jnp.concatenate([west[:, lanes], own[:, lanes], east[:, lanes]], axis=0).astype(F32)
+        sides = [ref[:, lanes].astype(F32) for ref in (west, own, east)]
+        whole = jnp.concatenate(
+            [sides[0][EDGE - MARGIN :], sides[1], sides[2][:MARGIN]], axis=0
+        )
         row = rows_before - 5 + 6 * g + lax.broadcasted_iota(jnp.int32, (px, LANES), 1) // 16
         whole = jnp.where((row >= 0) & (row < rows_total) & (inside[:, 0:LANES] > 0), whole, 0.0)
         turned[g, :, 0:LANES] = pltpu.roll(whole, 1, 0).astype(BF)
@@ -295,7 +299,7 @@
     for p in range(pairs - 2):
         noise = None
         for dx in range(3):
-            at = EDGE - 1 + dx
+            at = MARGIN - 1 + dx
             term = (
                 taps[p, dx * 32 : dx * 32 + 16, at : at + cols]
                 + taps[p + 1, dx * 32 + 16 : dx * 32 + 32, at : at + cols]
@@ -461,11 +465,12 @@
                 part = noise[ROWS3 * o : ROWS3 * o + ROWS3]
                 noise_two[o, rows, cols] = part
                 fine_next[o, rows, cols] = keep * fine[o, rows, cols] + blend * part
-        rows = pl.ds(s, ROWS3)
-        for k, (near, far) in enumerate(((noise_two, noise_far), (fine_next, fine_far_next))):
-            sem = sems.at[1 + 2 * (s // ROWS3) + k]
-            sends.append(pltpu.make_async_copy(near.at[:, rows], far.at[:, rows], sem))
-            sends[-1].start()
+            if m % 2 == 1:
+                there = (slice(None), pl.ds(s, ROWS3), pl.ds(4 * LANES * (m - 1), 8 * LANES))
+                for near, far in ((noise_two, noise_far), (fine_next, fine_far_next)):
+                    sem = sems.at[1 + len(sends)]
+                    sends.append(pltpu.make_async_copy(near.at[there], far.at[there], sem))
+                    sends[-1].start()
     for send in sends:
         send.wait()
 
@@ -601,7 +606,7 @@
         name="fine_weights",
     )(step_index, ladder, timing_two, inlet_two, middle_two, outlet_two, land_bias[:, None])
 
-    px = cols + 2 * EDGE
+    px = cols + 2 * MARGIN
     pairs = (tile_rows + 8) // 2
     each = tile_rows // col_count
     coarse_next, noise_one, sends = pl.pallas_call(
@@ -647,7 +652,7 @@
             pltpu.VMEM((fields, band, width), F32),
             pltpu.VMEM((fields, band, width), F32),
             pltpu.VMEM((fields, band, width), F32),
-            pltpu.SemaphoreType.DMA((1 + 2 * (band // ROWS3),)),
+            pltpu.SemaphoreType.DMA((1 + (band // ROWS3) * (quarter // LANES),)),
         ],
         compiler_params=params(60),
         name="fine",

time: 56.4 us -> 55.6 us (0.986)
  Pallas kernels: 33.2 us -> 32.4 us
  transfers between devices with their start and end apart: 7 -> 7, of which waited for: 1 -> 1; matrix products, arithmetic and copies ran while one was open for 4% -> 4% of each run, Pallas kernels for 30% -> 29%
where the time goes in v4:
time: 55.6 us; the launch traced here: 55.2 us
  Pallas kernels  32.4 us (58%)
  starting transfers between devices  16.5 us (30%)
  local copies, waits for them, and re-layouts  3.74 us (7%)
  waiting for transfers between devices  1.63 us (3%)
  between operations  0.96 us (2%)
    pallas_call x1, Pallas kernels, body(): pl.pallas_call(functools.partial(fine_kernel, band, quarter), out_shape=(...  14.2 us
    pallas_call x1, Pallas kernels, body(): pl.pallas_call(functools.partial(coarse_kernel, tile_rows, cols, col_coun...  7.53 us
    ppermute x1, starting transfers between devices, body(): below = lax.ppermute(to_prev, ('row', 'col'), shift_pairs(count, -1))  5.33 us
    pallas_call x1, Pallas kernels, body(): pl.pallas_call(sort_kernel, grid=(width // split,), out_shape=[jax.ShapeD...  3.78 us
    all_to_all x1, starting transfers between devices, body(): lax.all_to_all(sends, 'col', split_axis=0, concat_axis=0, tiled=True)  3.55 us
    ppermute x1, starting transfers between devices, body(): east = lax.ppermute(first_cols, 'col', shift_pairs(col_count, -1))  3.54 us
    unnamed x26, local copies, waits for them, and re-layouts  3.06 us
    ppermute x1, starting transfers between devices, body(): north = lax.ppermute(last_rows, 'row', shift_pairs(row_count, 1))  2.99 us
  transfers between devices with their start and end apart: 7, of which 1 were waited for; matrix products, arithmetic and copies ran while one was open for 4% of the time, Pallas kernels for 29%

profile of v4, /device:TPU:0, one launch (start us, length us, event | category | flops | bytes accessed | tf_op | source)
XLA Modules:
  0.0 55.2 jit_solution(8900369738470954412)
XLA Ops:
  0.6 1.7 %pack.1 = (bf16[32,16,128]{2,1,0:T(8,128)(2,1)}, bf16[5,16,128]{2,1,0:T(8,128)(2,1)}, bf16[5,16,128]{2,1,0:T(8,128)(2,1)}) custom-call(f32[256,128]{1,0:T(8,128)} %bitcast.9, bf16[256,128]{1,0:T(8,128)(2,1)} %bitcast.11), custom_call_target="tpu_custom_call" | custom-call | tf_op jit(solution)/shard_map/pack/pallas_call | solution.py:515
  2.4 0.0 copy-start.1
  2.4 3.0 %collective-permute-start = (bf16[5,16,128]{2,1,0:T(8,128)(2,1)}, bf16[5,16,128]{2,1,0:T(8,128)(2,1)S(1)}, u32[]{:S(2)}, u32[]{:S(2)}) collective-permute-start(bf16[5,16,128]{2,1,0:T(8,128)(2,1)} %get-tuple-element.35), channel_id=1, source_target_pairs={{0,8},{8,16},{16,24},{24,0},{1,9},{9,17},{17,25},{25,1},{2,10},{10... | collective-permute-start | bytes 61448 | tf_op jit(solution)/shard_map/ppermute | solution.py:533
  5.4 1.0 %collective-permute-start.1 = (bf16[5,16,128]{2,1,0:T(8,128)(2,1)}, bf16[5,16,128]{2,1,0:T(8,128)(2,1)S(1)}, u32[]{:S(2)}, u32[]{:S(2)}) collective-permute-start(bf16[5,16,128]{2,1,0:T(8,128)(2,1)} %get-tuple-element.39), channel_id=1, source_target_pairs={{0,24},{8,0},{16,8},{24,16},{1,25},{9,1},{17,9},{25,17},{2,26},{10... | collective-permute-start | bytes 61448 | tf_op jit(solution)/shard_map/ppermute | solution.py:534
  6.4 3.8 %sort.1 = (bf16[4,144,1024]{2,1,0:T(8,128)(2,1)}, bf16[4,16,1024]{2,1,0:T(8,128)(2,1)}, bf16[4,32,1024]{2,1,0:T(8,128)(2,1)}, bf16[4,32,1024]{2,1,0:T(8,128)(2,1)}) custom-call(f32[128,4096]{1,0:T(8,128)} %bitcast.8, s32[16,4096]{1,0:T(8,128)} %land.1, bf16[512,512]{1,0:T(8,128)(2,1)} %constant.9.clone.turn, bf16[224,144]{1,0:T(8,128)(2,1)} %constant.10.clone.order), custom_call_target="tpu_custom_call" | custom-call | tf_op jit(solution)/shard_map/sort/pallas_call | solution.py:540
  10.2 0.0 copy-start.11
  10.2 0.0 copy-start.10
  10.2 0.0 copy-start.7
  10.2 0.0 collective-permute-done.north
  10.2 0.0 copy-start.2
  10.2 0.0 collective-permute-done.1.south
  10.2 0.0 copy-start.3
  10.3 0.0 copy-done.1
  10.3 0.1 edges.1
  10.4 0.0 copy-start
  10.4 0.7 %copy-done = bf16[128,896]{1,0:T(8,128)(2,1)} copy-done((bf16[128,896]{1,0:T(8,128)(2,1)}, bf16[128,896]{1,0:T(8,128)(2,1)S(1)}, u32[]{:S(2)}) %copy-start) | copy-done | bytes 229400
  11.1 0.0 collective-permute-start.2
  11.1 3.5 %collective-permute-start.3 = (bf16[16,896]{1,0:T(8,128)(2,1)S(1)}, bf16[16,896]{1,0:T(8,128)(2,1)S(1)}, u32[]{:S(2)}, u32[]{:S(2)}) collective-permute-start(bf16[16,896]{1,0:T(8,128)(2,1)S(1)} %get-tuple-element.45), channel_id=1, source_target_pairs={{0,7},{1,0},{2,1},{3,2},{4,3},{5,4},{6,5},{7,6},{8,15},{9,8},{10,9... | collective-permute-start | bytes 86024 | tf_op jit(solution)/shard_map/ppermute | solution.py:569
  14.7 2.3 %coarse_weights.1 = (bf16[3,384,256]{2,1,0:T(8,128)(2,1)}, bf16[1536,256]{1,0:T(8,128)(2,1)}, bf16[96,256]{1,0:T(8,128)(2,1)}, f32[8,256]{1,0:T(8,128)}) custom-call(s32[2]{0:T(128)} %steps.7, f32[8,128]{1,0:T(8,128)} %constant.8.clone.ladder, bf16[128,128]{1,0:T(8,128)(2,1)} %timing.2, bf16[3,3,16,128]{3,2,1,0:T(8,128)(2,1)} %bitcast.12, ...), custom_call_target="tpu_custom_call" | custom-call | tf_op jit(solution)/shard_map/coarse_weights/pallas_call | solution.py:573
  16.9 0.0 collective-permute-done.2.west
  16.9 0.0 copy-start.8
  16.9 0.0 collective-permute-done.3.east
  16.9 0.0 copy-start.9
  16.9 0.1 collective-permute-start.4
  17.0 5.3 %collective-permute-start.5 = (bf16[4,32,1024]{2,1,0:T(8,128)(2,1)}, bf16[4,32,1024]{2,1,0:T(8,128)(2,1)S(1)}, u32[]{:S(2)}, u32[]{:S(2)}) collective-permute-start(bf16[4,32,1024]{2,1,0:T(8,128)(2,1)} %get-tuple-element.60), channel_id=1, source_target_pairs={{0,31},{1,0},{2,1},{3,2},{4,3},{5,4},{6,5},{7,6},{8,7},{9,8},{10,9... | collective-permute-start | bytes 786440 | tf_op jit(solution)/shard_map/ppermute | solution.py:588
  22.3 0.0 copy-done.2
  22.3 0.0 copy-done.3
  22.3 0.0 copy-done.8
  22.3 0.0 copy-done.9
  22.3 7.5 %coarse.1 = (f32[256,128]{1,0:T(8,128)}, f32[256,128]{1,0:T(8,128)}, bf16[8,64,128]{2,1,0:T(8,128)(2,1)}) custom-call(s32[2]{0:T(128)} %steps.7, bf16[5,16,128]{2,1,0:T(8,128)(2,1)} %copy-done.2, bf16[5,16,128]{2,1,0:T(8,128)(2,1)} %copy-done.3, bf16[128,896]{1,0:T(8,128)(2,1)} %copy-done, bf16[16,896]{1,0:T(8,128)(2,1)} %copy-done.8, ...), custom_call_target="tpu_custom_call" | custom-call | tf_op jit(solution)/shard_map/coarse/pallas_call | solution.py:612
  29.9 3.5 %all-to-all-start = ((bf16[8,64,128]{2,1,0:T(8,128)(2,1)}), bf16[8,64,128]{2,1,0:T(8,128)(2,1)S(1)}, u32[]{:S(2)}, u32[]{:S(2)}) async-start(bf16[8,64,128]{2,1,0:T(8,128)(2,1)} %get-tuple-element.56), calls=%async_computation | async-start | bytes 262144 | tf_op jit(solution)/shard_map/all_to_all | solution.py:635
  33.4 0.0 copy-done.11
  33.4 0.7 %copy.25.land_bias = f32[32,1]{1,0:T(8,128)} copy(f32[32,1]{0,1:T(1,128)S(1)} %bitcast.14) | data formatting | bytes 256 | tf_op jit(solution)/shard_map/broadcast_in_dim | solution.py:607
  34.1 0.0 copy-done.10
  34.1 0.7 %copy.23.timing = bf16[128,32]{1,0:T(8,128)(2,1)} copy(bf16[128,32]{0,1:T(8,128)(2,1)S(1)} %copy-done.10) | data formatting | bytes 16384 | tf_op args[11]
  34.9 0.0 copy-done.7
  34.9 0.8 %copy.24.inlet_two = bf16[3,3,32,17]{3,2,1,0:T(8,128)(2,1)} copy(bf16[3,3,32,17]{2,1,3,0:T(4,128)(2,1)S(1)} %copy-done.7) | data formatting | bytes 19584 | tf_op args[10]
  35.6 2.7 %fine_weights.1 = (bf16[4,192,512]{2,1,0:T(8,128)(2,1)}, bf16[192,768]{1,0:T(8,128)(2,1)}, bf16[192,320]{1,0:T(8,128)(2,1)}) custom-call(s32[2]{0:T(128)} %steps.7, f32[8,128]{1,0:T(8,128)} %constant.8.clone.ladder, bf16[128,32]{1,0:T(8,128)(2,1)} %copy.23.timing, bf16[3,3,32,17]{3,2,1,0:T(8,128)(2,1)} %copy.24.inlet_two, bf16[3,3,32,32]{3,2,1,0:T(8,128)(2,1)} %middle_two.1, ...), custom_call_target="tpu_custom_call" | custom-call | tf_op jit(solution)/shard_map/fine_weights/pallas_call | solution.py:591
  38.3 1.6 %all-to-all-done.coarse = bf16[8,64,128]{2,1,0:T(8,128)(2,1)S(1)} async-done(((bf16[8,64,128]{2,1,0:T(8,128)(2,1)}), bf16[8,64,128]{2,1,0:T(8,128)(2,1)S(1)}, u32[]{:S(2)}, u32[]{:S(2)}) %all-to-all-start) | async-done | bytes 131104 | tf_op jit(solution)/shard_map/all_to_all | solution.py:635
  40.0 0.0 copy-start.4
  40.0 0.0 collective-permute-done.4.above
  40.0 0.0 copy-start.5
  40.0 0.0 collective-permute-done.5.below
  40.0 0.0 copy-start.6
  40.0 0.6 %copy-done.4 = bf16[8,64,128]{2,1,0:T(8,128)(2,1)} copy-done((bf16[8,64,128]{2,1,0:T(8,128)(2,1)}, bf16[8,64,128]{2,1,0:T(8,128)(2,1)S(1)}, u32[]{:S(2)}) %copy-start.4) | copy-done | bytes 131096
  40.6 0.1 copy-done.5
  40.7 0.1 copy-done.6
  40.8 14.2 %fine.1 = (f32[8,16,4096]{2,1,0:T(8,128)}, f32[8,16,4096]{2,1,0:T(8,128)}) custom-call(s32[2]{0:T(128)} %steps.7, bf16[8,64,128]{2,1,0:T(8,128)(2,1)} %copy-done.4, f32[8,16,4096]{2,1,0:T(8,128)} %fine_far.1, bf16[4,144,1024]{2,1,0:T(8,128)(2,1)} %get-tuple-element.57.own, bf16[4,16,1024]{2,1,0:T(8,128)(2,1)} %get-tuple-element.58.land, ...), custom_call_target="tpu_custom_call" | custom-call | tf_op jit(solution)/shard_map/fine/pallas_call | solution.py:637
Async XLA Ops:
  2.4 7.9 %copy-start.1 = (bf16[32,16,128]{2,1,0:T(8,128)(2,1)S(1)}, bf16[32,16,128]{2,1,0:T(8,128)(2,1)}, u32[]{:S(2)}) copy-start(bf16[32,16,128]{2,1,0:T(8,128)(2,1)} %get-tuple-element.40.comb) | copy-start | bytes 393220
  2.4 7.8 %collective-permute-start = (bf16[5,16,128]{2,1,0:T(8,128)(2,1)}, bf16[5,16,128]{2,1,0:T(8,128)(2,1)S(1)}, u32[]{:S(2)}, u32[]{:S(2)}) collective-permute-start(bf16[5,16,128]{2,1,0:T(8,128)(2,1)} %get-tuple-element.35), channel_id=1, source_target_pairs={{0,8},{8,16},{16,24},{24,0},{1,9},{9,17},{17,25},{25,1},{2,10},{10... | collective-permute-start | bytes 61448 | tf_op jit(solution)/shard_map/ppermute | solution.py:533
  5.4 4.9 %collective-permute-start.1 = (bf16[5,16,128]{2,1,0:T(8,128)(2,1)}, bf16[5,16,128]{2,1,0:T(8,128)(2,1)S(1)}, u32[]{:S(2)}, u32[]{:S(2)}) collective-permute-start(bf16[5,16,128]{2,1,0:T(8,128)(2,1)} %get-tuple-element.39), channel_id=1, source_target_pairs={{0,24},{8,0},{16,8},{24,16},{1,25},{9,1},{17,9},{25,17},{2,26},{10... | collective-permute-start | bytes 61448 | tf_op jit(solution)/shard_map/ppermute | solution.py:534
  10.2 23.3 %copy-start.11 = (f32[32]{0:T(128)S(1)}, f32[32]{0:T(128)}, u32[]{:S(2)}) copy-start(f32[32]{0:T(128)} %param.31) | copy-start | bytes 388
  10.2 23.9 %copy-start.10 = (bf16[128,32]{0,1:T(8,128)(2,1)S(1)}, bf16[128,32]{0,1:T(8,128)(2,1)}, u32[]{:S(2)}) copy-start(bf16[128,32]{0,1:T(8,128)(2,1)} %param.30) | copy-start | bytes 24580
  10.2 24.6 %copy-start.7 = (bf16[3,3,32,17]{2,1,3,0:T(4,128)(2,1)S(1)}, bf16[3,3,32,17]{2,1,3,0:T(4,128)(2,1)}, u32[]{:S(2)}) copy-start(bf16[3,3,32,17]{2,1,3,0:T(4,128)(2,1)} %param.29) | copy-start | bytes 29380
  10.2 12.1 %copy-start.2 = (bf16[5,16,128]{2,1,0:T(8,128)(2,1)}, bf16[5,16,128]{2,1,0:T(8,128)(2,1)S(1)}, u32[]{:S(2)}) copy-start(bf16[5,16,128]{2,1,0:T(8,128)(2,1)S(1)} %collective-permute-done.north) | copy-start | bytes 61444
  10.2 12.1 %copy-start.3 = (bf16[5,16,128]{2,1,0:T(8,128)(2,1)}, bf16[5,16,128]{2,1,0:T(8,128)(2,1)S(1)}, u32[]{:S(2)}) copy-start(bf16[5,16,128]{2,1,0:T(8,128)(2,1)S(1)} %collective-permute-done.1.south) | copy-start | bytes 61444
  10.4 0.7 %copy-start = (bf16[128,896]{1,0:T(8,128)(2,1)}, bf16[128,896]{1,0:T(8,128)(2,1)S(1)}, u32[]{:S(2)}) copy-start(bf16[128,896]{1,0:T(8,128)(2,1)S(1)} %get-tuple-element.41.own) | copy-start | bytes 688132
  11.1 5.8 %collective-permute-start.2 = (bf16[16,896]{1,0:T(8,128)(2,1)S(1)}, bf16[16,896]{1,0:T(8,128)(2,1)S(1)}, u32[]{:S(2)}, u32[]{:S(2)}) collective-permute-start(bf16[16,896]{1,0:T(8,128)(2,1)S(1)} %get-tuple-element.44), channel_id=1, source_target_pairs={{0,1},{1,2},{2,3},{3,4},{4,5},{5,6},{6,7},{7,0},{8,9},{9,10},{10,1... | collective-permute-start | bytes 86024 | tf_op jit(solution)/shard_map/ppermute | solution.py:568
  11.1 5.8 %collective-permute-start.3 = (bf16[16,896]{1,0:T(8,128)(2,1)S(1)}, bf16[16,896]{1,0:T(8,128)(2,1)S(1)}, u32[]{:S(2)}, u32[]{:S(2)}) collective-permute-start(bf16[16,896]{1,0:T(8,128)(2,1)S(1)} %get-tuple-element.45), channel_id=1, source_target_pairs={{0,7},{1,0},{2,1},{3,2},{4,3},{5,4},{6,5},{7,6},{8,15},{9,8},{10,9... | collective-permute-start | bytes 86024 | tf_op jit(solution)/shard_map/ppermute | solution.py:569
  16.9 5.4 %copy-start.8 = (bf16[16,896]{1,0:T(8,128)(2,1)}, bf16[16,896]{1,0:T(8,128)(2,1)S(1)}, u32[]{:S(2)}) copy-start(bf16[16,896]{1,0:T(8,128)(2,1)S(1)} %collective-permute-done.2.west) | copy-start | bytes 86020
  16.9 5.4 %copy-start.9 = (bf16[16,896]{1,0:T(8,128)(2,1)}, bf16[16,896]{1,0:T(8,128)(2,1)S(1)}, u32[]{:S(2)}) copy-start(bf16[16,896]{1,0:T(8,128)(2,1)S(1)} %collective-permute-done.3.east) | copy-start | bytes 86020
  16.9 23.0 %collective-permute-start.4 = (bf16[4,32,1024]{2,1,0:T(8,128)(2,1)}, bf16[4,32,1024]{2,1,0:T(8,128)(2,1)S(1)}, u32[]{:S(2)}, u32[]{:S(2)}) collective-permute-start(bf16[4,32,1024]{2,1,0:T(8,128)(2,1)} %get-tuple-element.59), channel_id=1, source_target_pairs={{0,1},{1,2},{2,3},{3,4},{4,5},{5,6},{6,7},{7,8},{8,9},{9,10},{10,1... | collective-permute-start | bytes 786440 | tf_op jit(solution)/shard_map/ppermute | solution.py:587
  17.0 23.0 %collective-permute-start.5 = (bf16[4,32,1024]{2,1,0:T(8,128)(2,1)}, bf16[4,32,1024]{2,1,0:T(8,128)(2,1)S(1)}, u32[]{:S(2)}, u32[]{:S(2)}) collective-permute-start(bf16[4,32,1024]{2,1,0:T(8,128)(2,1)} %get-tuple-element.60), channel_id=1, source_target_pairs={{0,31},{1,0},{2,1},{3,2},{4,3},{5,4},{6,5},{7,6},{8,7},{9,8},{10,9... | collective-permute-start | bytes 786440 | tf_op jit(solution)/shard_map/ppermute | solution.py:588
  29.9 10.1 %all-to-all-start = ((bf16[8,64,128]{2,1,0:T(8,128)(2,1)}), bf16[8,64,128]{2,1,0:T(8,128)(2,1)S(1)}, u32[]{:S(2)}, u32[]{:S(2)}) async-start(bf16[8,64,128]{2,1,0:T(8,128)(2,1)} %get-tuple-element.56), calls=%async_computation | async-start | bytes 262144 | tf_op jit(solution)/shard_map/all_to_all | solution.py:635
  40.0 0.6 %copy-start.4 = (bf16[8,64,128]{2,1,0:T(8,128)(2,1)}, bf16[8,64,128]{2,1,0:T(8,128)(2,1)S(1)}, u32[]{:S(2)}) copy-start(bf16[8,64,128]{2,1,0:T(8,128)(2,1)S(1)} %all-to-all-done.coarse) | copy-start | bytes 393220
  40.0 0.8 %copy-start.5 = (bf16[4,32,1024]{2,1,0:T(8,128)(2,1)}, bf16[4,32,1024]{2,1,0:T(8,128)(2,1)S(1)}, u32[]{:S(2)}) copy-start(bf16[4,32,1024]{2,1,0:T(8,128)(2,1)S(1)} %collective-permute-done.4.above) | copy-start | bytes 786436
  40.0 0.8 %copy-start.6 = (bf16[4,32,1024]{2,1,0:T(8,128)(2,1)}, bf16[4,32,1024]{2,1,0:T(8,128)(2,1)S(1)}, u32[]{:S(2)}) copy-start(bf16[4,32,1024]{2,1,0:T(8,128)(2,1)S(1)} %collective-permute-done.5.below) | copy-start | bytes 786436

commit v5 on v4

--- a/solution.py
+++ b/solution.py
@@ -406,8 +406,9 @@
             operand += [states[j + k, window] for k in range(3)]
             operand += [lifted[j + k, window] for k in range(3)]
             value = jnp.dot(
-                first_two[b], jnp.concatenate(operand, axis=0), preferred_element_type=F32
-            )[32 * (done - s) :]
+                first_two[b, 32 * (done - s) :, :], jnp.concatenate(operand, axis=0),
+                preferred_element_type=F32,
+            )
             value = silu(value)
             parts = []
             for i in range(done, s + ROWS1):

time: 55.6 us -> 55.5 us (level)
  transfers between devices with their start and end apart: 7 -> 7, of which waited for: 1 -> 1; matrix products, arithmetic and copies ran while one was open for 4% -> 4% of each run, Pallas kernels for 29% -> 30%
where the time goes in v5:
time: 55.5 us; the launch traced here: 55.1 us
  Pallas kernels  32.3 us (58%)
  starting transfers between devices  16.5 us (30%)
  local copies, waits for them, and re-layouts  3.74 us (7%)
  waiting for transfers between devices  1.63 us (3%)
  between operations  0.96 us (2%)
    pallas_call x1, Pallas kernels, body(): pl.pallas_call(functools.partial(fine_kernel, band, quarter), out_shape=(...  14.2 us
    pallas_call x1, Pallas kernels, body(): pl.pallas_call(functools.partial(coarse_kernel, tile_rows, cols, col_coun...  7.53 us
    ppermute x1, starting transfers between devices, body(): below = lax.ppermute(to_prev, ('row', 'col'), shift_pairs(count, -1))  5.33 us
    pallas_call x1, Pallas kernels, body(): pl.pallas_call(sort_kernel, grid=(width // split,), out_shape=[jax.ShapeD...  3.78 us
    all_to_all x1, starting transfers between devices, body(): lax.all_to_all(sends, 'col', split_axis=0, concat_axis=0, tiled=True)  3.55 us
    ppermute x1, starting transfers between devices, body(): east = lax.ppermute(first_cols, 'col', shift_pairs(col_count, -1))  3.54 us
    unnamed x26, local copies, waits for them, and re-layouts  3.06 us
    ppermute x1, starting transfers between devices, body(): north = lax.ppermute(last_rows, 'row', shift_pairs(row_count, 1))  2.99 us
  transfers between devices with their start and end apart: 7, of which 1 were waited for; matrix products, arithmetic and copies ran while one was open for 4% of the time, Pallas kernels for 30%

profile of v5, /device:TPU:0, one launch (start us, length us, event | category | flops | bytes accessed | tf_op | source)
XLA Modules:
  0.0 55.1 jit_solution(10085545703039736623)
XLA Ops:
  0.6 1.7 %pack.1 = (bf16[32,16,128]{2,1,0:T(8,128)(2,1)}, bf16[5,16,128]{2,1,0:T(8,128)(2,1)}, bf16[5,16,128]{2,1,0:T(8,128)(2,1)}) custom-call(f32[256,128]{1,0:T(8,128)} %bitcast.9, bf16[256,128]{1,0:T(8,128)(2,1)} %bitcast.11), custom_call_target="tpu_custom_call" | custom-call | tf_op jit(solution)/shard_map/pack/pallas_call | solution.py:516
  2.4 0.0 copy-start.1
  2.4 3.0 %collective-permute-start = (bf16[5,16,128]{2,1,0:T(8,128)(2,1)}, bf16[5,16,128]{2,1,0:T(8,128)(2,1)S(1)}, u32[]{:S(2)}, u32[]{:S(2)}) collective-permute-start(bf16[5,16,128]{2,1,0:T(8,128)(2,1)} %get-tuple-element.35), channel_id=1, source_target_pairs={{0,8},{8,16},{16,24},{24,0},{1,9},{9,17},{17,25},{25,1},{2,10},{10... | collective-permute-start | bytes 61448 | tf_op jit(solution)/shard_map/ppermute | solution.py:534
  5.4 1.0 %collective-permute-start.1 = (bf16[5,16,128]{2,1,0:T(8,128)(2,1)}, bf16[5,16,128]{2,1,0:T(8,128)(2,1)S(1)}, u32[]{:S(2)}, u32[]{:S(2)}) collective-permute-start(bf16[5,16,128]{2,1,0:T(8,128)(2,1)} %get-tuple-element.39), channel_id=1, source_target_pairs={{0,24},{8,0},{16,8},{24,16},{1,25},{9,1},{17,9},{25,17},{2,26},{10... | collective-permute-start | bytes 61448 | tf_op jit(solution)/shard_map/ppermute | solution.py:535
  6.4 3.8 %sort.1 = (bf16[4,144,1024]{2,1,0:T(8,128)(2,1)}, bf16[4,16,1024]{2,1,0:T(8,128)(2,1)}, bf16[4,32,1024]{2,1,0:T(8,128)(2,1)}, bf16[4,32,1024]{2,1,0:T(8,128)(2,1)}) custom-call(f32[128,4096]{1,0:T(8,128)} %bitcast.8, s32[16,4096]{1,0:T(8,128)} %land.1, bf16[512,512]{1,0:T(8,128)(2,1)} %constant.9.clone.turn, bf16[224,144]{1,0:T(8,128)(2,1)} %constant.10.clone.order), custom_call_target="tpu_custom_call" | custom-call | tf_op jit(solution)/shard_map/sort/pallas_call | solution.py:541
  10.2 0.0 copy-start.11
  10.2 0.0 copy-start.10
  10.2 0.0 copy-start.7
  10.2 0.0 collective-permute-done.north
  10.2 0.0 copy-start.2
  10.2 0.0 collective-permute-done.1.south
  10.2 0.0 copy-start.3
  10.3 0.0 copy-done.1
  10.3 0.1 edges.1
  10.4 0.0 copy-start
  10.4 0.7 %copy-done = bf16[128,896]{1,0:T(8,128)(2,1)} copy-done((bf16[128,896]{1,0:T(8,128)(2,1)}, bf16[128,896]{1,0:T(8,128)(2,1)S(1)}, u32[]{:S(2)}) %copy-start) | copy-done | bytes 229400
  11.1 0.0 collective-permute-start.2
  11.1 3.5 %collective-permute-start.3 = (bf16[16,896]{1,0:T(8,128)(2,1)S(1)}, bf16[16,896]{1,0:T(8,128)(2,1)S(1)}, u32[]{:S(2)}, u32[]{:S(2)}) collective-permute-start(bf16[16,896]{1,0:T(8,128)(2,1)S(1)} %get-tuple-element.45), channel_id=1, source_target_pairs={{0,7},{1,0},{2,1},{3,2},{4,3},{5,4},{6,5},{7,6},{8,15},{9,8},{10,9... | collective-permute-start | bytes 86024 | tf_op jit(solution)/shard_map/ppermute | solution.py:570
  14.7 2.3 %coarse_weights.1 = (bf16[3,384,256]{2,1,0:T(8,128)(2,1)}, bf16[1536,256]{1,0:T(8,128)(2,1)}, bf16[96,256]{1,0:T(8,128)(2,1)}, f32[8,256]{1,0:T(8,128)}) custom-call(s32[2]{0:T(128)} %steps.7, f32[8,128]{1,0:T(8,128)} %constant.8.clone.ladder, bf16[128,128]{1,0:T(8,128)(2,1)} %timing.2, bf16[3,3,16,128]{3,2,1,0:T(8,128)(2,1)} %bitcast.12, ...), custom_call_target="tpu_custom_call" | custom-call | tf_op jit(solution)/shard_map/coarse_weights/pallas_call | solution.py:574
  16.9 0.0 collective-permute-done.2.west
  16.9 0.0 copy-start.8
  16.9 0.0 collective-permute-done.3.east
  16.9 0.0 copy-start.9
  16.9 0.1 collective-permute-start.4
  17.0 5.3 %collective-permute-start.5 = (bf16[4,32,1024]{2,1,0:T(8,128)(2,1)}, bf16[4,32,1024]{2,1,0:T(8,128)(2,1)S(1)}, u32[]{:S(2)}, u32[]{:S(2)}) collective-permute-start(bf16[4,32,1024]{2,1,0:T(8,128)(2,1)} %get-tuple-element.60), channel_id=1, source_target_pairs={{0,31},{1,0},{2,1},{3,2},{4,3},{5,4},{6,5},{7,6},{8,7},{9,8},{10,9... | collective-permute-start | bytes 786440 | tf_op jit(solution)/shard_map/ppermute | solution.py:589
  22.3 0.0 copy-done.2
  22.3 0.0 copy-done.3
  22.3 0.0 copy-done.8
  22.3 0.0 copy-done.9
  22.3 7.5 %coarse.1 = (f32[256,128]{1,0:T(8,128)}, f32[256,128]{1,0:T(8,128)}, bf16[8,64,128]{2,1,0:T(8,128)(2,1)}) custom-call(s32[2]{0:T(128)} %steps.7, bf16[5,16,128]{2,1,0:T(8,128)(2,1)} %copy-done.2, bf16[5,16,128]{2,1,0:T(8,128)(2,1)} %copy-done.3, bf16[128,896]{1,0:T(8,128)(2,1)} %copy-done, bf16[16,896]{1,0:T(8,128)(2,1)} %copy-done.8, ...), custom_call_target="tpu_custom_call" | custom-call | tf_op jit(solution)/shard_map/coarse/pallas_call | solution.py:613
  29.9 3.5 %all-to-all-start = ((bf16[8,64,128]{2,1,0:T(8,128)(2,1)}), bf16[8,64,128]{2,1,0:T(8,128)(2,1)S(1)}, u32[]{:S(2)}, u32[]{:S(2)}) async-start(bf16[8,64,128]{2,1,0:T(8,128)(2,1)} %get-tuple-element.56), calls=%async_computation | async-start | bytes 262144 | tf_op jit(solution)/shard_map/all_to_all | solution.py:636
  33.4 0.0 copy-done.11
  33.4 0.7 %copy.25.land_bias = f32[32,1]{1,0:T(8,128)} copy(f32[32,1]{0,1:T(1,128)S(1)} %bitcast.14) | data formatting | bytes 256 | tf_op jit(solution)/shard_map/broadcast_in_dim | solution.py:608
  34.1 0.0 copy-done.10
  34.1 0.7 %copy.23.timing = bf16[128,32]{1,0:T(8,128)(2,1)} copy(bf16[128,32]{0,1:T(8,128)(2,1)S(1)} %copy-done.10) | data formatting | bytes 16384 | tf_op args[11]
  34.9 0.0 copy-done.7
  34.9 0.8 %copy.24.inlet_two = bf16[3,3,32,17]{3,2,1,0:T(8,128)(2,1)} copy(bf16[3,3,32,17]{2,1,3,0:T(4,128)(2,1)S(1)} %copy-done.7) | data formatting | bytes 19584 | tf_op args[10]
  35.6 2.7 %fine_weights.1 = (bf16[4,192,512]{2,1,0:T(8,128)(2,1)}, bf16[192,768]{1,0:T(8,128)(2,1)}, bf16[192,320]{1,0:T(8,128)(2,1)}) custom-call(s32[2]{0:T(128)} %steps.7, f32[8,128]{1,0:T(8,128)} %constant.8.clone.ladder, bf16[128,32]{1,0:T(8,128)(2,1)} %copy.23.timing, bf16[3,3,32,17]{3,2,1,0:T(8,128)(2,1)} %copy.24.inlet_two, bf16[3,3,32,32]{3,2,1,0:T(8,128)(2,1)} %middle_two.1, ...), custom_call_target="tpu_custom_call" | custom-call | tf_op jit(solution)/shard_map/fine_weights/pallas_call | solution.py:592
  38.3 1.6 %all-to-all-done.coarse = bf16[8,64,128]{2,1,0:T(8,128)(2,1)S(1)} async-done(((bf16[8,64,128]{2,1,0:T(8,128)(2,1)}), bf16[8,64,128]{2,1,0:T(8,128)(2,1)S(1)}, u32[]{:S(2)}, u32[]{:S(2)}) %all-to-all-start) | async-done | bytes 131104 | tf_op jit(solution)/shard_map/all_to_all | solution.py:636
  40.0 0.0 copy-start.4
  40.0 0.0 collective-permute-done.4.above
  40.0 0.0 copy-start.5
  40.0 0.0 collective-permute-done.5.below
  40.0 0.0 copy-start.6
  40.0 0.6 %copy-done.4 = bf16[8,64,128]{2,1,0:T(8,128)(2,1)} copy-done((bf16[8,64,128]{2,1,0:T(8,128)(2,1)}, bf16[8,64,128]{2,1,0:T(8,128)(2,1)S(1)}, u32[]{:S(2)}) %copy-start.4) | copy-done | bytes 131096
  40.6 0.1 copy-done.5
  40.7 0.1 copy-done.6
  40.8 14.2 %fine.1 = (f32[8,16,4096]{2,1,0:T(8,128)}, f32[8,16,4096]{2,1,0:T(8,128)}) custom-call(s32[2]{0:T(128)} %steps.7, bf16[8,64,128]{2,1,0:T(8,128)(2,1)} %copy-done.4, f32[8,16,4096]{2,1,0:T(8,128)} %fine_far.1, bf16[4,144,1024]{2,1,0:T(8,128)(2,1)} %get-tuple-element.57.own, bf16[4,16,1024]{2,1,0:T(8,128)(2,1)} %get-tuple-element.58.land, ...), custom_call_target="tpu_custom_call" | custom-call | tf_op jit(solution)/shard_map/fine/pallas_call | solution.py:638
Async XLA Ops:
  2.4 7.9 %copy-start.1 = (bf16[32,16,128]{2,1,0:T(8,128)(2,1)S(1)}, bf16[32,16,128]{2,1,0:T(8,128)(2,1)}, u32[]{:S(2)}) copy-start(bf16[32,16,128]{2,1,0:T(8,128)(2,1)} %get-tuple-element.40.comb) | copy-start | bytes 393220
  2.4 7.8 %collective-permute-start = (bf16[5,16,128]{2,1,0:T(8,128)(2,1)}, bf16[5,16,128]{2,1,0:T(8,128)(2,1)S(1)}, u32[]{:S(2)}, u32[]{:S(2)}) collective-permute-start(bf16[5,16,128]{2,1,0:T(8,128)(2,1)} %get-tuple-element.35), channel_id=1, source_target_pairs={{0,8},{8,16},{16,24},{24,0},{1,9},{9,17},{17,25},{25,1},{2,10},{10... | collective-permute-start | bytes 61448 | tf_op jit(solution)/shard_map/ppermute | solution.py:534
  5.4 4.9 %collective-permute-start.1 = (bf16[5,16,128]{2,1,0:T(8,128)(2,1)}, bf16[5,16,128]{2,1,0:T(8,128)(2,1)S(1)}, u32[]{:S(2)}, u32[]{:S(2)}) collective-permute-start(bf16[5,16,128]{2,1,0:T(8,128)(2,1)} %get-tuple-element.39), channel_id=1, source_target_pairs={{0,24},{8,0},{16,8},{24,16},{1,25},{9,1},{17,9},{25,17},{2,26},{10... | collective-permute-start | bytes 61448 | tf_op jit(solution)/shard_map/ppermute | solution.py:535
  10.2 23.3 %copy-start.11 = (f32[32]{0:T(128)S(1)}, f32[32]{0:T(128)}, u32[]{:S(2)}) copy-start(f32[32]{0:T(128)} %param.31) | copy-start | bytes 388
  10.2 23.9 %copy-start.10 = (bf16[128,32]{0,1:T(8,128)(2,1)S(1)}, bf16[128,32]{0,1:T(8,128)(2,1)}, u32[]{:S(2)}) copy-start(bf16[128,32]{0,1:T(8,128)(2,1)} %param.30) | copy-start | bytes 24580
  10.2 24.6 %copy-start.7 = (bf16[3,3,32,17]{2,1,3,0:T(4,128)(2,1)S(1)}, bf16[3,3,32,17]{2,1,3,0:T(4,128)(2,1)}, u32[]{:S(2)}) copy-start(bf16[3,3,32,17]{2,1,3,0:T(4,128)(2,1)} %param.29) | copy-start | bytes 29380
  10.2 12.1 %copy-start.2 = (bf16[5,16,128]{2,1,0:T(8,128)(2,1)}, bf16[5,16,128]{2,1,0:T(8,128)(2,1)S(1)}, u32[]{:S(2)}) copy-start(bf16[5,16,128]{2,1,0:T(8,128)(2,1)S(1)} %collective-permute-done.north) | copy-start | bytes 61444
  10.2 12.1 %copy-start.3 = (bf16[5,16,128]{2,1,0:T(8,128)(2,1)}, bf16[5,16,128]{2,1,0:T(8,128)(2,1)S(1)}, u32[]{:S(2)}) copy-start(bf16[5,16,128]{2,1,0:T(8,128)(2,1)S(1)} %collective-permute-done.1.south) | copy-start | bytes 61444
  10.4 0.7 %copy-start = (bf16[128,896]{1,0:T(8,128)(2,1)}, bf16[128,896]{1,0:T(8,128)(2,1)S(1)}, u32[]{:S(2)}) copy-start(bf16[128,896]{1,0:T(8,128)(2,1)S(1)} %get-tuple-element.41.own) | copy-start | bytes 688132
  11.1 5.8 %collective-permute-start.2 = (bf16[16,896]{1,0:T(8,128)(2,1)S(1)}, bf16[16,896]{1,0:T(8,128)(2,1)S(1)}, u32[]{:S(2)}, u32[]{:S(2)}) collective-permute-start(bf16[16,896]{1,0:T(8,128)(2,1)S(1)} %get-tuple-element.44), channel_id=1, source_target_pairs={{0,1},{1,2},{2,3},{3,4},{4,5},{5,6},{6,7},{7,0},{8,9},{9,10},{10,1... | collective-permute-start | bytes 86024 | tf_op jit(solution)/shard_map/ppermute | solution.py:569
  11.1 5.8 %collective-permute-start.3 = (bf16[16,896]{1,0:T(8,128)(2,1)S(1)}, bf16[16,896]{1,0:T(8,128)(2,1)S(1)}, u32[]{:S(2)}, u32[]{:S(2)}) collective-permute-start(bf16[16,896]{1,0:T(8,128)(2,1)S(1)} %get-tuple-element.45), channel_id=1, source_target_pairs={{0,7},{1,0},{2,1},{3,2},{4,3},{5,4},{6,5},{7,6},{8,15},{9,8},{10,9... | collective-permute-start | bytes 86024 | tf_op jit(solution)/shard_map/ppermute | solution.py:570
  16.9 5.4 %copy-start.8 = (bf16[16,896]{1,0:T(8,128)(2,1)}, bf16[16,896]{1,0:T(8,128)(2,1)S(1)}, u32[]{:S(2)}) copy-start(bf16[16,896]{1,0:T(8,128)(2,1)S(1)} %collective-permute-done.2.west) | copy-start | bytes 86020
  16.9 5.4 %copy-start.9 = (bf16[16,896]{1,0:T(8,128)(2,1)}, bf16[16,896]{1,0:T(8,128)(2,1)S(1)}, u32[]{:S(2)}) copy-start(bf16[16,896]{1,0:T(8,128)(2,1)S(1)} %collective-permute-done.3.east) | copy-start | bytes 86020
  16.9 23.0 %collective-permute-start.4 = (bf16[4,32,1024]{2,1,0:T(8,128)(2,1)}, bf16[4,32,1024]{2,1,0:T(8,128)(2,1)S(1)}, u32[]{:S(2)}, u32[]{:S(2)}) collective-permute-start(bf16[4,32,1024]{2,1,0:T(8,128)(2,1)} %get-tuple-element.59), channel_id=1, source_target_pairs={{0,1},{1,2},{2,3},{3,4},{4,5},{5,6},{6,7},{7,8},{8,9},{9,10},{10,1... | collective-permute-start | bytes 786440 | tf_op jit(solution)/shard_map/ppermute | solution.py:588
  17.0 23.0 %collective-permute-start.5 = (bf16[4,32,1024]{2,1,0:T(8,128)(2,1)}, bf16[4,32,1024]{2,1,0:T(8,128)(2,1)S(1)}, u32[]{:S(2)}, u32[]{:S(2)}) collective-permute-start(bf16[4,32,1024]{2,1,0:T(8,128)(2,1)} %get-tuple-element.60), channel_id=1, source_target_pairs={{0,31},{1,0},{2,1},{3,2},{4,3},{5,4},{6,5},{7,6},{8,7},{9,8},{10,9... | collective-permute-start | bytes 786440 | tf_op jit(solution)/shard_map/ppermute | solution.py:589
  29.9 10.1 %all-to-all-start = ((bf16[8,64,128]{2,1,0:T(8,128)(2,1)}), bf16[8,64,128]{2,1,0:T(8,128)(2,1)S(1)}, u32[]{:S(2)}, u32[]{:S(2)}) async-start(bf16[8,64,128]{2,1,0:T(8,128)(2,1)} %get-tuple-element.56), calls=%async_computation | async-start | bytes 262144 | tf_op jit(solution)/shard_map/all_to_all | solution.py:636
  40.0 0.6 %copy-start.4 = (bf16[8,64,128]{2,1,0:T(8,128)(2,1)}, bf16[8,64,128]{2,1,0:T(8,128)(2,1)S(1)}, u32[]{:S(2)}) copy-start(bf16[8,64,128]{2,1,0:T(8,128)(2,1)S(1)} %all-to-all-done.coarse) | copy-start | bytes 393220
  40.0 0.8 %copy-start.5 = (bf16[4,32,1024]{2,1,0:T(8,128)(2,1)}, bf16[4,32,1024]{2,1,0:T(8,128)(2,1)S(1)}, u32[]{:S(2)}) copy-start(bf16[4,32,1024]{2,1,0:T(8,128)(2,1)S(1)} %collective-permute-done.4.above) | copy-start | bytes 786436
  40.0 0.8 %copy-start.6 = (bf16[4,32,1024]{2,1,0:T(8,128)(2,1)}, bf16[4,32,1024]{2,1,0:T(8,128)(2,1)S(1)}, u32[]{:S(2)}) copy-start(bf16[4,32,1024]{2,1,0:T(8,128)(2,1)S(1)} %collective-permute-done.5.below) | copy-start | bytes 786436
